TPU v7x, 256 devices: a whole 4x4x8 slice. The times are simulated.
256 devices in a mesh: seq: 32 (over z, y_lo, core), fsdp: 8 (over y_hi, x).
Axes of the slice: x: 4, y: 4 (y_hi: 2, y_lo: 2; y = y_hi * 2 + y_lo), z: 8, core: 2. Of those that a mesh axis runs over, the one named last changes fastest.
Arguments:
- hidden: bfloat16 [8, 4096, 2048], P('fsdp', 'seq'), may hold values from -6 to 6
- tokens: int32 [8, 4096], P('fsdp', 'seq'), may hold values from 0 to 4
- base_bias: bfloat16 [5, 2048], replicated, may hold values from -3 to 3
- in_weight: bfloat16 [1024, 4384], P('fsdp'), may hold values from -0.1875 to 0.1875
- conv_weight: float32 [4, 2304], replicated, may hold values from -3 to 3
- conv_bias: float32 [2304], replicated, may hold values from -2 to 2
- dt_bias: float32 [32], replicated, may hold values from -1 to 1
- decay_rate: float32 [32], replicated, may hold values from 7.3242186e-06 to 0.04
- norm_gain: float32 [2048], replicated, may hold values from 0.1 to 1.9
- out_weight: bfloat16 [2048, 1024], P('fsdp'), may hold values from -0.125 to 0.125
Outputs:
- mixed: bfloat16 [8, 4096, 2048], P('fsdp', 'seq')
Inputs may be any that keep to these rules, and one draw needn't show every extreme that they name: `tokens`: 0 to 3 are the bases A, C, G, T and 4 is an unknown base.
All inputs are finite; a program needn't handle non-finite values.
Results may differ from a plain program's by a relative error of at most 0.0069.
Values may be sent and summed in bfloat16 or wider, within the bound.
No kernel may reach another device: no remote copies, remote signals or barrier semaphores. Data moves between devices by JAX's collectives and lax.ppermute only.
A program may use at most 256 MiB of HBM per device.

v0:
```python
import jax
import jax.numpy as jnp
from jax import lax
from jax.sharding import PartitionSpec as P

D = 1024
HEADS = 32
HEADDIM = 64
STATE = 128
CONV = 4
GROUP = 128
E = 2048
WIDE = 4384


def from_partner(value, axis, bit):
    mask = 2**bit
    pairs = [(source, source ^ mask) for source in range(lax.axis_size(axis))]
    return lax.ppermute(value, axis, pairs)


def shifted(value, axis, steps):
    count = lax.axis_size(axis)
    first, last = (max(0, -steps), min(count, count - steps))
    return lax.ppermute(value, axis, [(source, source + steps) for source in range(first, last)])


def carried_in_2(value, axis, join, neutral):
    count, mine = (lax.axis_size(axis), lax.axis_index(axis))
    pieces = jax.tree.map(lambda part: lax.all_gather(part, axis), value)
    subtotal = jax.tree.map(
        lambda part, zero: jnp.full_like(part, 0) + jnp.asarray(zero, part.dtype), value, neutral
    )

    def turn(position, subtotal):
        longer = join(subtotal, jax.tree.map(lambda part: part[position], pieces))
        return jax.tree.map(lambda new, old: jnp.where(position < mine, new, old), longer, subtotal)

    return lax.fori_loop(0, count - 1, turn, subtotal)


def group_pass(carried, pieces, rates):
    values, in_map, out_map, step_size = pieces
    span = values.shape[0]
    log_decay = -step_size * rates[None, :]
    cumulated = jnp.cumsum(log_decay, axis=0)
    position = jnp.arange(span)
    causal = position[:, None] >= position[None, :]
    log_gap = jnp.where(causal[:, :, None], cumulated[:, None, :] - cumulated[None, :, :], -1e30)
    affinity = jnp.dot(
        out_map.astype(jnp.bfloat16),
        in_map.astype(jnp.bfloat16).T,
        preferred_element_type=jnp.float32,
    )
    mixing = affinity[:, :, None] * jnp.exp(log_gap) * step_size[None, :, :]
    within = jnp.einsum("tsh,shp->thp", mixing, values, precision=lax.Precision.HIGHEST)
    entering_part = (
        jnp.einsum("tn,hpn->thp", out_map, carried, precision=lax.Precision.HIGHEST)
        * jnp.exp(cumulated)[:, :, None]
    )
    remaining = jnp.exp(cumulated[-1][None, :] - cumulated) * step_size
    updated = carried * jnp.exp(cumulated[-1])[:, None, None] + jnp.einsum(
        "sh,shp,sn->hpn", remaining, values, in_map, precision=lax.Precision.HIGHEST
    )
    return (updated, within + entering_part)


def prepare(projected, preceding, conv_weight, conv_bias, dt_bias):
    row_count = projected.shape[0]
    gate_part = projected[:, :E].astype(jnp.float32)
    conv_input = projected[:, E : 2 * E + 2 * STATE]
    padded = jnp.concatenate([preceding, conv_input], axis=0).astype(jnp.float32)
    convolved = jnp.zeros((row_count, E + 2 * STATE), jnp.float32) + conv_bias[None, :]
    for offset in range(CONV):
        convolved = convolved + conv_weight[offset][None, :] * padded[offset : offset + row_count]
    activated = lax.optimization_barrier(jax.nn.silu(convolved).astype(jnp.bfloat16)).astype(
        jnp.float32
    )
    values = activated[:, :E].reshape(row_count, HEADS, HEADDIM)
    in_map = activated[:, E : E + STATE]
    out_map = activated[:, E + STATE :]
    step_size = jax.nn.softplus(
        projected[:, 2 * E + 2 * STATE :].astype(jnp.float32) + dt_bias[None, :]
    )
    return (values, in_map, out_map, step_size, gate_part)


def block_pass(values, in_map, out_map, step_size, rates):
    row_count = values.shape[0]
    count = row_count // GROUP
    pieces = (
        values.reshape(count, GROUP, HEADS, HEADDIM),
        in_map.reshape(count, GROUP, STATE),
        out_map.reshape(count, GROUP, STATE),
        step_size.reshape(count, GROUP, HEADS),
    )
    start_state = jnp.zeros((HEADS, HEADDIM, STATE), jnp.float32)
    block_state, outputs = lax.scan(
        lambda carried, piece: group_pass(carried, piece, rates), start_state, pieces
    )
    cumulated = jnp.cumsum(-step_size * rates[None, :], axis=0)
    return (block_state, outputs.reshape(row_count, HEADS, HEADDIM), cumulated)


def finish(outputs, gate_part, norm_gain):
    row_count = outputs.shape[0]
    full = outputs.reshape(row_count, E)
    gated = full * jax.nn.silu(gate_part)
    scale = lax.rsqrt(jnp.mean(gated * gated, axis=-1, keepdims=True) + 1e-05)
    return (gated * scale * norm_gain[None, :]).astype(jnp.bfloat16)


def combine(earlier, later):
    return (earlier[0] * later[0], later[0][..., None, None] * earlier[1] + later[1])


def body(
    hidden,
    tokens,
    base_bias,
    in_weight,
    conv_weight,
    conv_bias,
    dt_bias,
    decay_rate,
    norm_gain,
    out_weight,
):
    row_count = hidden.shape[1]
    base_ids = tokens[0]
    paired = jnp.where(base_ids == 4, 4, 3 - base_ids)
    letters = jnp.arange(5, dtype=jnp.int32)
    onehot_fwd = (base_ids[:, None] == letters[None, :]).astype(jnp.bfloat16)
    onehot_rev = (paired[:, None] == letters[None, :]).astype(jnp.bfloat16)
    forward_input = (
        hidden[0, :, :D].astype(jnp.float32)
        + jnp.dot(onehot_fwd, base_bias[:, :D], preferred_element_type=jnp.float32)
    ).astype(jnp.bfloat16)
    reverse_input = (
        hidden[0, :, D:].astype(jnp.float32)
        + jnp.dot(onehot_rev, base_bias[:, D:], preferred_element_type=jnp.float32)
    ).astype(jnp.bfloat16)
    reverse_input = jnp.flip(reverse_input, axis=1)
    for bit_index in range(lax.axis_size("seq").bit_length() - 1):
        reverse_input = from_partner(reverse_input, "seq", bit_index)
    reverse_input = jnp.flip(reverse_input, axis=0)
    stacked = jnp.concatenate([forward_input, reverse_input], axis=0)
    columns = stacked
    projected = jnp.dot(
        columns,
        lax.all_gather(in_weight, "fsdp", axis=0, tiled=True),
        preferred_element_type=jnp.float32,
    )
    projected = lax.optimization_barrier(projected.astype(jnp.bfloat16)).reshape(2, row_count, WIDE)
    trailing = projected[:, row_count - (CONV - 1) :, E : 2 * E + 2 * STATE]
    preceding = shifted(trailing, "seq", 1)
    values, in_map, out_map, step_size, gate_part = jax.vmap(
        prepare, in_axes=(0, 0, None, None, None)
    )(projected, preceding, conv_weight, conv_bias, dt_bias)
    block_state, outputs, cumulated = jax.vmap(block_pass, in_axes=(0, 0, 0, 0, None))(
        values, in_map, out_map, step_size, decay_rate
    )
    block_decay = jnp.exp(cumulated[:, -1])
    unit_pair = (
        jnp.ones((2, HEADS), jnp.float32),
        jnp.zeros((2, HEADS, HEADDIM, STATE), jnp.float32),
    )
    entering = carried_in_2((block_decay, block_state), "seq", combine, unit_pair)[1]
    carried_in = (
        jnp.einsum("ktn,khpn->kthp", out_map, entering, precision=lax.Precision.HIGHEST)
        * jnp.exp(cumulated)[:, :, :, None]
    )
    outputs = outputs + carried_in
    normed = jax.vmap(finish, in_axes=(0, 0, None))(outputs, gate_part, norm_gain)
    normed = normed.reshape(2 * row_count, E)
    columns = normed
    strand_output = jnp.dot(
        columns,
        lax.all_gather(out_weight, "fsdp", axis=0, tiled=True),
        preferred_element_type=jnp.float32,
    )
    strand_output = strand_output.astype(jnp.bfloat16).reshape(2, row_count, D)
    forward_out = strand_output[0]
    reverse_out = jnp.flip(jnp.flip(strand_output[1], axis=0), axis=1)
    for bit_index in range(lax.axis_size("seq").bit_length() - 1):
        reverse_out = from_partner(reverse_out, "seq", bit_index)
    return jnp.concatenate([forward_out, reverse_out], axis=1)[None]


def solution(mesh):
    placed = (
        P("fsdp", "seq", None),
        P("fsdp", "seq"),
        P(),
        P("fsdp", None),
        P(),
        P(),
        P(),
        P(),
        P(),
        P("fsdp", None),
    )
    return jax.shard_map(
        body, mesh=mesh, in_specs=placed, out_specs=P("fsdp", "seq", None), check_vma=False
    )
```

profile of v0, /device:TPU:1, one launch (start us, length us, event | category | flops | bytes accessed | tf_op | source)
XLA Modules:
  0.0 658.2 jit_solution(11649739707584376955)
XLA Ops:
  10.1 3.3 collective-permute-start
  14.6 7.5 %collective-permute-done.1 = bf16[128,1024]{1,0:T(8,128)(2,1)S(1)} collective-permute-done((bf16[128,1024]{1,0:T(8,128)(2,1)S(1)}, bf16[128,1024]{1,0:T(8,128)(2,1)S(1)}, u32[]{:S(2)}, u32[]{:S(2)}) %collective-permute-start.1) | collective-permute-done | bytes 262176 | tf_op jit(solution)/shard_map/ppermute | solution.py:19
  22.1 6.6 %collective-permute-done.2 = bf16[128,1024]{1,0:T(8,128)(2,1)S(1)} collective-permute-done((bf16[128,1024]{1,0:T(8,128)(2,1)S(1)}, bf16[128,1024]{1,0:T(8,128)(2,1)S(1)}, u32[]{:S(2)}, u32[]{:S(2)}) %collective-permute-start.2) | collective-permute-done | bytes 262176 | tf_op jit(solution)/shard_map/ppermute | solution.py:19
  30.3 13.0 %collective-permute-done.3 = bf16[128,1024]{1,0:T(8,128)(2,1)S(1)} collective-permute-done((bf16[128,1024]{1,0:T(8,128)(2,1)S(1)}, bf16[128,1024]{1,0:T(8,128)(2,1)S(1)}, u32[]{:S(2)}, u32[]{:S(2)}) %collective-permute-start.3) | collective-permute-done | bytes 262176 | tf_op jit(solution)/shard_map/ppermute | solution.py:19
  43.3 4.9 collective-permute-start.4
  48.6 11.4 %collective-permute-done.4 = bf16[128,1024]{1,0:T(8,128)(2,1)S(1)} collective-permute-done((bf16[128,1024]{1,0:T(8,128)(2,1)S(1)}, bf16[128,1024]{1,0:T(8,128)(2,1)S(1)}, u32[]{:S(2)}, u32[]{:S(2)}) %collective-permute-start.4) | collective-permute-done | bytes 262176 | tf_op jit(solution)/shard_map/ppermute | solution.py:19
  60.4 84.1 %all-gather.6.cloned.1.call-done = bf16[1024,4384]{0,1:T(8,128)(2,1)} async-done(((bf16[128,4384]{0,1:T(8,128)(2,1)}), bf16[1024,4384]{0,1:T(8,128)(2,1)}) %all-gather.6.cloned.1.call-update) | async-done | bytes 8978448 | tf_op jit(solution)/shard_map/all_gather | solution.py:151
  144.5 7.4 %convolution_convert_fusion = bf16[256,4384]{0,1:T(8,128)(2,1)} fusion(bf16[1024,4384]{0,1:T(8,128)(2,1)} %all-gather.6.cloned.1.call-done, bf16[128,1024]{1,0:T(8,128)(2,1)S(1)} %rev.13, bf16[128,1024]{1,0:T(8,128)(2,1)S(1)} %fusion.28), kind=kOutput, calls=%fused_computation.3 | convolution fusion | flops 2300649472 | bytes 11747328 | tf_op jit(solution)/shard_map/dot_general | solution.py:149
  151.9 3.0 copy.40
  155.6 3.6 collective-permute-start.5
  166.1 2.5 fusion.25
  170.2 34.1 %all-gather = f32[64,1,32]{2,1,0:T(1,128)S(1)} all-gather(f32[2,1,32]{2,1,0:T(1,128)} %get-tuple-element.162), channel_id=2, replica_groups=mesh['seq'=32,'fsdp'=8] {'seq'}, dimensions={0}, use_global_device_ids=true | all-gather | bytes 8448 | tf_op jit(solution)/shard_map/all_gather | solution.py:30
  206.2 2.3 fusion.31
  208.5 6.0 fusion.1
  214.5 307.6 %all-gather.10.cloned.1.call-done = f32[64,32,64,128]{3,2,1,0:T(8,128)} async-done(((f32[2,32,64,128]{3,2,1,0:T(8,128)}), f32[64,32,64,128]{3,2,1,0:T(8,128)}) %all-gather.10.cloned.1.call-update) | async-done | bytes 67108880 | tf_op jit(solution)/shard_map/all_gather | solution.py:30
  522.1 66.1 %while.9 = (s32[]{:T(128)}, f32[2,32,64,128]{3,2,1,0:T(8,128)S(1)}, s32[]{:T(128)}, f32[32,2,32]{2,1,0:T(2,128)S(1)}, f32[32,2,32,64,128]{4,3,2,1,0:T(8,128)}, /*index=5*/s32[]{:T(128)}, s32[]{:T(128)}) while((s32[]{:T(128)}, f32[2,32,64,128]{3,2,1,0:T(8,128)S(1)}, s32[]{:T(128)}, f32[32,2,32]{2,1,0:T(2,128)S(1)}, ...), condition=%wide.region_2.3_spmd.clone, body=%wide.region_1.2_spmd.clone.sunk | while | flops 2097156 | bytes 6292329 | solution.py:39
  524.2 2.1 fusion.60
  526.4 2.1 fusion.60
  528.5 2.1 fusion.60
  530.6 2.1 fusion.60
  532.7 2.1 fusion.60
  534.9 2.1 fusion.60
  537.0 2.2 fusion.60
  539.2 2.1 fusion.60
  541.4 2.1 fusion.60
  543.5 2.1 fusion.60
  545.6 2.1 fusion.60
  547.8 2.1 fusion.60
  549.9 2.1 fusion.60
  552.0 2.1 fusion.60
  554.2 2.1 fusion.60
  564.8 2.2 fusion.60
  567.0 2.1 fusion.60
  569.1 2.1 fusion.60
  571.2 2.1 fusion.60
  573.4 2.1 fusion.60
  579.7 2.1 fusion.60
  581.9 2.1 fusion.60
  584.0 2.1 fusion.60
  586.1 2.1 fusion.60
  588.2 4.9 fusion.15
  601.0 3.4 convolution_convert_fusion.1
  608.1 7.2 %collective-permute-done.7 = bf16[128,1024]{1,0:T(8,128)(2,1)S(1)} collective-permute-done((bf16[128,1024]{1,0:T(8,128)(2,1)S(1)}, bf16[128,1024]{1,0:T(8,128)(2,1)S(1)}, u32[]{:S(2)}, u32[]{:S(2)}) %collective-permute-start.7) | collective-permute-done | bytes 262176 | tf_op jit(solution)/shard_map/ppermute | solution.py:19
  616.6 5.3 collective-permute-done.8
  621.9 2.3 collective-permute-start.9
  624.2 11.4 %collective-permute-done.9 = bf16[128,1024]{1,0:T(8,128)(2,1)S(1)} collective-permute-done((bf16[128,1024]{1,0:T(8,128)(2,1)S(1)}, bf16[128,1024]{1,0:T(8,128)(2,1)S(1)}, u32[]{:S(2)}, u32[]{:S(2)}) %collective-permute-start.9) | collective-permute-done | bytes 262176 | tf_op jit(solution)/shard_map/ppermute | solution.py:19
  635.6 6.4 collective-permute-start.10
  642.0 8.8 %collective-permute-done.10 = bf16[128,1024]{1,0:T(8,128)(2,1)S(1)} collective-permute-done((bf16[128,1024]{1,0:T(8,128)(2,1)S(1)}, bf16[128,1024]{1,0:T(8,128)(2,1)S(1)}, u32[]{:S(2)}, u32[]{:S(2)}) %collective-permute-start.10) | collective-permute-done | bytes 262176 | tf_op jit(solution)/shard_map/ppermute | solution.py:19
  (119 shorter events, 46.1 us)
Async XLA Ops:
  6.5 41.8 %copy-start.15 = (s32[1,128]{1,0:T(1,128)S(1)}, s32[1,128]{1,0:T(1,128)}, u32[]{:S(2)}) copy-start(s32[1,128]{1,0:T(1,128)} %param.13) | copy-start | bytes 1540
  6.5 41.8 %copy-start.5 = (bf16[1,128,2048]{2,1,0:T(8,128)(2,1)S(1)}, bf16[1,128,2048]{2,1,0:T(8,128)(2,1)}, u32[]{:S(2)}) copy-start(bf16[1,128,2048]{2,1,0:T(8,128)(2,1)} %param.12) | copy-start | bytes 1572868
  6.5 41.8 %copy-start.8 = (bf16[5,2048]{1,0:T(8,128)(2,1)S(1)}, bf16[5,2048]{1,0:T(8,128)(2,1)}, u32[]{:S(2)}) copy-start(bf16[5,2048]{1,0:T(8,128)(2,1)} %param.14) | copy-start | bytes 61444
  6.5 41.6 %copy-start.7 = (f32[4,2304]{1,0:T(4,128)S(1)}, f32[4,2304]{1,0:T(4,128)}, u32[]{:S(2)}) copy-start(f32[4,2304]{1,0:T(4,128)} %param.16) | copy-start | bytes 110596
  6.5 138.0 %all-gather.6.cloned.1.call-start = ((), (), s32[]{:S(2)}) async-start(), calls=%async_computation | async-start | bytes 10100736 | tf_op jit(solution)/shard_map/all_gather | solution.py:151
  7.3 514.9 %all-gather.10.cloned.1.call-start = ((), (), s32[]{:S(2)}) async-start(), calls=%async_computation.2 | async-start | bytes 69206016 | tf_op jit(solution)/shard_map/all_gather | solution.py:30
  10.1 4.5 collective-permute-start
  14.6 7.5 %collective-permute-start.1 = (bf16[128,1024]{1,0:T(8,128)(2,1)S(1)}, bf16[128,1024]{1,0:T(8,128)(2,1)S(1)}, u32[]{:S(2)}, u32[]{:S(2)}) collective-permute-start(bf16[128,1024]{1,0:T(8,128)(2,1)S(1)} %collective-permute-done), channel_id=1, source_target_pairs={{0,16},{8,24},{16,0},{24,8},{32,48},{40,56},{48,32},{56,40},{64,80... | collective-permute-start | bytes 786440 | tf_op jit(solution)/shard_map/ppermute | solution.py:19
  22.1 6.6 %collective-permute-start.2 = (bf16[128,1024]{1,0:T(8,128)(2,1)S(1)}, bf16[128,1024]{1,0:T(8,128)(2,1)S(1)}, u32[]{:S(2)}, u32[]{:S(2)}) collective-permute-start(bf16[128,1024]{1,0:T(8,128)(2,1)S(1)} %collective-permute-done.1), channel_id=1, source_target_pairs={{0,32},{8,40},{16,48},{24,56},{32,0},{40,8},{48,16},{56,24},{64,96... | collective-permute-start | bytes 786440 | tf_op jit(solution)/shard_map/ppermute | solution.py:19
  28.7 14.6 %collective-permute-start.3 = (bf16[128,1024]{1,0:T(8,128)(2,1)S(1)}, bf16[128,1024]{1,0:T(8,128)(2,1)S(1)}, u32[]{:S(2)}, u32[]{:S(2)}) collective-permute-start(bf16[128,1024]{1,0:T(8,128)(2,1)S(1)} %collective-permute-done.2), channel_id=1, source_target_pairs={{0,64},{8,72},{16,80},{24,88},{32,96},{40,104},{48,112},{56,120},{... | collective-permute-start | bytes 786440 | tf_op jit(solution)/shard_map/ppermute | solution.py:19
  43.3 16.7 %collective-permute-start.4 = (bf16[128,1024]{1,0:T(8,128)(2,1)S(1)}, bf16[128,1024]{1,0:T(8,128)(2,1)S(1)}, u32[]{:S(2)}, u32[]{:S(2)}) collective-permute-start(bf16[128,1024]{1,0:T(8,128)(2,1)S(1)} %collective-permute-done.3), channel_id=1, source_target_pairs={{0,128},{8,136},{16,144},{24,152},{32,160},{40,168},{48,176},{56,1... | collective-permute-start | bytes 786440 | tf_op jit(solution)/shard_map/ppermute | solution.py:19
  151.9 7.4 %copy-start.14 = (f32[32]{0:T(128)S(1)}, f32[32]{0:T(128)}, u32[]{:S(2)}) copy-start(f32[32]{0:T(128)} %param.18) | copy-start | bytes 388
  151.9 7.4 %copy-start.16 = (f32[32]{0:T(128)S(1)}, f32[32]{0:T(128)}, u32[]{:S(2)}) copy-start(f32[32]{0:T(128)} %param.19) | copy-start | bytes 388
  154.9 8.8 %copy-start = (bf16[256,4384]{1,0:T(8,128)(2,1)}, bf16[256,4384]{1,0:T(8,128)(2,1)S(1)}, u32[]{:S(2)}) copy-start(bf16[256,4384]{1,0:T(8,128)(2,1)S(1)} %copy.40) | copy-start | bytes 6733828
  155.6 7.1 %collective-permute-start.5 = (bf16[2,3,2304]{2,1,0:T(4,128)(2,1)}, bf16[2,3,2304]{2,1,0:T(4,128)(2,1)}, u32[]{:S(2)}, u32[]{:S(2)}) collective-permute-start(bf16[2,3,2304]{2,1,0:T(4,128)(2,1)} %slice.95), channel_id=1, source_target_pairs={{0,8},{8,16},{16,24},{24,32},{32,40},{40,48},{48,56},{56,64},{64,7... | collective-permute-start | bytes 82952 | tf_op jit(solution)/shard_map/ppermute | solution.py:25
  159.6 1.5 copy-start.3
  162.7 1.1 copy-start.11
  165.3 0.8 copy-start.13
  166.1 2.6 copy-start.1
  168.6 0.9 copy-start.4
  168.6 37.3 %copy-start.6 = (f32[2,128,32]{2,1,0:T(8,128)S(1)}, f32[2,128,32]{2,1,0:T(8,128)}, u32[]{:S(2)}) copy-start(f32[2,128,32]{2,1,0:T(8,128)} %get-tuple-element.160) | copy-start | bytes 98308
  168.6 432.4 %all-gather.8.cloned.1.call-start = ((), (), s32[]{:S(2)}) async-start(), calls=%async_computation.1 | async-start | bytes 4718592 | tf_op jit(solution)/shard_map/all_gather | solution.py:179
  170.2 38.3 %copy-start.9 = (f32[2,128,32]{1,2,0:T(8,128)S(1)}, f32[2,128,32]{1,2,0:T(8,128)}, u32[]{:S(2)}) copy-start(f32[2,128,32]{1,2,0:T(8,128)} %copy.42) | copy-start | bytes 98308
  206.0 2.5 copy-start.2
  206.0 2.5 copy-start.10
  595.0 2.0 copy-start.12
  605.4 2.3 collective-permute-start.6
  607.8 7.5 %collective-permute-start.7 = (bf16[128,1024]{1,0:T(8,128)(2,1)S(1)}, bf16[128,1024]{1,0:T(8,128)(2,1)S(1)}, u32[]{:S(2)}, u32[]{:S(2)}) collective-permute-start(bf16[128,1024]{1,0:T(8,128)(2,1)S(1)} %collective-permute-done.6), channel_id=1, source_target_pairs={{0,16},{8,24},{16,0},{24,8},{32,48},{40,56},{48,32},{56,40},{64,80... | collective-permute-start | bytes 786440 | tf_op jit(solution)/shard_map/ppermute | solution.py:19
  615.3 6.6 %collective-permute-start.8 = (bf16[128,1024]{1,0:T(8,128)(2,1)S(1)}, bf16[128,1024]{1,0:T(8,128)(2,1)S(1)}, u32[]{:S(2)}, u32[]{:S(2)}) collective-permute-start(bf16[128,1024]{1,0:T(8,128)(2,1)S(1)} %collective-permute-done.7), channel_id=1, source_target_pairs={{0,32},{8,40},{16,48},{24,56},{32,0},{40,8},{48,16},{56,24},{64,96... | collective-permute-start | bytes 786440 | tf_op jit(solution)/shard_map/ppermute | solution.py:19
  621.9 13.7 %collective-permute-start.9 = (bf16[128,1024]{1,0:T(8,128)(2,1)S(1)}, bf16[128,1024]{1,0:T(8,128)(2,1)S(1)}, u32[]{:S(2)}, u32[]{:S(2)}) collective-permute-start(bf16[128,1024]{1,0:T(8,128)(2,1)S(1)} %collective-permute-done.8), channel_id=1, source_target_pairs={{0,64},{8,72},{16,80},{24,88},{32,96},{40,104},{48,112},{56,120},{... | collective-permute-start | bytes 786440 | tf_op jit(solution)/shard_map/ppermute | solution.py:19
  635.6 15.2 %collective-permute-start.10 = (bf16[128,1024]{1,0:T(8,128)(2,1)S(1)}, bf16[128,1024]{1,0:T(8,128)(2,1)S(1)}, u32[]{:S(2)}, u32[]{:S(2)}) collective-permute-start(bf16[128,1024]{1,0:T(8,128)(2,1)S(1)} %collective-permute-done.9), channel_id=1, source_target_pairs={{0,128},{8,136},{16,144},{24,152},{32,160},{40,168},{48,176},{56,1... | collective-permute-start | bytes 786440 | tf_op jit(solution)/shard_map/ppermute | solution.py:19
Sparse Core Ops, SparseCore 0:
  9.8 134.5 all-gather.5
  168.8 353.3 all-gather.9
  524.8 76.2 all-gather.7
where the time goes:
time: 661 us; the launch traced here: 658 us
  waiting for transfers between devices  469 us (71%)
  other arithmetic  74.6 us (11%)
  blocking collectives  34.1 us (5%)
  matrix products  28.3 us (4%)
  starting transfers between devices  25 us (4%)
  between operations  13.4 us (2%)
  local copies, waits for them, and re-layouts  13 us (2%)
    all_gather x1, waiting for transfers between devices, carried_in_2(): pieces = jax.tree.map(lambda part: lax.all_gather(part, axis), value)  308 us
    all_gather x1, waiting for transfers between devices, body(): lax.all_gather(in_weight, 'fsdp', axis=0, tiled=True)  84.1 us
    ppermute x10, waiting for transfers between devices, from_partner(): return lax.ppermute(value, axis, pairs)  73.7 us
    select_n x31, other arithmetic, turn(): jnp.where(position < mine, new, old)  64.8 us
    all_gather x1, blocking collectives, carried_in_2(): pieces = jax.tree.map(lambda part: lax.all_gather(part, axis), value)  34.1 us
    ppermute x10, starting transfers between devices, from_partner(): return lax.ppermute(value, axis, pairs)  21.3 us
  transfers between devices with their start and end apart: 14, of which 13 were waited for; matrix products, arithmetic and copies ran while one was open for 14% of the time, Pallas kernels for 0%

commit v1 on v0

v1 whole, which is shorter than its diff:
```python
import jax
import jax.numpy as jnp
from jax import lax
from jax.experimental import pallas as pl
from jax.experimental.pallas import tpu as pltpu
from jax.sharding import PartitionSpec as P

D = 1024
HEADS = 32
HEADDIM = 64
STATE = 128
CONV = 4
GROUP = 128
E = 2048
WIDE = 4384
ROWS = 128
SPAN = 512
OWN = 512
HALO = 16
PAD = HALO + SPAN
WA = OWN + 2 * STATE + 128
Z = 8

F32 = jnp.float32
BF16 = jnp.bfloat16
EXACT = lax.Precision.HIGHEST
ANY = pl.BlockSpec(memory_space=pl.ANY)
VMEM = pl.BlockSpec(memory_space=pltpu.VMEM)


def place():
    s, f = lax.axis_index("seq"), lax.axis_index("fsdp")
    t = lax.rem(s, 4)
    return s // 4, t // 2, lax.rem(t, 2), f // 4, lax.rem(f, 4), t


def move(value, to):
    pairs = []
    for s in range(32):
        for f in range(8):
            here = dict(z=s // 4, yl=(s // 2) % 2, c=s % 2, yh=f // 4, x=f % 4)
            change = to(**here)
            if change is None:
                continue
            there = {**here, **change}
            target = (there["z"] * 4 + there["yl"] * 2 + there["c"]) * 8 + there["yh"] * 4 + there["x"]
            pairs.append((s * 8 + f, target))
    return lax.ppermute(value, ("seq", "fsdp"), pairs)


def params(mb, flops=0, bytes_accessed=0):
    return dict(
        compiler_params=pltpu.CompilerParams(vmem_limit_bytes=mb << 20),
        cost_estimate=pl.CostEstimate(flops=flops, bytes_accessed=bytes_accessed, transcendentals=0),
    )


def iota2(shape, dim):
    return lax.broadcasted_iota(jnp.int32, shape, dim)


def ones_at(where):
    return jnp.where(where, 1.0, 0.0)


def anti_identity():
    return ones_at(iota2((128, 128), 0) + iota2((128, 128), 1) == 127).astype(BF16)


def flipped(block):
    anti = anti_identity()
    rows = jnp.dot(anti, block, preferred_element_type=F32).astype(BF16)
    parts = [
        jnp.dot(rows[:, 128 * j : 128 * j + 128], anti, preferred_element_type=F32).astype(BF16)
        for j in range(D // 128)
    ]
    return jnp.concatenate(parts[::-1], axis=1)


def pack_weights(iw, ow, cw, cb, dtb, rate, gain, ua, ua_other, ub, ub_other, prm, stack):
    _, yl, c, _, _, t = place()
    t_other = (1 - yl) * 2 + c
    row, col = iota2((512, 256), 0), iota2((512, 256), 1)
    inner = lax.rem(col, 128)
    head = jnp.where(col < 128, t, t_other)
    pick = ones_at(row == 256 * (inner // 64) + 64 * head + lax.rem(inner, 64))
    pick_bf = pick.astype(BF16)
    for j in range(4):
        got = jnp.dot(iw[:, E + 512 * j : E + 512 * j + 512], pick_bf, preferred_element_type=F32).astype(BF16)
        ua[:, 128 * j : 128 * j + 128] = got[:, :128]
        ua_other[:, 128 * j : 128 * j + 128] = got[:, 128:]
        got = jnp.dot(iw[:, 512 * j : 512 * j + 512], pick_bf, preferred_element_type=F32).astype(BF16)
        ub[:128, 128 * j : 128 * j + 128] = got[:, :128]
        ub_other[:128, 128 * j : 128 * j + 128] = got[:, 128:]
    both = iw[:, 2 * E : 2 * E + 2 * STATE]
    ua[:, OWN : OWN + 2 * STATE] = both
    ua_other[:, OWN : OWN + 2 * STATE] = both
    lane, out = iota2((HEADS, 256), 0), iota2((HEADS, 256), 1)
    inner = lax.rem(out, 128)
    step_pick = ones_at((lane == 4 * inner + jnp.where(out < 128, t, t_other)) & (inner < 8))
    got = jnp.dot(iw[:, 2 * E + 2 * STATE :], step_pick.astype(BF16), preferred_element_type=F32).astype(BF16)
    ua[:, OWN + 2 * STATE :] = got[:, :128]
    ua_other[:, OWN + 2 * STATE :] = got[:, 128:]
    for ref, which in ((ub, t), (ub_other, t_other)):
        rows = ow[pl.ds(pl.multiple_of(64 * which, 64), 64), :]
        ref[128:192, :] = rows[:, :512]
        ref[192:256, :] = rows[:, 512:]
    stack[...] = jnp.zeros_like(stack)
    stack[0:4, :] = cw[:, :E]
    stack[4:5, :] = cb[:, :E]
    stack[5:6, :] = gain[...]
    prm[...] = jnp.zeros_like(prm)
    for j in range(4):
        prm[:, 128 * j : 128 * j + 128] = jnp.dot(
            stack[:, 512 * j : 512 * j + 512], pick[:, :128], precision=EXACT, preferred_element_type=F32
        )
    prm[0:4, OWN : OWN + 2 * STATE] = cw[:, E:]
    prm[4:5, OWN : OWN + 2 * STATE] = cb[:, E:]
    stack[0:1, :HEADS] = dtb[...]
    stack[1:2, :HEADS] = rate[...]
    prm[:, OWN + 2 * STATE :] = jnp.dot(
        stack[:, :HEADS], step_pick[:, :128], precision=EXACT, preferred_element_type=F32
    )


def prepare_inputs(hidden, tokens, base_bias, act, halo):
    _, _, c, _, _, _ = place()
    ids = tokens[...]
    letter = iota2((8, ROWS), 0)
    paired = jnp.where(ids == 4, 4, 3 - ids)
    for strand, chosen in ((0, ids), (1, paired)):
        onehot = ones_at(letter == chosen).astype(BF16)
        bias = lax.dot_general(
            onehot, base_bias[:, D * strand : D * strand + D], (((0,), (0,)), ((), ())), preferred_element_type=F32
        )
        block = (hidden[:, D * strand : D * strand + D].astype(F32) + bias).astype(BF16)
        if strand:
            block = flipped(block)
        act[ROWS * strand : ROWS * strand + ROWS, :] = block
    halo[...] = jnp.where(c == 1, act[ROWS - HALO : ROWS, :], act[2 * ROWS - HALO :, :])


def fetch(copies):
    for copy in copies:
        copy.start()
    for copy in copies:
        copy.wait()


def weight_rows():
    _, _, _, yh, x, _ = place()
    return [which * 4 + lax.rem(x - k + 4, 4) for which in (yh, 1 - yh) for k in range(4)]


def act_copies(blocks, act, sems):
    _, _, _, _, _, t = place()
    copies = []
    for n, (block, other) in enumerate(zip(blocks, (0, 2, 1, 3))):
        at = t ^ other
        for strand, row in ((0, at), (1, 3 - at)):
            copies.append(
                pltpu.make_async_copy(
                    block.at[pl.ds(ROWS * strand, ROWS)],
                    act.at[strand, pl.ds(pl.multiple_of(HALO + ROWS * row, 16), ROWS)],
                    sems.at[2 * n + strand],
                )
            )
    return copies


def spread():
    return ones_at(iota2((128, OWN), 0) == iota2((128, OWN), 1) // HEADDIM)


def lower():
    return ones_at(iota2((GROUP, GROUP), 0) >= iota2((GROUP, GROUP), 1))


def exact_dot(a, b):
    return jnp.dot(a, b, precision=EXACT, preferred_element_type=F32)


def hi_lo(v):
    hi = v.astype(BF16).astype(F32)
    return hi, v - hi


def scan_kernel(*refs):
    blocks, refs = refs[:4], refs[4:]
    halos, refs = refs[:3], refs[3:]
    units, refs = refs[:8], refs[8:]
    prm, refs = refs[0], refs[1:]
    xs, maps, step, starts, *sends = refs[:11]
    act, halo, weight, proj, ends, asem, hsem, wsem, ssem = refs[11:]
    z, _, c, _, _, _ = place()
    copies = act_copies(blocks, act, asem)
    copies += [pltpu.make_async_copy(h, halo.at[n], hsem.at[n]) for n, h in enumerate(halos)]
    for n, (unit, f) in enumerate(zip(units, weight_rows())):
        rows = pl.ds(pl.multiple_of(128 * f, 128), 128)
        copies.append(pltpu.make_async_copy(unit, weight.at[rows], wsem.at[n]))
    fetch(copies)
    near = halo[0] + halo[1]
    far = halo[2]
    act[0, :HALO, :] = jnp.where(c == 1, near, far)
    act[1, :HALO, :] = jnp.where(c == 1, far, near)
    expand = spread()
    triangle = lower()

    def one_strand(strand, _):
        proj[...] = jnp.dot(act[strand], weight[...], preferred_element_type=F32).astype(BF16).astype(F32)
        for j in range(6):
            cols = slice(128 * j, 128 * j + 128)
            acc = prm[4:5, cols] + prm[0:1, cols] * proj[HALO - 3 : HALO - 3 + SPAN, cols]
            for k in range(1, CONV):
                acc = acc + prm[k : k + 1, cols] * proj[HALO - 3 + k : HALO - 3 + k + SPAN, cols]
            half = 0.5 * acc
            done = (half + half * jnp.tanh(half)).astype(BF16)
            if j < 4:
                xs[strand, :, cols] = done
            else:
                maps[strand, :, 128 * (j - 4) : 128 * (j - 4) + 128] = done
        raw = proj[HALO:, OWN + 2 * STATE :] + prm[0:1, OWN + 2 * STATE :]
        size = jnp.maximum(raw, 0.0) + jnp.log1p(jnp.exp(-jnp.abs(raw)))
        step[strand] = size
        decay = -size * prm[1:2, OWN + 2 * STATE :]
        state = jnp.zeros((STATE, OWN), F32)
        total = jnp.zeros((1, 128), F32)
        for g in range(SPAN // GROUP):
            rows = slice(GROUP * g, GROUP * g + GROUP)
            cumulated = exact_dot(triangle, decay[rows])
            last = cumulated[GROUP - 1 :, :]
            total = total + last
            remaining = exact_dot(jnp.exp(last - cumulated) * size[rows], expand)
            weighted = (xs[strand, rows, :].astype(F32) * remaining).astype(BF16)
            starts[strand, g] = state.astype(BF16)
            added = lax.dot_general(
                maps[strand, rows, :STATE], weighted, (((0,), (0,)), ((), ())), preferred_element_type=F32
            )
            kept = exact_dot(jnp.broadcast_to(jnp.exp(last), (8, 128)), expand)[0:1]
            state = state * kept + added
        ends[strand, :STATE, :] = state.astype(BF16)
        hi, lo = hi_lo(exact_dot(jnp.broadcast_to(total, (8, 128)), expand))
        line = iota2((HALO, OWN), 0)
        ends[strand, STATE:, :] = jnp.where(line == 0, hi[0:1], jnp.where(line == 1, lo[0:1], 0.0)).astype(BF16)
        return 0

    lax.fori_loop(0, 2, one_strand, 0)
    out = []
    for k in range(1, Z):
        strand = jnp.where(z + k < Z, 0, 1)
        out.append(pltpu.make_async_copy(ends.at[strand], sends[k - 1], ssem.at[k - 1]))
    fetch(out)


def local_kernel(*refs):
    blocks, refs = refs[:4], refs[4:]
    units, refs = refs[:8], refs[8:]
    prm, xs, maps, step, starts, local, carry, act, weight, asem, wsem = refs
    copies = act_copies(blocks, act, asem)
    for n, (unit, f) in enumerate(zip(units, weight_rows())):
        rows = pl.ds(pl.multiple_of(128 * f, 128), 128)
        copies.append(pltpu.make_async_copy(unit.at[pl.ds(0, 128)], weight.at[rows], wsem.at[n]))
    fetch(copies)
    expand = spread()
    triangle = lower()
    left = iota2((GROUP, 128), 1) < HEADDIM

    def one_strand(strand, _):
        rates = prm[1:2, OWN + 2 * STATE :]

        def one_group(g, before):
            at = pl.multiple_of(GROUP * g, GROUP)
            rows = pl.ds(at, GROUP)
            gate = jnp.dot(
                act[strand, pl.ds(pl.multiple_of(HALO + at, 16), GROUP), :], weight[...], preferred_element_type=F32
            )
            half = 0.5 * gate.astype(BF16).astype(F32)
            gate = half + half * jnp.tanh(half)
            size = step[strand, rows, :]
            cumulated = exact_dot(triangle, -size * rates)
            turned = cumulated.T
            size_turned = size.T
            in_map = maps[strand, rows, :STATE]
            out_map = maps[strand, rows, STATE:]
            affinity = lax.dot_general(
                out_map, in_map, (((1,), (1,)), ((), ())), preferred_element_type=F32
            ) * triangle
            parts = []
            for pair in range(4):
                mixes = []
                for h in (2 * pair, 2 * pair + 1):
                    gap = jnp.minimum(cumulated[:, h : h + 1] - turned[h : h + 1, :], 0.0)
                    mixes.append((affinity * jnp.exp(gap) * size_turned[h : h + 1, :]).astype(BF16))
                x = xs[strand, rows, 128 * pair : 128 * pair + 128]
                zero = jnp.zeros_like(x)
                tall = jnp.concatenate([jnp.where(left, x, zero), jnp.where(left, zero, x)], axis=0)
                parts.append(jnp.dot(jnp.concatenate(mixes, axis=1), tall, preferred_element_type=F32))
            within = jnp.concatenate(parts, axis=1)
            grown = exact_dot(jnp.exp(cumulated), expand)
            entering = jnp.dot(out_map, starts[strand, g], preferred_element_type=F32) * grown
            local[strand, rows, :] = (within + entering) * gate
            earlier = exact_dot(jnp.broadcast_to(jnp.exp(before), (8, 128)), expand)[0:1]
            carry[strand, rows, :] = grown * earlier * gate
            return before + cumulated[GROUP - 1 :, :]

        lax.fori_loop(0, SPAN // GROUP, one_group, jnp.zeros((1, 128), F32))
        return 0

    lax.fori_loop(0, 2, one_strand, 0)


def finish_kernel(*refs):
    came, refs = refs[:7], refs[7:]
    units, refs = refs[:8], refs[8:]
    prm, maps, local, carry, mine, other, weight, states, entering, wsem, ssem = refs
    z, yl, c, _, _, t = place()
    copies = [pltpu.make_async_copy(came[n], states.at[n], ssem.at[n]) for n in range(7)]
    for n, (unit, f) in enumerate(zip(units, weight_rows())):
        for half in range(2):
            copies.append(
                pltpu.make_async_copy(
                    unit.at[pl.ds(128 + 64 * half, 64)],
                    weight.at[half, pl.ds(pl.multiple_of(64 * f, 64), 64)],
                    wsem.at[2 * n + half],
                )
            )
    fetch(copies)

    def gather(strand, count, slot):
        def one(k, held):
            total, gone = held
            at = slot(k)
            total = total + jnp.exp(gone) * states[at, :STATE, :].astype(F32)
            tail = states[at, STATE:, :].astype(F32)
            return total, gone + tail[0:1] + tail[1:2]

        total, _ = lax.fori_loop(0, count, one, (jnp.zeros((STATE, OWN), F32), jnp.zeros((1, OWN), F32)))
        entering[strand] = total.astype(BF16)

    gather(0, z, lambda k: k)
    gather(1, Z - 1 - z, lambda k: 6 - k)
    gain = prm[5:6, :OWN]
    top = jnp.ones((8, OWN), F32)

    def one_strand(strand, _):
        def one_block(b, _):
            at = pl.multiple_of(ROWS * b, ROWS)
            rows = pl.ds(at, ROWS)
            held = jnp.dot(maps[strand, rows, STATE:], entering[strand], preferred_element_type=F32)
            gated = local[strand, rows, :] + held * carry[strand, rows, :]
            squares = lax.dot_general(
                top, gated * gated, (((1,), (1,)), ((), ())), precision=EXACT, preferred_element_type=F32
            )
            normed = (gated * gain).astype(BF16)
            place_of = jnp.where(strand == 0, b, 3 - b)
            row, core = place_of // 2, lax.rem(place_of, 2)
            row = jnp.where(row == yl, 1, 0)
            hi, lo = hi_lo(squares[0:1])
            line = iota2((8, ROWS), 0)
            tail = jnp.where(line == 0, hi, jnp.where(line == 1, lo, 0.0))

            def put(ref):
                lines = pl.ds(pl.multiple_of(ROWS * strand, ROWS), ROWS)
                for half in range(2):
                    ref[row, lines, 512 * half : 512 * half + 512] = jnp.dot(
                        normed, weight[half], preferred_element_type=F32
                    ).astype(BF16)
                lanes = pl.ds(pl.multiple_of(ROWS * strand, ROWS), ROWS)
                ref[row, 2 * ROWS :, lanes] = jnp.concatenate([tail, jnp.zeros_like(tail)], axis=0).astype(BF16)

            @pl.when(core == c)
            def _():
                put(mine)

            @pl.when(core != c)
            def _():
                put(other)

            return 0

        return lax.fori_loop(0, SPAN // ROWS, one_block, 0)

    for n in range(2):
        mine[n, 2 * ROWS :, 2 * ROWS :] = jnp.zeros((HALO, D - 2 * ROWS), BF16)
        other[n, 2 * ROWS :, 2 * ROWS :] = jnp.zeros((HALO, D - 2 * ROWS), BF16)
    lax.fori_loop(0, 2, one_strand, 0)


def pair_sum(mine, came, out):
    main = mine[0, : 2 * ROWS, :].astype(F32) + came[0, : 2 * ROWS, :].astype(F32)
    out[: 2 * ROWS, :] = main.astype(BF16)
    tail = mine[0, 2 * ROWS :, :].astype(F32) + came[0, 2 * ROWS :, :].astype(F32)
    hi, lo = hi_lo(tail[0:1] + tail[1:2])
    line = iota2((HALO, D), 0)
    out[2 * ROWS :, :] = jnp.where(line == 0, hi, jnp.where(line == 1, lo, 0.0)).astype(BF16)


def last_kernel(mine, came, far, out):
    def tail(ref):
        rows = ref[2 * ROWS :, :].astype(F32)
        return rows[0:1] + rows[1:2]

    squares = tail(mine.at[1]) + tail(came.at[1]) + tail(far)
    diagonal = iota2((ROWS, ROWS), 0) == iota2((ROWS, ROWS), 1)
    for strand in range(2):
        rows = slice(ROWS * strand, ROWS * strand + ROWS)
        mean = jnp.sum(jnp.where(diagonal, squares[:, rows], 0.0), axis=1, keepdims=True) * (1.0 / E)
        main = mine[1, rows, :].astype(F32) + came[1, rows, :].astype(F32) + far[rows, :].astype(F32)
        block = (main * lax.rsqrt(mean + 1e-05)).astype(BF16)
        if strand:
            block = flipped(block)
        out[:, D * strand : D * strand + D] = block


def shape(*dims, dtype=BF16):
    return jax.ShapeDtypeStruct(dims, dtype)


def gathered(own, other):
    far = move(other, lambda z, yl, c, yh, x: dict(yl=1 - yl, yh=1 - yh))
    units = []
    for base in (own, far):
        units.append(base)
        for k in (1, 2, 3):
            units.append(move(base, lambda z, yl, c, yh, x, k=k: dict(x=(x + k) % 4)))
    return units


def swap_core(value):
    return move(value, lambda z, yl, c, yh, x: dict(c=1 - c))


def swap_y(value):
    return move(value, lambda z, yl, c, yh, x: dict(yl=1 - yl))


def halo_step(same):
    def to(z, yl, c, yh, x):
        t = 2 * yl + c
        if t == 3 and z < Z - 1:
            return dict(z=z + 1, yl=1 if same else 0)
        if t == 0 and z > 0:
            return dict(z=z - 1, yl=0 if same else 1)
        return None

    return to


def body(hidden, tokens, base_bias, in_weight, conv_weight, conv_bias, dt_bias, decay_rate, norm_gain, out_weight):
    ua, ua_other, ub, ub_other, prm = pl.pallas_call(
        pack_weights,
        out_shape=[
            shape(128, WA),
            shape(128, WA),
            shape(256, OWN),
            shape(256, OWN),
            shape(8, WA, dtype=F32),
        ],
        in_specs=[VMEM] * 7,
        out_specs=[VMEM] * 5,
        scratch_shapes=[pltpu.VMEM((8, E), F32)],
        name="pack_weights",
        **params(40),
    )(
        in_weight,
        out_weight,
        conv_weight,
        conv_bias[None],
        dt_bias[None],
        decay_rate[None],
        norm_gain[None],
    )
    act, halo = pl.pallas_call(
        prepare_inputs,
        out_shape=[shape(2 * ROWS, D), shape(HALO, D)],
        in_specs=[VMEM] * 3,
        out_specs=[VMEM] * 2,
        name="prepare_inputs",
        **params(40),
    )(hidden[0], tokens, jnp.pad(base_bias, ((0, 3), (0, 0))))
    wa = gathered(ua, ua_other)
    act_y = swap_y(act)
    halo_a = move(halo, halo_step(True))
    halo_b = move(halo, halo_step(False))
    act_c = swap_core(act)
    halo_c = swap_core(halo_a + halo_b)
    act_yc = swap_core(act_y)
    wb = gathered(ub, ub_other)
    blocks = (act, act_y, act_c, act_yc)
    xs, maps, step, starts, *sends = pl.pallas_call(
        scan_kernel,
        out_shape=[
            shape(2, SPAN, OWN),
            shape(2, SPAN, 2 * STATE),
            shape(2, SPAN, 128, dtype=F32),
            shape(2, SPAN // GROUP, STATE, OWN),
        ]
        + [shape(STATE + HALO, OWN)] * 7,
        in_specs=[ANY] * 15 + [VMEM],
        out_specs=[VMEM] * 4 + [ANY] * 7,
        scratch_shapes=[
            pltpu.VMEM((2, PAD, D), BF16),
            pltpu.VMEM((3, HALO, D), BF16),
            pltpu.VMEM((D, WA), BF16),
            pltpu.VMEM((PAD, WA), F32),
            pltpu.VMEM((2, STATE + HALO, OWN), BF16),
            pltpu.SemaphoreType.DMA((8,)),
            pltpu.SemaphoreType.DMA((3,)),
            pltpu.SemaphoreType.DMA((8,)),
            pltpu.SemaphoreType.DMA((7,)),
        ],
        name="scan_kernel",
        **params(56, flops=2 * 1056 * D * WA, bytes_accessed=8 << 20),
    )(*blocks, halo_a, halo_b, halo_c, *wa, prm)
    came = [
        move(sends[k - 1], lambda z, yl, c, yh, x, k=k: dict(z=(z + k) % Z)) for k in range(1, Z)
    ]
    local, carry = pl.pallas_call(
        local_kernel,
        out_shape=[shape(2, SPAN, OWN, dtype=F32)] * 2,
        in_specs=[ANY] * 12 + [VMEM] * 5,
        out_specs=[VMEM] * 2,
        scratch_shapes=[
            pltpu.VMEM((2, PAD, D), BF16),
            pltpu.VMEM((D, OWN), BF16),
            pltpu.SemaphoreType.DMA((8,)),
            pltpu.SemaphoreType.DMA((8,)),
        ],
        name="local_kernel",
        **params(56, flops=4 * 1024 * D * OWN, bytes_accessed=16 << 20),
    )(*blocks, *wb, prm, xs, maps, step, starts)
    mine, other = pl.pallas_call(
        finish_kernel,
        out_shape=[shape(2, 2 * ROWS + HALO, D)] * 2,
        in_specs=[ANY] * 15 + [VMEM] * 4,
        out_specs=[VMEM] * 2,
        scratch_shapes=[
            pltpu.VMEM((2, OWN, 512), BF16),
            pltpu.VMEM((7, STATE + HALO, OWN), BF16),
            pltpu.VMEM((2, STATE, OWN), BF16),
            pltpu.SemaphoreType.DMA((16,)),
            pltpu.SemaphoreType.DMA((7,)),
        ],
        name="finish_kernel",
        **params(56, flops=2 * 1024 * D * OWN, bytes_accessed=8 << 20),
    )(*came, *wb, prm, maps, local, carry)
    core_sum = swap_core(other)
    part = pl.pallas_call(
        pair_sum,
        out_shape=shape(2 * ROWS + HALO, D),
        in_specs=[VMEM] * 2,
        out_specs=VMEM,
        name="pair_sum",
        **params(40),
    )(mine, core_sum)
    far = swap_y(part)
    out = pl.pallas_call(
        last_kernel,
        out_shape=shape(ROWS, 2 * D),
        in_specs=[VMEM] * 3,
        out_specs=VMEM,
        name="last_kernel",
        **params(40),
    )(mine, core_sum, far)
    return out[None]


def solution(mesh):
    placed = (
        P("fsdp", "seq", None),
        P("fsdp", "seq"),
        P(),
        P("fsdp", None),
        P(),
        P(),
        P(),
        P(),
        P(),
        P("fsdp", None),
    )
    return jax.shard_map(
        body, mesh=mesh, in_specs=placed, out_specs=P("fsdp", "seq", None), check_vma=False
    )
```

time: 661 us -> 144 us (0.22)
  waiting for transfers between devices: 469 us -> 33 us
  other arithmetic: 74.6 us -> 0.01 us
  Pallas kernels: 0 us -> 46.6 us
  blocking collectives: 34.1 us -> 0 us
  starting transfers between devices: 25 us -> 55.8 us
  matrix products: 28.3 us -> 0 us
  between operations: 13.4 us -> 0.5 us
    all_gather x3 -> x0, waiting for transfers between devices: 394 us -> none  [the longest x1 308 us: carried_in_2(): pieces = jax.tree.map(lambda part: lax.all_gather(part, axis), value)]
    select_n x32 -> x0, other arithmetic: 65.4 us -> none  [the longest x31 64.8 us: turn(): jnp.where(position < mine, new, old)]
    pallas_call x0 -> x7, Pallas kernels: none -> 46.6 us  [the longest x1 15.5 us: body(): pl.pallas_call(scan_kernel, out_shape=[shape(2, SPAN, OWN), shape(2, SPAN...]
    ppermute x11 -> x29, waiting for transfers between devices: 73.7 us -> 33 us  [move(): return lax.ppermute(value, ('seq', 'fsdp'), pairs)]
    all_gather x1 -> x0, blocking collectives: 34.1 us -> none  [carried_in_2(): pieces = jax.tree.map(lambda part: lax.all_gather(part, axis), value)]
    ppermute x11 -> x29, starting transfers between devices: 24.9 us -> 55.8 us  [move(): return lax.ppermute(value, ('seq', 'fsdp'), pairs)]
    dot_general x9 -> x0, matrix products: 28.3 us -> none  [the longest x1 7.44 us: body(): jnp.dot(columns, lax.all_gather(in_weight, 'fsdp', axis=0, tiled=True), p...]
  transfers between devices with their start and end apart: 14 -> 29, of which waited for: 13 -> 10; matrix products, arithmetic and copies ran while one was open for 14% -> 2% of each run, Pallas kernels for 0% -> 22%
where the time goes in v1:
time: 144 us; the launch traced here: 143 us
  starting transfers between devices  55.8 us (39%)
  Pallas kernels  46.6 us (32%)
  waiting for transfers between devices  33 us (23%)
  local copies, waits for them, and re-layouts  7.58 us (5%)
    ppermute x29, starting transfers between devices, move(): return lax.ppermute(value, ('seq', 'fsdp'), pairs)  55.8 us
    ppermute x29, waiting for transfers between devices, move(): return lax.ppermute(value, ('seq', 'fsdp'), pairs)  33 us
    pallas_call x1, Pallas kernels, body(): pl.pallas_call(scan_kernel, out_shape=[shape(2, SPAN, OWN), shape(2, SPAN...  15.5 us
    pallas_call x1, Pallas kernels, body(): pl.pallas_call(local_kernel, out_shape=[shape(2, SPAN, OWN, dtype=F32)] *...  15.5 us
    pallas_call x1, Pallas kernels, body(): pl.pallas_call(finish_kernel, out_shape=[shape(2, 2 * ROWS + HALO, D)] *...  12.6 us
    unnamed x79, local copies, waits for them, and re-layouts  6.1 us
  transfers between devices with their start and end apart: 29, of which 10 were waited for; matrix products, arithmetic and copies ran while one was open for 2% of the time, Pallas kernels for 22%

profile of v1, /device:TPU:1, one launch (start us, length us, event | category | flops | bytes accessed | tf_op | source)
XLA Modules:
  0.0 143.5 jit_solution(14791852036188306229)
XLA Ops:
  0.0 0.8 pad.4.base_bias
  0.8 1.0 copy-done.1
  1.8 0.7 copy-done.7
  2.5 0.6 prepare_inputs.1
  3.1 2.2 %collective-permute-start = (bf16[256,1024]{1,0:T(8,128)(2,1)S(1)}, bf16[256,1024]{1,0:T(8,128)(2,1)S(1)}, u32[]{:S(2)}, u32[]{:S(2)}) collective-permute-start(bf16[256,1024]{1,0:T(8,128)(2,1)S(1)} %get-tuple-element.27.refs_0_), channel_id=1, source_target_pairs={{0,16},{1,17},{2,18},{3,19},{4,20},{5,21},{6,22},{7,23},{8,24},{9,... | collective-permute-start | bytes 1572872 | tf_op jit(solution)/shard_map/ppermute | solution.py:48
  5.3 0.7 broadcast_in_dim.15.cb
  6.1 1.7 %copy.11.iw = bf16[128,4384]{1,0:T(8,128)(2,1)S(1)} copy(bf16[128,4384]{0,1:T(8,128)(2,1)} %param.13) | data formatting | bytes 2244608 | tf_op args[3]
  7.9 0.9 pack_weights.1
  8.8 0.6 copy-done.5
  9.4 1.9 %collective-permute-start.9 = (bf16[128,896]{1,0:T(8,128)(2,1)S(1)}, bf16[128,896]{1,0:T(8,128)(2,1)S(1)}, u32[]{:S(2)}, u32[]{:S(2)}) collective-permute-start(bf16[128,896]{1,0:T(8,128)(2,1)S(1)} %get-tuple-element.30), channel_id=1, source_target_pairs={{0,20},{1,21},{2,22},{3,23},{4,16},{5,17},{6,18},{7,19},{8,28},{9,... | collective-permute-start | bytes 688136 | tf_op jit(solution)/shard_map/ppermute | solution.py:48
  11.3 2.5 %collective-permute-start.8 = (bf16[128,896]{1,0:T(8,128)(2,1)S(1)}, bf16[128,896]{1,0:T(8,128)(2,1)S(1)}, u32[]{:S(2)}, u32[]{:S(2)}) collective-permute-start(bf16[128,896]{1,0:T(8,128)(2,1)S(1)} %get-tuple-element.29.refs_7_), channel_id=1, source_target_pairs={{0,3},{1,0},{2,1},{3,2},{4,7},{5,4},{6,5},{7,6},{8,11},{9,8},{10,9... | collective-permute-start | bytes 688136 | tf_op jit(solution)/shard_map/ppermute | solution.py:48
  13.8 0.5 collective-permute-start.7
  14.3 0.7 collective-permute-start.4
  15.0 0.7 collective-permute-start.3
  15.7 9.9 %collective-permute-start.5 = (bf16[16,1024]{1,0:T(8,128)(2,1)S(1)}, bf16[16,1024]{1,0:T(8,128)(2,1)S(1)}, u32[]{:S(2)}, u32[]{:S(2)}) collective-permute-start(bf16[16,1024]{1,0:T(8,128)(2,1)S(1)} %add.5), channel_id=1, source_target_pairs={{0,8},{1,9},{2,10},{3,11},{4,12},{5,13},{6,14},{7,15},{8,0},{9,1},... | collective-permute-start | bytes 98312 | tf_op jit(solution)/shard_map/ppermute | solution.py:48
  25.6 0.9 collective-permute-done.5.refs_6_
  26.5 0.7 collective-permute-start.6
  27.2 0.7 collective-permute-start.1
  28.0 2.1 %collective-permute-start.22 = (bf16[256,512]{1,0:T(8,128)(2,1)S(1)}, bf16[256,512]{1,0:T(8,128)(2,1)S(1)}, u32[]{:S(2)}, u32[]{:S(2)}) collective-permute-start(bf16[256,512]{1,0:T(8,128)(2,1)S(1)} %get-tuple-element.39.refs_4_.refs_7_), channel_id=1, source_target_pairs={{0,3},{1,0},{2,1},{3,2},{4,7},{5,4},{6,5},{7,6},{8,11},{9,8},{10,9... | collective-permute-start | bytes 786440 | tf_op jit(solution)/shard_map/ppermute | solution.py:48
  30.1 4.5 %collective-permute-done.6.refs_8_ = bf16[128,896]{1,0:T(8,128)(2,1)S(1)} collective-permute-done((bf16[128,896]{1,0:T(8,128)(2,1)S(1)}, bf16[128,896]{1,0:T(8,128)(2,1)S(1)}, u32[]{:S(2)}, u32[]{:S(2)}) %collective-permute-start.6) | collective-permute-done | bytes 229408 | tf_op jit(solution)/shard_map/ppermute | solution.py:48
  34.6 0.4 collective-permute-start.12
  35.0 0.2 collective-permute-done.23.refs_8_.refs_11_
  35.2 2.5 %collective-permute-start.11 = (bf16[128,896]{1,0:T(8,128)(2,1)S(1)}, bf16[128,896]{1,0:T(8,128)(2,1)S(1)}, u32[]{:S(2)}, u32[]{:S(2)}) collective-permute-start(bf16[128,896]{1,0:T(8,128)(2,1)S(1)} %collective-permute-done.9.refs_11_), channel_id=1, source_target_pairs={{0,2},{1,3},{2,0},{3,1},{4,6},{5,7},{6,4},{7,5},{8,10},{9,11},{10,... | collective-permute-start | bytes 688136 | tf_op jit(solution)/shard_map/ppermute | solution.py:48
  37.7 3.3 %collective-permute-done.12.refs_14_ = bf16[128,896]{1,0:T(8,128)(2,1)S(1)} collective-permute-done((bf16[128,896]{1,0:T(8,128)(2,1)S(1)}, bf16[128,896]{1,0:T(8,128)(2,1)S(1)}, u32[]{:S(2)}, u32[]{:S(2)}) %collective-permute-start.12) | collective-permute-done | bytes 229408 | tf_op jit(solution)/shard_map/ppermute | solution.py:48
  41.0 0.9 collective-permute-start.21
  41.9 0.8 collective-permute-done.11.refs_13_
  42.7 3.4 %collective-permute-start.20 = (bf16[256,512]{1,0:T(8,128)(2,1)S(1)}, bf16[256,512]{1,0:T(8,128)(2,1)S(1)}, u32[]{:S(2)}, u32[]{:S(2)}) collective-permute-start(bf16[256,512]{1,0:T(8,128)(2,1)S(1)} %get-tuple-element.39.refs_4_.refs_7_), channel_id=1, source_target_pairs={{0,1},{1,2},{2,3},{3,0},{4,5},{5,6},{6,7},{7,4},{8,9},{9,10},{10,1... | collective-permute-start | bytes 786440 | tf_op jit(solution)/shard_map/ppermute | solution.py:48
  46.1 3.9 %collective-permute-done.10.refs_12_ = bf16[128,896]{1,0:T(8,128)(2,1)S(1)} collective-permute-done((bf16[128,896]{1,0:T(8,128)(2,1)S(1)}, bf16[128,896]{1,0:T(8,128)(2,1)S(1)}, u32[]{:S(2)}, u32[]{:S(2)}) %collective-permute-start.10) | collective-permute-done | bytes 229408 | tf_op jit(solution)/shard_map/ppermute | solution.py:48
  50.0 0.4 collective-permute-start.25
  50.4 1.1 collective-permute-start.24
  51.7 15.5 %scan_kernel.1 = (bf16[2,512,512]{2,1,0:T(8,128)(2,1)}, bf16[2,512,256]{2,1,0:T(8,128)(2,1)}, f32[2,512,128]{2,1,0:T(8,128)}, bf16[2,4,128,512]{3,2,1,0:T(8,128)...) custom-call(bf16[256,1024]{1,0:T(8,128)(2,1)} %copy-done.10, ...), custom_call_target="tpu_custom_call" | custom-call | flops 1937768448 | bytes 8388608 | tf_op jit(solution)/shard_map/scan_kernel/pallas_call | solution.py:490
  67.2 1.8 %collective-permute-start.13 = (bf16[144,512]{1,0:T(8,128)(2,1)}, bf16[144,512]{1,0:T(8,128)(2,1)S(1)}, u32[]{:S(2)}, u32[]{:S(2)}) collective-permute-start(bf16[144,512]{1,0:T(8,128)(2,1)} %get-tuple-element.32), channel_id=1, source_target_pairs={{0,32},{1,33},{2,34},{3,35},{4,36},{5,37},{6,38},{7,39},{8,40},{9,... | collective-permute-start | bytes 442376 | tf_op jit(solution)/shard_map/ppermute | solution.py:48
  69.1 4.2 %collective-permute-start.14 = (bf16[144,512]{1,0:T(8,128)(2,1)}, bf16[144,512]{1,0:T(8,128)(2,1)S(1)}, u32[]{:S(2)}, u32[]{:S(2)}) collective-permute-start(bf16[144,512]{1,0:T(8,128)(2,1)} %get-tuple-element.33), channel_id=1, source_target_pairs={{0,64},{1,65},{2,66},{3,67},{4,68},{5,69},{6,70},{7,71},{8,72},{9,... | collective-permute-start | bytes 442376 | tf_op jit(solution)/shard_map/ppermute | solution.py:48
  73.3 3.4 %collective-permute-start.15 = (bf16[144,512]{1,0:T(8,128)(2,1)}, bf16[144,512]{1,0:T(8,128)(2,1)S(1)}, u32[]{:S(2)}, u32[]{:S(2)}) collective-permute-start(bf16[144,512]{1,0:T(8,128)(2,1)} %get-tuple-element.34), channel_id=1, source_target_pairs={{0,96},{1,97},{2,98},{3,99},{4,100},{5,101},{6,102},{7,103},{8,104... | collective-permute-start | bytes 442376 | tf_op jit(solution)/shard_map/ppermute | solution.py:48
  76.7 4.3 %collective-permute-start.17 = (bf16[144,512]{1,0:T(8,128)(2,1)}, bf16[144,512]{1,0:T(8,128)(2,1)S(1)}, u32[]{:S(2)}, u32[]{:S(2)}) collective-permute-start(bf16[144,512]{1,0:T(8,128)(2,1)} %get-tuple-element.36), channel_id=1, source_target_pairs={{0,160},{1,161},{2,162},{3,163},{4,164},{5,165},{6,166},{7,167},{8... | collective-permute-start | bytes 442376 | tf_op jit(solution)/shard_map/ppermute | solution.py:48
  81.0 3.0 %collective-permute-start.18 = (bf16[144,512]{1,0:T(8,128)(2,1)}, bf16[144,512]{1,0:T(8,128)(2,1)S(1)}, u32[]{:S(2)}, u32[]{:S(2)}) collective-permute-start(bf16[144,512]{1,0:T(8,128)(2,1)} %get-tuple-element.37), channel_id=1, source_target_pairs={{0,192},{1,193},{2,194},{3,195},{4,196},{5,197},{6,198},{7,199},{8... | collective-permute-start | bytes 442376 | tf_op jit(solution)/shard_map/ppermute | solution.py:48
  84.1 15.5 %local_kernel.1 = (f32[2,512,512]{2,1,0:T(8,128)}, f32[2,512,512]{2,1,0:T(8,128)}) custom-call(bf16[256,1024]{1,0:T(8,128)(2,1)} %copy-done.10, bf16[256,1024]{1,0:T(8,128)(2,1)} %copy-done.28, bf16[256,1024]{1,0:T(8,128)(2,1)} %copy-done.29, bf16[256,1024]{1,0:T(8,128)(2,1)} %copy-done.30, bf16[256,512]{1,0:T(8,128)(2,1)} %copy-done.3, ...), custom_call_target="tpu_custom_call" | custom-call | flops 2147483648 | bytes 16777216 | tf_op jit(solution)/shard_map/local_kernel/pallas_call | solution.py:518
  99.7 0.4 collective-permute-done.18.refs_5_
  100.0 3.9 %collective-permute-done.19.refs_6_ = bf16[144,512]{1,0:T(8,128)(2,1)S(1)} collective-permute-done((bf16[144,512]{1,0:T(8,128)(2,1)}, bf16[144,512]{1,0:T(8,128)(2,1)S(1)}, u32[]{:S(2)}, u32[]{:S(2)}) %collective-permute-start.19) | collective-permute-done | bytes 147488 | tf_op jit(solution)/shard_map/ppermute | solution.py:48
  103.9 0.6 copy-done.25
  104.6 12.6 %finish_kernel.1 = (bf16[2,272,1024]{2,1,0:T(8,128)(2,1)}, bf16[2,272,1024]{2,1,0:T(8,128)(2,1)}) custom-call(bf16[144,512]{1,0:T(8,128)(2,1)} %copy-done.19, bf16[144,512]{1,0:T(8,128)(2,1)} %copy-done.20, bf16[144,512]{1,0:T(8,128)(2,1)} %copy-done.21, bf16[144,512]{1,0:T(8,128)(2,1)} %copy-done.22, bf16[144,512]{1,0:T(8,128)(2,1)} %copy-done.23, ...), custom_call_target="tpu_custom_call" | custom-call | flops 1073741824 | bytes 8388608 | tf_op jit(solution)/shard_map/finish_kernel/pallas_call | solution.py:532
  117.2 6.7 %collective-permute-start.27 = (bf16[2,272,1024]{2,1,0:T(8,128)(2,1)}, bf16[2,272,1024]{2,1,0:T(8,128)(2,1)S(1)}, u32[]{:S(2)}, u32[]{:S(2)}) collective-permute-start(bf16[2,272,1024]{2,1,0:T(8,128)(2,1)} %get-tuple-element.48), channel_id=1, source_target_pairs={{0,8},{1,9},{2,10},{3,11},{4,12},{5,13},{6,14},{7,15},{8,0},{9,1},... | collective-permute-start | bytes 3342344 | tf_op jit(solution)/shard_map/ppermute | solution.py:48
  123.9 2.6 %collective-permute-done.27.came = bf16[2,272,1024]{2,1,0:T(8,128)(2,1)S(1)} collective-permute-done((bf16[2,272,1024]{2,1,0:T(8,128)(2,1)}, bf16[2,272,1024]{2,1,0:T(8,128)(2,1)S(1)}, u32[]{:S(2)}, u32[]{:S(2)}) %collective-permute-start.27) | collective-permute-done | bytes 1114144 | tf_op jit(solution)/shard_map/ppermute | solution.py:48
  126.5 1.2 copy-done
  127.7 0.1 pair_sum.1
  127.9 1.7 %collective-permute-start.28 = (bf16[272,1024]{1,0:T(8,128)(2,1)S(1)}, bf16[272,1024]{1,0:T(8,128)(2,1)S(1)}, u32[]{:S(2)}, u32[]{:S(2)}) collective-permute-start(bf16[272,1024]{1,0:T(8,128)(2,1)S(1)} %pair_sum.1), channel_id=1, source_target_pairs={{0,16},{1,17},{2,18},{3,19},{4,20},{5,21},{6,22},{7,23},{8,24},{9,... | collective-permute-start | bytes 1671176 | tf_op jit(solution)/shard_map/ppermute | solution.py:48
  129.6 12.6 %collective-permute-done.28.far = bf16[272,1024]{1,0:T(8,128)(2,1)S(1)} collective-permute-done((bf16[272,1024]{1,0:T(8,128)(2,1)S(1)}, bf16[272,1024]{1,0:T(8,128)(2,1)S(1)}, u32[]{:S(2)}, u32[]{:S(2)}) %collective-permute-start.28) | collective-permute-done | bytes 557088 | tf_op jit(solution)/shard_map/ppermute | solution.py:48
  142.2 1.3 last_kernel.1
  (99 shorter events, 0.3 us)
Async XLA Ops:
  3.1 24.1 %copy-start.10 = (bf16[256,1024]{1,0:T(8,128)(2,1)}, bf16[256,1024]{1,0:T(8,128)(2,1)S(1)}, u32[]{:S(2)}) copy-start(bf16[256,1024]{1,0:T(8,128)(2,1)S(1)} %get-tuple-element.27.refs_0_) | copy-start | bytes 1572868
  3.1 24.8 %collective-permute-start = (bf16[256,1024]{1,0:T(8,128)(2,1)S(1)}, bf16[256,1024]{1,0:T(8,128)(2,1)S(1)}, u32[]{:S(2)}, u32[]{:S(2)}) collective-permute-start(bf16[256,1024]{1,0:T(8,128)(2,1)S(1)} %get-tuple-element.27.refs_0_), channel_id=1, source_target_pairs={{0,16},{1,17},{2,18},{3,19},{4,20},{5,21},{6,22},{7,23},{8,24},{9,... | collective-permute-start | bytes 1572872 | tf_op jit(solution)/shard_map/ppermute | solution.py:48
  9.4 42.1 %copy-start.11 = (bf16[128,896]{1,0:T(8,128)(2,1)}, bf16[128,896]{1,0:T(8,128)(2,1)S(1)}, u32[]{:S(2)}) copy-start(bf16[128,896]{1,0:T(8,128)(2,1)S(1)} %get-tuple-element.29.refs_7_) | copy-start | bytes 688132
  9.4 57.8 %copy-start.3 = (bf16[256,512]{1,0:T(8,128)(2,1)}, bf16[256,512]{1,0:T(8,128)(2,1)S(1)}, u32[]{:S(2)}) copy-start(bf16[256,512]{1,0:T(8,128)(2,1)S(1)} %get-tuple-element.39.refs_4_.refs_7_) | copy-start | bytes 786436
  9.4 17.1 %collective-permute-start.9 = (bf16[128,896]{1,0:T(8,128)(2,1)S(1)}, bf16[128,896]{1,0:T(8,128)(2,1)S(1)}, u32[]{:S(2)}, u32[]{:S(2)}) collective-permute-start(bf16[128,896]{1,0:T(8,128)(2,1)S(1)} %get-tuple-element.30), channel_id=1, source_target_pairs={{0,20},{1,21},{2,22},{3,23},{4,16},{5,17},{6,18},{7,19},{8,28},{9,... | collective-permute-start | bytes 688136 | tf_op jit(solution)/shard_map/ppermute | solution.py:48
  11.3 15.9 %collective-permute-start.8 = (bf16[128,896]{1,0:T(8,128)(2,1)S(1)}, bf16[128,896]{1,0:T(8,128)(2,1)S(1)}, u32[]{:S(2)}, u32[]{:S(2)}) collective-permute-start(bf16[128,896]{1,0:T(8,128)(2,1)S(1)} %get-tuple-element.29.refs_7_), channel_id=1, source_target_pairs={{0,3},{1,0},{2,1},{3,2},{4,7},{5,4},{6,5},{7,6},{8,11},{9,8},{10,9... | collective-permute-start | bytes 688136 | tf_op jit(solution)/shard_map/ppermute | solution.py:48
  13.8 14.2 %collective-permute-start.7 = (bf16[128,896]{1,0:T(8,128)(2,1)S(1)}, bf16[128,896]{1,0:T(8,128)(2,1)S(1)}, u32[]{:S(2)}, u32[]{:S(2)}) collective-permute-start(bf16[128,896]{1,0:T(8,128)(2,1)S(1)} %get-tuple-element.29.refs_7_), channel_id=1, source_target_pairs={{0,2},{1,3},{2,0},{3,1},{4,6},{5,7},{6,4},{7,5},{8,10},{9,11},{10,... | collective-permute-start | bytes 688136 | tf_op jit(solution)/shard_map/ppermute | solution.py:48
  14.3 0.7 collective-permute-start.4
  15.0 36.6 %copy-start.26 = (bf16[16,1024]{1,0:T(8,128)(2,1)}, bf16[16,1024]{1,0:T(8,128)(2,1)S(1)}, u32[]{:S(2)}) copy-start(bf16[16,1024]{1,0:T(8,128)(2,1)S(1)} %collective-permute-done.4.refs_5_) | copy-start | bytes 98308
  15.0 0.7 collective-permute-start.3
  15.7 35.9 %copy-start.27 = (bf16[16,1024]{1,0:T(8,128)(2,1)}, bf16[16,1024]{1,0:T(8,128)(2,1)S(1)}, u32[]{:S(2)}) copy-start(bf16[16,1024]{1,0:T(8,128)(2,1)S(1)} %collective-permute-done.3.refs_4_) | copy-start | bytes 98308
  15.7 10.8 %collective-permute-start.5 = (bf16[16,1024]{1,0:T(8,128)(2,1)S(1)}, bf16[16,1024]{1,0:T(8,128)(2,1)S(1)}, u32[]{:S(2)}, u32[]{:S(2)}) collective-permute-start(bf16[16,1024]{1,0:T(8,128)(2,1)S(1)} %add.5), channel_id=1, source_target_pairs={{0,8},{1,9},{2,10},{3,11},{4,12},{5,13},{6,14},{7,15},{8,0},{9,1},... | collective-permute-start | bytes 98312 | tf_op jit(solution)/shard_map/ppermute | solution.py:48
  26.5 25.1 %copy-start.38 = (bf16[16,1024]{1,0:T(8,128)(2,1)}, bf16[16,1024]{1,0:T(8,128)(2,1)S(1)}, u32[]{:S(2)}) copy-start(bf16[16,1024]{1,0:T(8,128)(2,1)S(1)} %collective-permute-done.5.refs_6_) | copy-start | bytes 98308
  26.5 8.8 %collective-permute-start.23 = (bf16[256,512]{1,0:T(8,128)(2,1)S(1)}, bf16[256,512]{1,0:T(8,128)(2,1)S(1)}, u32[]{:S(2)}, u32[]{:S(2)}) collective-permute-start(bf16[256,512]{1,0:T(8,128)(2,1)S(1)} %get-tuple-element.40), channel_id=1, source_target_pairs={{0,20},{1,21},{2,22},{3,23},{4,16},{5,17},{6,18},{7,19},{8,28},{9,... | collective-permute-start | bytes 786440 | tf_op jit(solution)/shard_map/ppermute | solution.py:48
  26.5 25.1 %copy-start.31 = (bf16[128,896]{1,0:T(8,128)(2,1)}, bf16[128,896]{1,0:T(8,128)(2,1)S(1)}, u32[]{:S(2)}) copy-start(bf16[128,896]{1,0:T(8,128)(2,1)S(1)} %collective-permute-done.9.refs_11_) | copy-start | bytes 688132
  26.5 8.1 %collective-permute-start.6 = (bf16[128,896]{1,0:T(8,128)(2,1)S(1)}, bf16[128,896]{1,0:T(8,128)(2,1)S(1)}, u32[]{:S(2)}, u32[]{:S(2)}) collective-permute-start(bf16[128,896]{1,0:T(8,128)(2,1)S(1)} %get-tuple-element.29.refs_7_), channel_id=1, source_target_pairs={{0,1},{1,2},{2,3},{3,0},{4,5},{5,6},{6,7},{7,4},{8,9},{9,10},{10,1... | collective-permute-start | bytes 688136 | tf_op jit(solution)/shard_map/ppermute | solution.py:48
  27.2 24.4 %copy-start.32 = (bf16[128,896]{1,0:T(8,128)(2,1)}, bf16[128,896]{1,0:T(8,128)(2,1)S(1)}, u32[]{:S(2)}) copy-start(bf16[128,896]{1,0:T(8,128)(2,1)S(1)} %collective-permute-done.8.refs_10_) | copy-start | bytes 688132
  27.2 22.8 %collective-permute-start.1 = (bf16[256,1024]{1,0:T(8,128)(2,1)S(1)}, bf16[256,1024]{1,0:T(8,128)(2,1)S(1)}, u32[]{:S(2)}, u32[]{:S(2)}) collective-permute-start(bf16[256,1024]{1,0:T(8,128)(2,1)S(1)} %get-tuple-element.27.refs_0_), channel_id=1, source_target_pairs={{0,8},{1,9},{2,10},{3,11},{4,12},{5,13},{6,14},{7,15},{8,0},{9,1},... | collective-permute-start | bytes 1572872 | tf_op jit(solution)/shard_map/ppermute | solution.py:48
  27.9 23.7 %copy-start.28 = (bf16[256,1024]{1,0:T(8,128)(2,1)}, bf16[256,1024]{1,0:T(8,128)(2,1)S(1)}, u32[]{:S(2)}) copy-start(bf16[256,1024]{1,0:T(8,128)(2,1)S(1)} %collective-permute-done.refs_1_) | copy-start | bytes 1572868
  27.9 22.5 %collective-permute-start.2 = (bf16[256,1024]{1,0:T(8,128)(2,1)S(1)}, bf16[256,1024]{1,0:T(8,128)(2,1)S(1)}, u32[]{:S(2)}, u32[]{:S(2)}) collective-permute-start(bf16[256,1024]{1,0:T(8,128)(2,1)S(1)} %collective-permute-done.refs_1_), channel_id=1, source_target_pairs={{0,8},{1,9},{2,10},{3,11},{4,12},{5,13},{6,14},{7,15},{8,0},{9,1},... | collective-permute-start | bytes 1572872 | tf_op jit(solution)/shard_map/ppermute | solution.py:48
  28.0 23.6 %copy-start.33 = (bf16[128,896]{1,0:T(8,128)(2,1)}, bf16[128,896]{1,0:T(8,128)(2,1)S(1)}, u32[]{:S(2)}) copy-start(bf16[128,896]{1,0:T(8,128)(2,1)S(1)} %collective-permute-done.7.refs_9_) | copy-start | bytes 688132
  28.0 9.7 %collective-permute-start.22 = (bf16[256,512]{1,0:T(8,128)(2,1)S(1)}, bf16[256,512]{1,0:T(8,128)(2,1)S(1)}, u32[]{:S(2)}, u32[]{:S(2)}) collective-permute-start(bf16[256,512]{1,0:T(8,128)(2,1)S(1)} %get-tuple-element.39.refs_4_.refs_7_), channel_id=1, source_target_pairs={{0,3},{1,0},{2,1},{3,2},{4,7},{5,4},{6,5},{7,6},{8,11},{9,8},{10,9... | collective-permute-start | bytes 786440 | tf_op jit(solution)/shard_map/ppermute | solution.py:48
  34.6 17.0 %copy-start.34 = (bf16[128,896]{1,0:T(8,128)(2,1)}, bf16[128,896]{1,0:T(8,128)(2,1)S(1)}, u32[]{:S(2)}) copy-start(bf16[128,896]{1,0:T(8,128)(2,1)S(1)} %collective-permute-done.6.refs_8_) | copy-start | bytes 688132
  34.6 6.3 %collective-permute-start.12 = (bf16[128,896]{1,0:T(8,128)(2,1)S(1)}, bf16[128,896]{1,0:T(8,128)(2,1)S(1)}, u32[]{:S(2)}, u32[]{:S(2)}) collective-permute-start(bf16[128,896]{1,0:T(8,128)(2,1)S(1)} %collective-permute-done.9.refs_11_), channel_id=1, source_target_pairs={{0,3},{1,0},{2,1},{3,2},{4,7},{5,4},{6,5},{7,6},{8,11},{9,8},{10,9... | collective-permute-start | bytes 688136 | tf_op jit(solution)/shard_map/ppermute | solution.py:48
  35.2 32.0 %copy-start.12 = (bf16[256,512]{1,0:T(8,128)(2,1)}, bf16[256,512]{1,0:T(8,128)(2,1)S(1)}, u32[]{:S(2)}) copy-start(bf16[256,512]{1,0:T(8,128)(2,1)S(1)} %collective-permute-done.23.refs_8_.refs_11_) | copy-start | bytes 786436
  35.2 7.4 %collective-permute-start.11 = (bf16[128,896]{1,0:T(8,128)(2,1)S(1)}, bf16[128,896]{1,0:T(8,128)(2,1)S(1)}, u32[]{:S(2)}, u32[]{:S(2)}) collective-permute-start(bf16[128,896]{1,0:T(8,128)(2,1)S(1)} %collective-permute-done.9.refs_11_), channel_id=1, source_target_pairs={{0,2},{1,3},{2,0},{3,1},{4,6},{5,7},{6,4},{7,5},{8,10},{9,11},{10,... | collective-permute-start | bytes 688136 | tf_op jit(solution)/shard_map/ppermute | solution.py:48
  37.7 29.5 %copy-start.13 = (bf16[256,512]{1,0:T(8,128)(2,1)}, bf16[256,512]{1,0:T(8,128)(2,1)S(1)}, u32[]{:S(2)}) copy-start(bf16[256,512]{1,0:T(8,128)(2,1)S(1)} %collective-permute-done.22.refs_7_.refs_10_) | copy-start | bytes 786436
  37.7 12.3 %collective-permute-start.10 = (bf16[128,896]{1,0:T(8,128)(2,1)S(1)}, bf16[128,896]{1,0:T(8,128)(2,1)S(1)}, u32[]{:S(2)}, u32[]{:S(2)}) collective-permute-start(bf16[128,896]{1,0:T(8,128)(2,1)S(1)} %collective-permute-done.9.refs_11_), channel_id=1, source_target_pairs={{0,1},{1,2},{2,3},{3,0},{4,5},{5,6},{6,7},{7,4},{8,9},{9,10},{10,1... | collective-permute-start | bytes 688136 | tf_op jit(solution)/shard_map/ppermute | solution.py:48
  41.0 10.7 %copy-start.35 = (bf16[128,896]{1,0:T(8,128)(2,1)}, bf16[128,896]{1,0:T(8,128)(2,1)S(1)}, u32[]{:S(2)}) copy-start(bf16[128,896]{1,0:T(8,128)(2,1)S(1)} %collective-permute-done.12.refs_14_) | copy-start | bytes 688132
  41.0 26.2 %collective-permute-start.21 = (bf16[256,512]{1,0:T(8,128)(2,1)S(1)}, bf16[256,512]{1,0:T(8,128)(2,1)S(1)}, u32[]{:S(2)}, u32[]{:S(2)}) collective-permute-start(bf16[256,512]{1,0:T(8,128)(2,1)S(1)} %get-tuple-element.39.refs_4_.refs_7_), channel_id=1, source_target_pairs={{0,2},{1,3},{2,0},{3,1},{4,6},{5,7},{6,4},{7,5},{8,10},{9,11},{10,... | collective-permute-start | bytes 786440 | tf_op jit(solution)/shard_map/ppermute | solution.py:48
  42.7 26.4 %collective-permute-start.20 = (bf16[256,512]{1,0:T(8,128)(2,1)S(1)}, bf16[256,512]{1,0:T(8,128)(2,1)S(1)}, u32[]{:S(2)}, u32[]{:S(2)}) collective-permute-start(bf16[256,512]{1,0:T(8,128)(2,1)S(1)} %get-tuple-element.39.refs_4_.refs_7_), channel_id=1, source_target_pairs={{0,1},{1,2},{2,3},{3,0},{4,5},{5,6},{6,7},{7,4},{8,9},{9,10},{10,1... | collective-permute-start | bytes 786440 | tf_op jit(solution)/shard_map/ppermute | solution.py:48
  50.0 23.3 %collective-permute-start.26 = (bf16[256,512]{1,0:T(8,128)(2,1)S(1)}, bf16[256,512]{1,0:T(8,128)(2,1)S(1)}, u32[]{:S(2)}, u32[]{:S(2)}) collective-permute-start(bf16[256,512]{1,0:T(8,128)(2,1)S(1)} %collective-permute-done.23.refs_8_.refs_11_), channel_id=1, source_target_pairs={{0,3},{1,0},{2,1},{3,2},{4,7},{5,4},{6,5},{7,6},{8,11},{9,8},{10,9... | collective-permute-start | bytes 786440 | tf_op jit(solution)/shard_map/ppermute | solution.py:48
  50.0 26.7 %collective-permute-start.25 = (bf16[256,512]{1,0:T(8,128)(2,1)S(1)}, bf16[256,512]{1,0:T(8,128)(2,1)S(1)}, u32[]{:S(2)}, u32[]{:S(2)}) collective-permute-start(bf16[256,512]{1,0:T(8,128)(2,1)S(1)} %collective-permute-done.23.refs_8_.refs_11_), channel_id=1, source_target_pairs={{0,2},{1,3},{2,0},{3,1},{4,6},{5,7},{6,4},{7,5},{8,10},{9,11},{10,... | collective-permute-start | bytes 786440 | tf_op jit(solution)/shard_map/ppermute | solution.py:48
  50.4 26.3 %collective-permute-start.24 = (bf16[256,512]{1,0:T(8,128)(2,1)S(1)}, bf16[256,512]{1,0:T(8,128)(2,1)S(1)}, u32[]{:S(2)}, u32[]{:S(2)}) collective-permute-start(bf16[256,512]{1,0:T(8,128)(2,1)S(1)} %collective-permute-done.23.refs_8_.refs_11_), channel_id=1, source_target_pairs={{0,1},{1,2},{2,3},{3,0},{4,5},{5,6},{6,7},{7,4},{8,9},{9,10},{10,1... | collective-permute-start | bytes 786440 | tf_op jit(solution)/shard_map/ppermute | solution.py:48
  67.2 16.8 %copy-start.14 = (bf16[256,512]{1,0:T(8,128)(2,1)}, bf16[256,512]{1,0:T(8,128)(2,1)S(1)}, u32[]{:S(2)}) copy-start(bf16[256,512]{1,0:T(8,128)(2,1)S(1)} %collective-permute-done.21.refs_6_.refs_9_) | copy-start | bytes 786436
  67.2 13.8 %collective-permute-start.13 = (bf16[144,512]{1,0:T(8,128)(2,1)}, bf16[144,512]{1,0:T(8,128)(2,1)S(1)}, u32[]{:S(2)}, u32[]{:S(2)}) collective-permute-start(bf16[144,512]{1,0:T(8,128)(2,1)} %get-tuple-element.32), channel_id=1, source_target_pairs={{0,32},{1,33},{2,34},{3,35},{4,36},{5,37},{6,38},{7,39},{8,40},{9,... | collective-permute-start | bytes 442376 | tf_op jit(solution)/shard_map/ppermute | solution.py:48
  69.1 15.0 %copy-start.15 = (bf16[256,512]{1,0:T(8,128)(2,1)}, bf16[256,512]{1,0:T(8,128)(2,1)S(1)}, u32[]{:S(2)}) copy-start(bf16[256,512]{1,0:T(8,128)(2,1)S(1)} %collective-permute-done.20.refs_5_.refs_8_) | copy-start | bytes 786436
  69.1 15.0 %collective-permute-start.14 = (bf16[144,512]{1,0:T(8,128)(2,1)}, bf16[144,512]{1,0:T(8,128)(2,1)S(1)}, u32[]{:S(2)}, u32[]{:S(2)}) collective-permute-start(bf16[144,512]{1,0:T(8,128)(2,1)} %get-tuple-element.33), channel_id=1, source_target_pairs={{0,64},{1,65},{2,66},{3,67},{4,68},{5,69},{6,70},{7,71},{8,72},{9,... | collective-permute-start | bytes 442376 | tf_op jit(solution)/shard_map/ppermute | solution.py:48
  73.3 10.8 %copy-start.16 = (bf16[256,512]{1,0:T(8,128)(2,1)}, bf16[256,512]{1,0:T(8,128)(2,1)S(1)}, u32[]{:S(2)}) copy-start(bf16[256,512]{1,0:T(8,128)(2,1)S(1)} %collective-permute-done.26.refs_11_.refs_14_) | copy-start | bytes 786436
  73.3 26.3 %collective-permute-start.15 = (bf16[144,512]{1,0:T(8,128)(2,1)}, bf16[144,512]{1,0:T(8,128)(2,1)S(1)}, u32[]{:S(2)}, u32[]{:S(2)}) collective-permute-start(bf16[144,512]{1,0:T(8,128)(2,1)} %get-tuple-element.34), channel_id=1, source_target_pairs={{0,96},{1,97},{2,98},{3,99},{4,100},{5,101},{6,102},{7,103},{8,104... | collective-permute-start | bytes 442376 | tf_op jit(solution)/shard_map/ppermute | solution.py:48
  76.7 22.9 %collective-permute-start.16 = (bf16[144,512]{1,0:T(8,128)(2,1)}, bf16[144,512]{1,0:T(8,128)(2,1)S(1)}, u32[]{:S(2)}, u32[]{:S(2)}) collective-permute-start(bf16[144,512]{1,0:T(8,128)(2,1)} %get-tuple-element.35), channel_id=1, source_target_pairs={{0,128},{1,129},{2,130},{3,131},{4,132},{5,133},{6,134},{7,135},{8... | collective-permute-start | bytes 442376 | tf_op jit(solution)/shard_map/ppermute | solution.py:48
  76.7 22.9 %collective-permute-start.17 = (bf16[144,512]{1,0:T(8,128)(2,1)}, bf16[144,512]{1,0:T(8,128)(2,1)S(1)}, u32[]{:S(2)}, u32[]{:S(2)}) collective-permute-start(bf16[144,512]{1,0:T(8,128)(2,1)} %get-tuple-element.36), channel_id=1, source_target_pairs={{0,160},{1,161},{2,162},{3,163},{4,164},{5,165},{6,166},{7,167},{8... | collective-permute-start | bytes 442376 | tf_op jit(solution)/shard_map/ppermute | solution.py:48
  81.0 18.6 %copy-start.19 = (bf16[144,512]{1,0:T(8,128)(2,1)}, bf16[144,512]{1,0:T(8,128)(2,1)S(1)}, u32[]{:S(2)}) copy-start(bf16[144,512]{1,0:T(8,128)(2,1)S(1)} %collective-permute-done.13.refs_0_) | copy-start | bytes 442372
  81.0 19.0 %collective-permute-start.18 = (bf16[144,512]{1,0:T(8,128)(2,1)}, bf16[144,512]{1,0:T(8,128)(2,1)S(1)}, u32[]{:S(2)}, u32[]{:S(2)}) collective-permute-start(bf16[144,512]{1,0:T(8,128)(2,1)} %get-tuple-element.37), channel_id=1, source_target_pairs={{0,192},{1,193},{2,194},{3,195},{4,196},{5,197},{6,198},{7,199},{8... | collective-permute-start | bytes 442376 | tf_op jit(solution)/shard_map/ppermute | solution.py:48
  84.0 15.5 %copy-start.20 = (bf16[144,512]{1,0:T(8,128)(2,1)}, bf16[144,512]{1,0:T(8,128)(2,1)S(1)}, u32[]{:S(2)}) copy-start(bf16[144,512]{1,0:T(8,128)(2,1)S(1)} %collective-permute-done.14.refs_1_) | copy-start | bytes 442372
  84.0 19.9 %collective-permute-start.19 = (bf16[144,512]{1,0:T(8,128)(2,1)}, bf16[144,512]{1,0:T(8,128)(2,1)S(1)}, u32[]{:S(2)}, u32[]{:S(2)}) collective-permute-start(bf16[144,512]{1,0:T(8,128)(2,1)} %get-tuple-element.38), channel_id=1, source_target_pairs={{0,224},{1,225},{2,226},{3,227},{4,228},{5,229},{6,230},{7,231},{8... | collective-permute-start | bytes 442376 | tf_op jit(solution)/shard_map/ppermute | solution.py:48
  117.2 9.3 %collective-permute-start.27 = (bf16[2,272,1024]{2,1,0:T(8,128)(2,1)}, bf16[2,272,1024]{2,1,0:T(8,128)(2,1)S(1)}, u32[]{:S(2)}, u32[]{:S(2)}) collective-permute-start(bf16[2,272,1024]{2,1,0:T(8,128)(2,1)} %get-tuple-element.48), channel_id=1, source_target_pairs={{0,8},{1,9},{2,10},{3,11},{4,12},{5,13},{6,14},{7,15},{8,0},{9,1},... | collective-permute-start | bytes 3342344 | tf_op jit(solution)/shard_map/ppermute | solution.py:48
  127.9 14.3 %collective-permute-start.28 = (bf16[272,1024]{1,0:T(8,128)(2,1)S(1)}, bf16[272,1024]{1,0:T(8,128)(2,1)S(1)}, u32[]{:S(2)}, u32[]{:S(2)}) collective-permute-start(bf16[272,1024]{1,0:T(8,128)(2,1)S(1)} %pair_sum.1), channel_id=1, source_target_pairs={{0,16},{1,17},{2,18},{3,19},{4,20},{5,21},{6,22},{7,23},{8,24},{9,... | collective-permute-start | bytes 1671176 | tf_op jit(solution)/shard_map/ppermute | solution.py:48
  (20 other events, 58.4 us)

commit v2 on v1

v2 whole, which is shorter than its diff:
```python
import jax
import jax.numpy as jnp
from jax import lax
from jax.experimental import pallas as pl
from jax.experimental.pallas import tpu as pltpu
from jax.sharding import PartitionSpec as P

D = 1024
HEADS = 32
HEADDIM = 64
STATE = 128
CONV = 4
GROUP = 128
E = 2048
WIDE = 4384
ROWS = 128
SPAN = 512
GROUPS = SPAN // GROUP
OWN = 512
MINE = 8
HALO = 16
PAD = HALO + SPAN
CONVED = OWN + 2 * STATE
WA = CONVED + 128
UNIT = 176
Z = 8
PAYLOAD = 4 * ROWS + HALO + 4 * 48

F32 = jnp.float32
BF16 = jnp.bfloat16
EXACT = lax.Precision.HIGHEST
ANY = pl.BlockSpec(memory_space=pl.ANY)
VMEM = pl.BlockSpec(memory_space=pltpu.VMEM)


def place():
    s, f = lax.axis_index("seq"), lax.axis_index("fsdp")
    t = lax.rem(s, 4)
    return s // 4, t // 2, lax.rem(t, 2), f // 4, lax.rem(f, 4), t


def move(value, to):
    pairs = []
    for s in range(32):
        for f in range(8):
            here = dict(z=s // 4, yl=(s // 2) % 2, c=s % 2, yh=f // 4, x=f % 4)
            change = to(**here)
            if change is None:
                continue
            there = {**here, **change}
            target = (there["z"] * 4 + there["yl"] * 2 + there["c"]) * 8 + there["yh"] * 4 + there["x"]
            pairs.append((s * 8 + f, target))
    return lax.ppermute(value, ("seq", "fsdp"), pairs)


def shape(*dims, dtype=BF16):
    return jax.ShapeDtypeStruct(dims, dtype)


def call(kernel, name, outs, ins, operands, scratch=(), mb=48, flops=0, bytes_accessed=0, out_specs=None):
    return pl.pallas_call(
        kernel,
        out_shape=outs,
        in_specs=ins,
        out_specs=jax.tree.map(lambda _: VMEM, outs) if out_specs is None else out_specs,
        scratch_shapes=scratch,
        name=name,
        compiler_params=pltpu.CompilerParams(vmem_limit_bytes=mb << 20),
        cost_estimate=pl.CostEstimate(flops=flops, bytes_accessed=bytes_accessed, transcendentals=0),
    )(*operands)


def after(value, *others):
    def kernel(*refs):
        refs[-1][...] = refs[0][...]

    return call(
        kernel,
        "after",
        shape(*value.shape, dtype=value.dtype),
        [VMEM] * (1 + len(others)),
        (value, *others),
    )


def iota2(dims, dim):
    return lax.broadcasted_iota(jnp.int32, dims, dim)


def ones_at(where):
    return jnp.where(where, 1.0, 0.0)


def anti_identity():
    return ones_at(iota2((128, 128), 0) + iota2((128, 128), 1) == 127).astype(BF16)


def flipped(block):
    anti = anti_identity()
    rows = jnp.dot(anti, block, preferred_element_type=F32).astype(BF16)
    parts = [
        jnp.dot(rows[:, 128 * j : 128 * j + 128], anti, preferred_element_type=F32).astype(BF16)
        for j in range(D // 128)
    ]
    return jnp.concatenate(parts[::-1], axis=1)


def head_pick():
    _, yl, c, _, _, t = place()
    t_other = (1 - yl) * 2 + c
    row, col = iota2((512, 256), 0), iota2((512, 256), 1)
    inner = lax.rem(col, 128)
    head = jnp.where(col < 128, t, t_other)
    return ones_at(row == 256 * (inner // 64) + 64 * head + lax.rem(inner, 64))


def tiles():
    for lane in range(3):
        for group in range(4):
            n = lane * 4 + group
            yield lane, group, slice(ROWS + 16 * (n % 3), ROWS + 16 * (n % 3) + 16), slice(128 * (n // 3), 128 * (n // 3) + 128)


def pack_input_weight(iw, ua, ua_other, held, sem):
    _, yl, c, _, _, _ = place()
    copy = pltpu.make_async_copy(iw.at[:, E:], held, sem)
    copy.start()
    pick = head_pick().astype(BF16)
    lane, out = iota2((HEADS, 256), 0), iota2((HEADS, 256), 1)
    inner = lax.rem(out, 128)
    both_cores = 4 * lax.rem(inner, MINE) + 2 * jnp.where(out < 128, yl, 1 - yl) + inner // MINE
    step_pick = ones_at((lane == both_cores) & (inner < 2 * MINE)).astype(BF16)
    copy.wait()
    for j in range(4):
        got = jnp.dot(held[:, 512 * j : 512 * j + 512], pick, preferred_element_type=F32).astype(BF16)
        ua[:ROWS, 128 * j : 128 * j + 128] = got[:, :128]
        ua_other[:ROWS, 128 * j : 128 * j + 128] = got[:, 128:]
    rows = pl.ds(pl.multiple_of(64 * c, 64), 64)
    steps = jnp.dot(held[rows, E + 2 * STATE :], step_pick, preferred_element_type=F32).astype(BF16)
    for lane, group, line, cols in tiles():
        part = slice(16 * group, 16 * group + 16)
        if lane < 2:
            block = held[rows, E + 128 * lane : E + 128 * lane + 128][part]
            ua[line, cols] = block
            ua_other[line, cols] = block
        else:
            ua[line, cols] = steps[part, :128]
            ua_other[line, cols] = steps[part, 128:]


def pack_late_weights(iw, ow, cw, cb, dtb, rate, gain, ub, ub_other, prm, heads, stack):
    _, yl, c, _, _, t = place()
    t_other = (1 - yl) * 2 + c
    pick = head_pick()
    pick_bf = pick.astype(BF16)
    for j in range(4):
        got = jnp.dot(iw[:, 512 * j : 512 * j + 512], pick_bf, preferred_element_type=F32).astype(BF16)
        ub[:ROWS, 128 * j : 128 * j + 128] = got[:, :128]
        ub_other[:ROWS, 128 * j : 128 * j + 128] = got[:, 128:]
    for ref, which in ((ub, t), (ub_other, t_other)):
        rows = ow[pl.ds(pl.multiple_of(64 * which, 64), 64), :]
        ref[128:192, :] = rows[:, :512]
        ref[192:256, :] = rows[:, 512:]
    stack[...] = jnp.zeros_like(stack)
    stack[0:4, :] = cw[:, :E]
    stack[4:5, :] = cb[:, :E]
    stack[5:6, :] = gain[...]
    prm[...] = jnp.zeros_like(prm)
    for j in range(4):
        prm[:, 128 * j : 128 * j + 128] = jnp.dot(
            stack[:, 512 * j : 512 * j + 512], pick[:, :128], precision=EXACT, preferred_element_type=F32
        )
    prm[0:4, OWN:] = cw[:, E:]
    prm[4:5, OWN:] = cb[:, E:]
    chosen = iota2((MINE, HEADS), 1) == 4 * iota2((MINE, HEADS), 0) + t
    for n, ref in enumerate((dtb, rate)):
        column = jnp.sum(jnp.where(chosen, ref[...], 0.0), axis=1, keepdims=True)
        heads[n] = jnp.broadcast_to(column, (MINE, 128))


def prepare_inputs(hidden, tokens, base_bias, act, halo):
    _, _, c, _, _, _ = place()
    ids = tokens[...]
    letter = iota2((5, ROWS), 0)
    paired = jnp.where(ids == 4, 4, 3 - ids)
    for strand, chosen in ((0, ids), (1, paired)):
        onehot = ones_at(letter == chosen).astype(BF16)
        bias = lax.dot_general(
            onehot, base_bias[:, D * strand : D * strand + D], (((0,), (0,)), ((), ())), preferred_element_type=F32
        )
        block = (hidden[:, D * strand : D * strand + D].astype(F32) + bias).astype(BF16)
        if strand:
            block = flipped(block)
        act[ROWS * strand : ROWS * strand + ROWS, :] = block
    halo[...] = jnp.where(c == 1, act[ROWS - HALO : ROWS, :], act[2 * ROWS - HALO :, :])


def pack_core(*refs):
    act, act_y, halo_a, halo_b = refs[:4]
    units, out = refs[4:12], refs[12]
    out[: 2 * ROWS, :] = act[...]
    out[2 * ROWS : 4 * ROWS, :] = act_y[...]
    out[4 * ROWS : 4 * ROWS + HALO, :] = halo_a[...] + halo_b[...]
    for n, unit in enumerate(units):
        line = 4 * ROWS + HALO + 48 * (n % 4)
        out[line : line + 48, 512 * (n // 4) : 512 * (n // 4) + 512] = unit[ROWS:, :]


def weight_rows():
    _, _, _, yh, x, _ = place()
    return [which * 4 + lax.rem(x - k + 4, 4) for which in (yh, 1 - yh) for k in range(4)]


def place_act(act, blocks):
    _, _, _, _, _, t = place()
    for (ref, first), other in zip(blocks, (0, 2, 1, 3)):
        at = t ^ other
        for strand, row in ((0, at), (1, 3 - at)):
            act[strand, pl.ds(pl.multiple_of(HALO + ROWS * row, 16), ROWS), :] = ref[
                first + ROWS * strand : first + ROWS * strand + ROWS, :
            ]


def spread_heads(count):
    return ones_at(lax.rem(iota2((MINE * count, OWN), 0), MINE) == iota2((MINE * count, OWN), 1) // HEADDIM)


def hi_lo(v):
    hi = v.astype(BF16).astype(F32)
    return hi, v - hi


def spread_columns(rows):
    both = jnp.concatenate(hi_lo(rows), axis=0).astype(BF16)
    return lax.dot_general(
        both, spread_heads(2).astype(BF16), (((0,), (0,)), ((), ())), preferred_element_type=F32
    )


def spread_row(column):
    return jnp.sum(spread_heads(1) * column, axis=0, keepdims=True)


def running_sum(rows):
    count = rows.shape[0]
    hi, rest = hi_lo(rows)
    mid, low = hi_lo(rest)
    upper = ones_at(iota2((GROUP, GROUP), 0) <= iota2((GROUP, GROUP), 1)).astype(BF16)
    pieces = jnp.concatenate([hi, mid, low], axis=0).astype(BF16)
    sums = jnp.dot(pieces, upper, preferred_element_type=F32)
    return sums[:count] + sums[count : 2 * count] + sums[2 * count :]


def scan_kernel(*refs):
    act_own, act_y, halo_a, halo_b, swapped = refs[:5]
    units, refs = refs[5:13], refs[13:]
    prm, heads, refs = refs[0], refs[1], refs[2:]
    xs, maps, sizes, sums, starts, *sends = refs[:12]
    act, weight, proj, ends = refs[12:]
    z, _, c, _, _, _ = place()
    for n, (unit, f) in enumerate(zip(units, weight_rows())):
        weight[pl.ds(pl.multiple_of(ROWS * f, ROWS), ROWS), :OWN] = unit[:ROWS, :]
        for lane, group, line, cols in tiles():
            left = OWN + 128 * lane
            row = pl.multiple_of(ROWS * f + 64 * c + 16 * group, 16)
            weight[pl.ds(row, 16), left : left + 128] = unit[line, cols]
            row = pl.multiple_of(ROWS * f + 64 * (1 - c) + 16 * group, 16)
            first = 4 * ROWS + HALO + 48 * (n % 4) + line.start - ROWS
            side = 512 * (n // 4) + cols.start
            weight[pl.ds(row, 16), left : left + 128] = swapped[first : first + 16, side : side + 128]
    place_act(act, ((act_own, 0), (act_y, 0), (swapped, 0), (swapped, 2 * ROWS)))
    near = halo_a[...] + halo_b[...]
    far = swapped[4 * ROWS : 4 * ROWS + HALO, :]
    act[0, :HALO, :] = jnp.where(c == 1, near, far)
    act[1, :HALO, :] = jnp.where(c == 1, far, near)

    def one_strand(strand, _):
        proj[...] = jnp.dot(act[strand], weight[...], preferred_element_type=F32).astype(BF16).astype(F32)
        turned = []
        for g in range(GROUPS):
            steps = proj[HALO + GROUP * g : HALO + GROUP * g + GROUP, CONVED:].T
            turned.append(jnp.where(c == 0, steps[:MINE], steps[MINE : 2 * MINE]))
        raw = jnp.concatenate(turned, axis=0) + jnp.concatenate([heads[0]] * GROUPS, axis=0)
        size = jnp.maximum(raw, 0.0) + jnp.log1p(jnp.exp(-jnp.abs(raw)))
        decay = -size * jnp.concatenate([heads[1]] * GROUPS, axis=0)
        cumulated = running_sum(decay)
        sizes[strand] = size
        sums[strand] = cumulated
        state = jnp.zeros((STATE, OWN), F32)
        total = jnp.zeros((MINE, 1), F32)
        for g in range(GROUPS):
            rows = slice(GROUP * g, GROUP * g + GROUP)
            for j in range(6):
                cols = slice(128 * j, 128 * j + 128)
                first = HALO - 3 + GROUP * g
                acc = prm[4:5, cols] + prm[0:1, cols] * proj[first : first + GROUP, cols]
                for k in range(1, CONV):
                    acc = acc + prm[k : k + 1, cols] * proj[first + k : first + k + GROUP, cols]
                half = 0.5 * acc
                done = (half + half * jnp.tanh(half)).astype(BF16)
                if j < 4:
                    xs[strand, rows, cols] = done
                else:
                    maps[strand, rows, 128 * (j - 4) : 128 * (j - 4) + 128] = done
            part = slice(MINE * g, MINE * g + MINE)
            last = cumulated[part, GROUP - 1 :]
            total = total + last
            remaining = spread_columns(jnp.exp(last - cumulated[part]) * size[part])
            weighted = (xs[strand, rows, :].astype(F32) * remaining).astype(BF16)
            starts[strand, g] = state.astype(BF16)
            added = lax.dot_general(
                maps[strand, rows, :STATE], weighted, (((0,), (0,)), ((), ())), preferred_element_type=F32
            )
            state = state * spread_row(jnp.exp(last)) + added
        ends[strand, :STATE, :] = state.astype(BF16)
        hi, lo = hi_lo(spread_row(total))
        line = iota2((HALO, OWN), 0)
        ends[strand, STATE:, :] = jnp.where(line == 0, hi, jnp.where(line == 1, lo, 0.0)).astype(BF16)
        return 0

    lax.fori_loop(0, 2, one_strand, 0)
    for k in range(1, Z):
        strand = jnp.where(z + k < Z, 0, 1)
        sends[k - 1][...] = ends[strand]


def local_kernel(*refs):
    xs, maps, sizes, sums, starts, local, carry = refs
    causal = ones_at(iota2((GROUP, GROUP), 0) >= iota2((GROUP, GROUP), 1))
    left = iota2((GROUP, 128), 1) < HEADDIM

    def one_strand(strand, _):
        def one_group(g, before):
            rows = pl.ds(pl.multiple_of(GROUP * g, GROUP), GROUP)
            part = pl.ds(pl.multiple_of(MINE * g, MINE), MINE)
            size = sizes[strand, part, :]
            cumulated = sums[strand, part, :]
            columns = jnp.concatenate([cumulated, jnp.zeros((GROUP - MINE, GROUP), F32)], axis=0).T
            in_map = maps[strand, rows, :STATE]
            out_map = maps[strand, rows, STATE:]
            affinity = lax.dot_general(
                out_map, in_map, (((1,), (1,)), ((), ())), preferred_element_type=F32
            ) * causal
            parts = []
            for pair in range(4):
                mixes = []
                for h in (2 * pair, 2 * pair + 1):
                    gap = jnp.minimum(columns[:, h : h + 1] - cumulated[h : h + 1, :], 0.0)
                    mixes.append((affinity * jnp.exp(gap) * size[h : h + 1, :]).astype(BF16))
                x = xs[strand, rows, 128 * pair : 128 * pair + 128]
                zero = jnp.zeros_like(x)
                tall = jnp.concatenate([jnp.where(left, x, zero), jnp.where(left, zero, x)], axis=0)
                parts.append(jnp.dot(jnp.concatenate(mixes, axis=1), tall, preferred_element_type=F32))
            within = jnp.concatenate(parts, axis=1)
            grown = spread_columns(jnp.exp(cumulated))
            local[strand, rows, :] = within + jnp.dot(out_map, starts[strand, g], preferred_element_type=F32) * grown
            carry[strand, rows, :] = grown * spread_row(jnp.exp(before))
            return before + cumulated[:, GROUP - 1 :]

        lax.fori_loop(0, GROUPS, one_group, jnp.zeros((MINE, 1), F32))
        return 0

    lax.fori_loop(0, 2, one_strand, 0)


def gate_kernel(*refs):
    act_own, act_y, swapped = refs[:3]
    units, refs = refs[3:11], refs[11:]
    local, carry, gated, gated_carry, out_weight, act, weight = refs
    for unit, f in zip(units, weight_rows()):
        weight[pl.ds(pl.multiple_of(ROWS * f, ROWS), ROWS), :] = unit[:ROWS, :]
        for half in range(2):
            rows = unit[ROWS + 64 * half : ROWS + 64 * half + 64, :]
            out_weight[half, pl.ds(pl.multiple_of(64 * f, 64), 64), :] = rows
    place_act(act, ((act_own, 0), (act_y, 0), (swapped, 0), (swapped, 2 * ROWS)))

    def one_strand(strand, _):
        for g in range(2):
            rows = slice(256 * g, 256 * g + 256)
            gate = jnp.dot(
                act[strand, HALO + 256 * g : HALO + 256 * g + 256, :], weight[...], preferred_element_type=F32
            )
            half = 0.5 * gate.astype(BF16).astype(F32)
            gate = half + half * jnp.tanh(half)
            gated[strand, rows, :] = local[strand, rows, :] * gate
            gated_carry[strand, rows, :] = carry[strand, rows, :] * gate
        return 0

    lax.fori_loop(0, 2, one_strand, 0)


def half_rows(own):
    _, yl, _, _, _, _ = place()
    y = yl if own else 1 - yl
    return 256 * y, 256 * (1 - y)


def project_half(own, weight, entering, prm, maps, local, carry, keep, give, normed):
    _, _, c, _, _, _ = place()
    gain = prm[5:6, :OWN]
    tails = []
    for strand, first in enumerate(half_rows(own)):
        for b in range(2):
            rows = pl.ds(pl.multiple_of(first + ROWS * b, ROWS), ROWS)
            held = jnp.dot(maps[strand, rows, STATE:], entering[strand], preferred_element_type=F32)
            gated = local[strand, rows, :] + held * carry[strand, rows, :]
            squared = gated * gated
            folded = (squared[:, :128] + squared[:, 128:256]) + (squared[:, 256:384] + squared[:, 384:])
            tails.append(jnp.sum(folded.T, axis=0, keepdims=True))
            normed[2 * strand + b] = (gated * gain).astype(BF16)
    line = iota2((HALO, ROWS), 0)
    for ref, core in ((keep, c), (give, 1 - c)):
        for strand in range(2):
            b = core if strand == 0 else 1 - core
            for half in range(2):
                ref[ROWS * strand : ROWS * strand + ROWS, 512 * half : 512 * half + 512] = jnp.dot(
                    normed[2 * strand + b], weight[half], preferred_element_type=F32
                ).astype(BF16)
            hi, lo = hi_lo(jnp.where(b == 0, tails[2 * strand], tails[2 * strand + 1]))
            tail = jnp.where(line == 0, hi, jnp.where(line == 1, lo, 0.0))
            ref[2 * ROWS :, ROWS * strand : ROWS * strand + ROWS] = tail.astype(BF16)
        ref[2 * ROWS :, 2 * ROWS :] = jnp.zeros((HALO, D - 2 * ROWS), BF16)


def first_half(*refs):
    came, refs = refs[:7], refs[7:]
    weight, prm, maps, local, carry, entering, keep, give, normed, total = refs
    z, _, _, _, _, _ = place()
    total[...] = jnp.zeros_like(total)
    for strand in range(2):
        gone = jnp.zeros((1, OWN), F32)
        for k in range(Z - 1):
            ref = came[k] if strand == 0 else came[6 - k]
            here = k < z if strand == 0 else k < Z - 1 - z
            factor = jnp.exp(gone)

            @pl.when(here)
            def _(ref=ref, factor=factor):
                total[strand] += factor * ref[:STATE, :].astype(F32)

            tail = ref[STATE:, :].astype(F32)
            gone = gone + jnp.where(here, tail[0:1] + tail[1:2], 0.0)
        entering[strand] = total[strand].astype(BF16)
    project_half(False, weight, entering, prm, maps, local, carry, keep, give, normed)


def second_half(part, weight, entering, prm, maps, local, carry, keep, give, normed):
    project_half(True, weight, entering, prm, maps, local, carry, keep, give, normed)


def pair_sum(mine, came, out):
    main = mine[: 2 * ROWS, :].astype(F32) + came[: 2 * ROWS, :].astype(F32)
    out[: 2 * ROWS, :] = main.astype(BF16)
    tail = mine[2 * ROWS :, :].astype(F32) + came[2 * ROWS :, :].astype(F32)
    hi, lo = hi_lo(tail[0:1] + tail[1:2])
    line = iota2((HALO, D), 0)
    out[2 * ROWS :, :] = jnp.where(line == 0, hi, jnp.where(line == 1, lo, 0.0)).astype(BF16)


def last_kernel(mine, came, far, out):
    def tail(ref):
        rows = ref[2 * ROWS :, :].astype(F32)
        return rows[0:1] + rows[1:2]

    squares = tail(mine) + tail(came) + tail(far)
    diagonal = iota2((ROWS, ROWS), 0) == iota2((ROWS, ROWS), 1)
    for strand in range(2):
        rows = slice(ROWS * strand, ROWS * strand + ROWS)
        mean = jnp.sum(jnp.where(diagonal, squares[:, rows], 0.0), axis=1, keepdims=True) * (1.0 / E)
        main = mine[rows, :].astype(F32) + came[rows, :].astype(F32) + far[rows, :].astype(F32)
        block = (main * lax.rsqrt(mean + 1e-05)).astype(BF16)
        if strand:
            block = flipped(block)
        out[:, D * strand : D * strand + D] = block


def gathered(own, other):
    far = swap_diagonal(other)
    return [own] + [along_x(own, k) for k in (1, 2, 3)] + [far] + [along_x(far, k) for k in (1, 2, 3)]


def swap_core(value):
    return move(value, lambda z, yl, c, yh, x: dict(c=1 - c))


def swap_y(value):
    return move(value, lambda z, yl, c, yh, x: dict(yl=1 - yl))


def swap_diagonal(value, k=0):
    return move(value, lambda z, yl, c, yh, x: dict(yl=1 - yl, yh=1 - yh, x=(x + k) % 4))


def along_x(value, k):
    return move(value, lambda z, yl, c, yh, x: dict(x=(x + k) % 4))


def along_z(value, k):
    return move(value, lambda z, yl, c, yh, x: dict(z=(z + k) % Z))


def halo_step(same):
    def to(z, yl, c, yh, x):
        t = 2 * yl + c
        if t == 3 and z < Z - 1:
            return dict(z=z + 1, yl=1 if same else 0)
        if t == 0 and z > 0:
            return dict(z=z - 1, yl=0 if same else 1)
        return None

    return to


def body(hidden, tokens, base_bias, in_weight, conv_weight, conv_bias, dt_bias, decay_rate, norm_gain, out_weight):
    ua, ua_other = call(
        pack_input_weight,
        "pack_input_weight",
        [shape(UNIT, OWN)] * 2,
        [ANY],
        (in_weight,),
        scratch=[pltpu.VMEM((ROWS, WIDE - E), BF16), pltpu.SemaphoreType.DMA(())],
    )
    act, halo = call(
        prepare_inputs,
        "prepare_inputs",
        [shape(2 * ROWS, D), shape(HALO, D)],
        [VMEM] * 3,
        (hidden[0], tokens, base_bias),
    )
    act_y = swap_y(act)
    units = gathered(ua, ua_other)
    halo_a = move(halo, halo_step(True))
    halo_b = move(halo, halo_step(False))
    swapped = swap_core(
        call(
            pack_core, "pack_core", shape(PAYLOAD, D), [VMEM] * 12, (act, act_y, halo_a, halo_b, *units)
        )
    )
    ub, ub_other, prm, heads = call(
        pack_late_weights,
        "pack_late_weights",
        [shape(256, OWN), shape(256, OWN), shape(8, CONVED, dtype=F32), shape(2, MINE, 128, dtype=F32)],
        [VMEM] * 7,
        (in_weight, out_weight, conv_weight, conv_bias[None], dt_bias[None], decay_rate[None], norm_gain[None]),
        scratch=[pltpu.VMEM((8, E), F32)],
    )
    late = gathered(ub, ub_other)
    xs, maps, sizes, sums, starts, *sends = call(
        scan_kernel,
        "scan_kernel",
        [
            shape(2, SPAN, OWN),
            shape(2, SPAN, 2 * STATE),
            shape(2, MINE * GROUPS, GROUP, dtype=F32),
            shape(2, MINE * GROUPS, GROUP, dtype=F32),
            shape(2, GROUPS, STATE, OWN),
        ]
        + [shape(STATE + HALO, OWN)] * 7,
        [VMEM] * 15,
        (act, act_y, halo_a, halo_b, swapped, *units, prm, heads),
        scratch=[
            pltpu.VMEM((2, PAD, D), BF16),
            pltpu.VMEM((D, WA), BF16),
            pltpu.VMEM((PAD, WA), F32),
            pltpu.VMEM((2, STATE + HALO, OWN), BF16),
        ],
        flops=2 * 1056 * D * WA,
        bytes_accessed=8 << 20,
    )
    came = [along_z(sends[k - 1], k) for k in range(1, Z)]
    local, carry = call(
        local_kernel,
        "local_kernel",
        [shape(2, SPAN, OWN, dtype=F32)] * 2,
        [VMEM] * 5,
        (xs, maps, sizes, sums, starts),
        flops=4 * 1024 * D * OWN,
        bytes_accessed=16 << 20,
    )
    local, carry, weight = call(
        gate_kernel,
        "gate_kernel",
        [shape(2, SPAN, OWN, dtype=F32)] * 2 + [shape(2, OWN, 512)],
        [VMEM] * 13,
        (act, act_y, swapped, *late, local, carry),
        scratch=[pltpu.VMEM((2, PAD, D), BF16), pltpu.VMEM((D, OWN), BF16)],
        flops=2 * 1024 * D * OWN,
        bytes_accessed=8 << 20,
    )
    half_out = [shape(2 * ROWS + HALO, D)] * 2
    half_scratch = [pltpu.VMEM((4, ROWS, OWN), BF16)]
    entering, keep, give = call(
        first_half,
        "first_half",
        [shape(2, STATE, OWN)] + half_out,
        [VMEM] * 12,
        (*came, weight, prm, maps, local, carry),
        scratch=half_scratch + [pltpu.VMEM((2, STATE, OWN), F32)],
        flops=1024 * D * OWN,
        bytes_accessed=4 << 20,
    )
    part = call(pair_sum, "pair_sum", shape(2 * ROWS + HALO, D), [VMEM] * 2, (keep, swap_core(give)))
    far_part = swap_y(part)
    keep, give = call(
        second_half,
        "second_half",
        half_out,
        [VMEM] * 7,
        (part, weight, entering, prm, maps, local, carry),
        scratch=half_scratch,
        flops=32 * 1024 * D * OWN,
        bytes_accessed=4 << 20,
    )
    out = call(last_kernel, "last_kernel", shape(ROWS, 2 * D), [VMEM] * 3, (keep, swap_core(give), far_part))
    return out[None]


def solution(mesh):
    placed = (
        P("fsdp", "seq", None),
        P("fsdp", "seq"),
        P(),
        P("fsdp", None),
        P(),
        P(),
        P(),
        P(),
        P(),
        P("fsdp", None),
    )
    return jax.shard_map(
        body, mesh=mesh, in_specs=placed, out_specs=P("fsdp", "seq", None), check_vma=False
    )
```

time: 144 us -> 126 us (0.88); the launches traced: 143 us -> 124 us
  Pallas kernels: 46.6 us -> 31.4 us
  starting transfers between devices: 55.8 us -> 53 us
  waiting for transfers between devices: 33 us -> 30.4 us
    pallas_call x7 -> x11, Pallas kernels: 46.6 us -> 31.4 us  [call(): pl.pallas_call(kernel, out_shape=outs, in_specs=ins, out_specs=jax.tree.m...]
    ppermute x29 -> x28, starting transfers between devices: 55.8 us -> 53 us  [move(): return lax.ppermute(value, ('seq', 'fsdp'), pairs)]
    unnamed x79 -> x31, local copies, waits for them, and re-layouts: 6.1 us -> 8.82 us
    ppermute x29 -> x28, waiting for transfers between devices: 33 us -> 30.4 us  [move(): return lax.ppermute(value, ('seq', 'fsdp'), pairs)]
  transfers between devices with their start and end apart: 29 -> 28, of which waited for: 10 -> 10; matrix products, arithmetic and copies ran while one was open for 2% -> 1% of each run, Pallas kernels for 22% -> 19%
where the time goes in v2:
time: 126 us; the launch traced here: 124 us
  starting transfers between devices  53 us (42%)
  Pallas kernels  31.4 us (25%)
  waiting for transfers between devices  30.4 us (24%)
  local copies, waits for them, and re-layouts  8.83 us (7%)
    ppermute x28, starting transfers between devices, move(): return lax.ppermute(value, ('seq', 'fsdp'), pairs)  53 us
    pallas_call x11, Pallas kernels, call(): pl.pallas_call(kernel, out_shape=outs, in_specs=ins, out_specs=jax.tree.m...  31.4 us
    ppermute x28, waiting for transfers between devices, move(): return lax.ppermute(value, ('seq', 'fsdp'), pairs)  30.4 us
    unnamed x31, local copies, waits for them, and re-layouts  8.82 us
  transfers between devices with their start and end apart: 28, of which 10 were waited for; matrix products, arithmetic and copies ran while one was open for 1% of the time, Pallas kernels for 19%

profile of v2, /device:TPU:1, one launch (start us, length us, event | category | flops | bytes accessed | tf_op | source)
XLA Modules:
  0.0 123.8 jit_solution(12667746276631357845)
XLA Ops:
  0.0 1.0 copy-done.5
  1.0 0.8 copy-done.8
  1.8 0.7 copy-done.10
  2.5 0.6 prepare_inputs.1
  3.1 2.2 %collective-permute-start = (bf16[256,1024]{1,0:T(8,128)(2,1)S(1)}, bf16[256,1024]{1,0:T(8,128)(2,1)S(1)}, u32[]{:S(2)}, u32[]{:S(2)}) collective-permute-start(bf16[256,1024]{1,0:T(8,128)(2,1)S(1)} %get-tuple-element.35.refs_0_), channel_id=1, source_target_pairs={{0,16},{1,17},{2,18},{3,19},{4,20},{5,21},{6,22},{7,23},{8,24},{9,... | collective-permute-start | bytes 1572872 | tf_op jit(solution)/shard_map/ppermute | solution.py:53
  5.3 1.7 %copy.11.iw = bf16[128,4384]{1,0:T(8,128)(2,1)S(1)} copy(bf16[128,4384]{0,1:T(8,128)(2,1)} %param.13) | data formatting | bytes 2244608 | tf_op args[3]
  7.6 2.0 %collective-permute-start.6 = (bf16[176,512]{1,0:T(8,128)(2,1)S(1)}, bf16[176,512]{1,0:T(8,128)(2,1)S(1)}, u32[]{:S(2)}, u32[]{:S(2)}) collective-permute-start(bf16[176,512]{1,0:T(8,128)(2,1)S(1)} %get-tuple-element.38), channel_id=1, source_target_pairs={{0,20},{1,21},{2,22},{3,23},{4,16},{5,17},{6,18},{7,19},{8,28},{9,... | collective-permute-start | bytes 540680 | tf_op jit(solution)/shard_map/ppermute | solution.py:53
  9.5 2.5 %collective-permute-start.5 = (bf16[176,512]{1,0:T(8,128)(2,1)S(1)}, bf16[176,512]{1,0:T(8,128)(2,1)S(1)}, u32[]{:S(2)}, u32[]{:S(2)}) collective-permute-start(bf16[176,512]{1,0:T(8,128)(2,1)S(1)} %get-tuple-element.37.refs_4_.refs_5_), channel_id=1, source_target_pairs={{0,3},{1,0},{2,1},{3,2},{4,7},{5,4},{6,5},{7,6},{8,11},{9,8},{10,9... | collective-permute-start | bytes 540680 | tf_op jit(solution)/shard_map/ppermute | solution.py:53
  12.0 0.5 collective-permute-start.4
  12.5 0.7 collective-permute-start.2
  13.2 0.7 collective-permute-start.1
  13.9 0.7 collective-permute-start.3
  14.6 2.1 %collective-permute-start.9 = (bf16[176,512]{1,0:T(8,128)(2,1)S(1)}, bf16[176,512]{1,0:T(8,128)(2,1)S(1)}, u32[]{:S(2)}, u32[]{:S(2)}) collective-permute-start(bf16[176,512]{1,0:T(8,128)(2,1)S(1)} %collective-permute-done.6.refs_8_.refs_9_), channel_id=1, source_target_pairs={{0,3},{1,0},{2,1},{3,2},{4,7},{5,4},{6,5},{7,6},{8,11},{9,8},{10,9... | collective-permute-start | bytes 540680 | tf_op jit(solution)/shard_map/ppermute | solution.py:53
  16.7 1.2 %collective-permute-start.8 = (bf16[176,512]{1,0:T(8,128)(2,1)S(1)}, bf16[176,512]{1,0:T(8,128)(2,1)S(1)}, u32[]{:S(2)}, u32[]{:S(2)}) collective-permute-start(bf16[176,512]{1,0:T(8,128)(2,1)S(1)} %collective-permute-done.6.refs_8_.refs_9_), channel_id=1, source_target_pairs={{0,2},{1,3},{2,0},{3,1},{4,6},{5,7},{6,4},{7,5},{8,10},{9,11},{10,... | collective-permute-start | bytes 540680 | tf_op jit(solution)/shard_map/ppermute | solution.py:53
  17.9 2.8 %collective-permute-start.7 = (bf16[176,512]{1,0:T(8,128)(2,1)S(1)}, bf16[176,512]{1,0:T(8,128)(2,1)S(1)}, u32[]{:S(2)}, u32[]{:S(2)}) collective-permute-start(bf16[176,512]{1,0:T(8,128)(2,1)S(1)} %collective-permute-done.6.refs_8_.refs_9_), channel_id=1, source_target_pairs={{0,1},{1,2},{2,3},{3,0},{4,5},{5,6},{6,7},{7,4},{8,9},{9,10},{10,1... | collective-permute-start | bytes 540680 | tf_op jit(solution)/shard_map/ppermute | solution.py:53
  20.7 1.2 collective-permute-done.3.refs_5_.refs_6_
  21.9 2.2 %collective-permute-done.9.refs_11_.refs_12_ = bf16[176,512]{1,0:T(8,128)(2,1)S(1)} collective-permute-done((bf16[176,512]{1,0:T(8,128)(2,1)S(1)}, bf16[176,512]{1,0:T(8,128)(2,1)S(1)}, u32[]{:S(2)}, u32[]{:S(2)}) %collective-permute-start.9) | collective-permute-done | bytes 180256 | tf_op jit(solution)/shard_map/ppermute | solution.py:53
  24.1 1.5 %collective-permute-done.7.refs_9_.refs_10_ = bf16[176,512]{1,0:T(8,128)(2,1)S(1)} collective-permute-done((bf16[176,512]{1,0:T(8,128)(2,1)S(1)}, bf16[176,512]{1,0:T(8,128)(2,1)S(1)}, u32[]{:S(2)}, u32[]{:S(2)}) %collective-permute-start.7) | collective-permute-done | bytes 180256 | tf_op jit(solution)/shard_map/ppermute | solution.py:53
  25.7 10.4 %collective-permute-start.10 = (bf16[720,1024]{1,0:T(8,128)(2,1)S(1)}, bf16[720,1024]{1,0:T(8,128)(2,1)S(1)}, u32[]{:S(2)}, u32[]{:S(2)}) collective-permute-start(bf16[720,1024]{1,0:T(8,128)(2,1)S(1)} %pack_core.1), channel_id=1, source_target_pairs={{0,8},{1,9},{2,10},{3,11},{4,12},{5,13},{6,14},{7,15},{8,0},{9,1},... | collective-permute-start | bytes 4423688 | tf_op jit(solution)/shard_map/ppermute | solution.py:53
  36.2 0.7 pack_late_weights.1
  36.9 2.5 %collective-permute-start.21 = (bf16[256,512]{1,0:T(8,128)(2,1)S(1)}, bf16[256,512]{1,0:T(8,128)(2,1)S(1)}, u32[]{:S(2)}, u32[]{:S(2)}) collective-permute-start(bf16[256,512]{1,0:T(8,128)(2,1)S(1)} %get-tuple-element.49), channel_id=1, source_target_pairs={{0,20},{1,21},{2,22},{3,23},{4,16},{5,17},{6,18},{7,19},{8,28},{9,... | collective-permute-start | bytes 786440 | tf_op jit(solution)/shard_map/ppermute | solution.py:53
  39.5 1.1 collective-permute-start.19
  40.6 0.9 collective-permute-start.18
  41.5 4.6 %collective-permute-done.21.refs_7_ = bf16[256,512]{1,0:T(8,128)(2,1)S(1)} collective-permute-done((bf16[256,512]{1,0:T(8,128)(2,1)S(1)}, bf16[256,512]{1,0:T(8,128)(2,1)S(1)}, u32[]{:S(2)}, u32[]{:S(2)}) %collective-permute-start.21) | collective-permute-done | bytes 262176 | tf_op jit(solution)/shard_map/ppermute | solution.py:53
  46.4 0.6 collective-permute-done.20.refs_6_
  47.0 1.2 collective-permute-start.23
  48.2 0.6 collective-permute-start.22
  49.4 9.7 %scan_kernel.1 = (bf16[2,512,512]{2,1,0:T(8,128)(2,1)S(1)}, bf16[2,512,256]{2,1,0:T(8,128)(2,1)S(1)}, f32[2,32,128]{2,1,0:T(8,128)S(1)}, f32[2,32,128]{2,1,0:T(8...) custom-call(bf16[256,1024]{1,0:T(8,128)(2,1)S(1)} %get-tuple-element, ...), custom_call_target="tpu_custom_call" | custom-call | flops 1937768448 | bytes 8388608 | tf_op jit(solution)/shard_map/scan_kernel/pallas_call | solution.py:61
  59.1 1.7 %collective-permute-start.11 = (bf16[144,512]{1,0:T(8,128)(2,1)S(1)}, bf16[144,512]{1,0:T(8,128)(2,1)S(1)}, u32[]{:S(2)}, u32[]{:S(2)}) collective-permute-start(bf16[144,512]{1,0:T(8,128)(2,1)S(1)} %get-tuple-element.41), channel_id=1, source_target_pairs={{0,32},{1,33},{2,34},{3,35},{4,36},{5,37},{6,38},{7,39},{8,40},{9,... | collective-permute-start | bytes 442376 | tf_op jit(solution)/shard_map/ppermute | solution.py:53
  60.8 4.2 %collective-permute-start.12 = (bf16[144,512]{1,0:T(8,128)(2,1)S(1)}, bf16[144,512]{1,0:T(8,128)(2,1)S(1)}, u32[]{:S(2)}, u32[]{:S(2)}) collective-permute-start(bf16[144,512]{1,0:T(8,128)(2,1)S(1)} %get-tuple-element.42), channel_id=1, source_target_pairs={{0,64},{1,65},{2,66},{3,67},{4,68},{5,69},{6,70},{7,71},{8,72},{9,... | collective-permute-start | bytes 442376 | tf_op jit(solution)/shard_map/ppermute | solution.py:53
  65.0 2.8 %collective-permute-start.13 = (bf16[144,512]{1,0:T(8,128)(2,1)S(1)}, bf16[144,512]{1,0:T(8,128)(2,1)S(1)}, u32[]{:S(2)}, u32[]{:S(2)}) collective-permute-start(bf16[144,512]{1,0:T(8,128)(2,1)S(1)} %get-tuple-element.43), channel_id=1, source_target_pairs={{0,96},{1,97},{2,98},{3,99},{4,100},{5,101},{6,102},{7,103},{8,104... | collective-permute-start | bytes 442376 | tf_op jit(solution)/shard_map/ppermute | solution.py:53
  68.1 4.0 %collective-permute-start.15 = (bf16[144,512]{1,0:T(8,128)(2,1)S(1)}, bf16[144,512]{1,0:T(8,128)(2,1)S(1)}, u32[]{:S(2)}, u32[]{:S(2)}) collective-permute-start(bf16[144,512]{1,0:T(8,128)(2,1)S(1)} %get-tuple-element.45), channel_id=1, source_target_pairs={{0,160},{1,161},{2,162},{3,163},{4,164},{5,165},{6,166},{7,167},{8... | collective-permute-start | bytes 442376 | tf_op jit(solution)/shard_map/ppermute | solution.py:53
  72.1 3.0 %collective-permute-start.16 = (bf16[144,512]{1,0:T(8,128)(2,1)S(1)}, bf16[144,512]{1,0:T(8,128)(2,1)S(1)}, u32[]{:S(2)}, u32[]{:S(2)}) collective-permute-start(bf16[144,512]{1,0:T(8,128)(2,1)S(1)} %get-tuple-element.46), channel_id=1, source_target_pairs={{0,192},{1,193},{2,194},{3,195},{4,196},{5,197},{6,198},{7,199},{8... | collective-permute-start | bytes 442376 | tf_op jit(solution)/shard_map/ppermute | solution.py:53
  75.2 0.9 collective-permute-start.17
  76.1 1.2 copy-done.13
  77.3 6.3 %local_kernel.1 = (f32[2,512,512]{2,1,0:T(8,128)S(1)}, f32[2,512,512]{2,1,0:T(8,128)}) custom-call(bf16[2,512,512]{2,1,0:T(8,128)(2,1)S(1)} %get-tuple-element.50.refs_0_, bf16[2,512,256]{2,1,0:T(8,128)(2,1)S(1)} %get-tuple-element.51.refs_1_.refs_9_.maps, f32[2,32,128]{2,1,0:T(8,128)S(1)} %get-tuple-element.52.refs_2_, ...), custom_call_target="tpu_custom_call" | custom-call | flops 2147483648 | bytes 16777216 | tf_op jit(solution)/shard_map/local_kernel/pallas_call | solution.py:61
  83.6 1.3 %copy-done.2 = f32[2,512,512]{2,1,0:T(8,128)} copy-done((f32[2,512,512]{2,1,0:T(8,128)}, f32[2,512,512]{2,1,0:T(8,128)S(1)}, u32[]{:S(2)}) %copy-start.2) | copy-done | bytes 2097176
  84.9 6.3 %gate_kernel.1 = (f32[2,512,512]{2,1,0:T(8,128)}, f32[2,512,512]{2,1,0:T(8,128)}, bf16[2,512,512]{2,1,0:T(8,128)(2,1)S(1)}) custom-call(bf16[256,1024]{1,0:T(8,128)(2,1)S(1)} %get-tuple-element.35.refs_0_, bf16[256,1024]{1,0:T(8,128)(2,1)S(1)} %collective-permute-done.refs_1_, bf16[720,1024]{1,0:T(8,128)(2,1)S(1)} %copy-done.4, ...), custom_call_target="tpu_custom_call" | custom-call | flops 1073741824 | bytes 8388608 | tf_op jit(solution)/shard_map/gate_kernel/pallas_call | solution.py:61
  91.2 3.0 %collective-permute-done.16.refs_5_ = bf16[144,512]{1,0:T(8,128)(2,1)S(1)} collective-permute-done((bf16[144,512]{1,0:T(8,128)(2,1)S(1)}, bf16[144,512]{1,0:T(8,128)(2,1)S(1)}, u32[]{:S(2)}, u32[]{:S(2)}) %collective-permute-start.16) | collective-permute-done | bytes 147488 | tf_op jit(solution)/shard_map/ppermute | solution.py:53
  94.2 1.5 %collective-permute-done.17.refs_6_ = bf16[144,512]{1,0:T(8,128)(2,1)S(1)} collective-permute-done((bf16[144,512]{1,0:T(8,128)(2,1)S(1)}, bf16[144,512]{1,0:T(8,128)(2,1)S(1)}, u32[]{:S(2)}, u32[]{:S(2)}) %collective-permute-start.17) | collective-permute-done | bytes 147488 | tf_op jit(solution)/shard_map/ppermute | solution.py:53
  95.8 1.6 %copy-done = f32[2,512,512]{2,1,0:T(8,128)S(1)} copy-done((f32[2,512,512]{2,1,0:T(8,128)S(1)}, f32[2,512,512]{2,1,0:T(8,128)}, u32[]{:S(2)}) %copy-start) | copy-done | bytes 2097176
  97.4 3.2 %first_half.1 = (bf16[2,128,512]{2,1,0:T(8,128)(2,1)S(1)}, bf16[272,1024]{1,0:T(8,128)(2,1)S(1)}, bf16[272,1024]{1,0:T(8,128)(2,1)S(1)}) custom-call(bf16[144,512]{1,0:T(8,128)(2,1)S(1)} %collective-permute-done.11.refs_0_, bf16[144,512]{1,0:T(8,128)(2,1)S(1)} %collective-permute-done.12.refs_1_, bf16[144,512]{1,0:T(8,128)(2,1)S(1)} %collective-permute-done.13.refs_2_, ...), custom_call_target="tpu_custom_call" | custom-call | flops 536870912 | bytes 4194304 | tf_op jit(solution)/shard_map/first_half/pallas_call | solution.py:61
  100.6 3.1 %collective-permute-start.25 = (bf16[272,1024]{1,0:T(8,128)(2,1)S(1)}, bf16[272,1024]{1,0:T(8,128)(2,1)S(1)}, u32[]{:S(2)}, u32[]{:S(2)}) collective-permute-start(bf16[272,1024]{1,0:T(8,128)(2,1)S(1)} %get-tuple-element.61), channel_id=1, source_target_pairs={{0,8},{1,9},{2,10},{3,11},{4,12},{5,13},{6,14},{7,15},{8,0},{9,1},... | collective-permute-start | bytes 1671176 | tf_op jit(solution)/shard_map/ppermute | solution.py:53
  103.7 1.6 %collective-permute-done.25.came = bf16[272,1024]{1,0:T(8,128)(2,1)S(1)} collective-permute-done((bf16[272,1024]{1,0:T(8,128)(2,1)S(1)}, bf16[272,1024]{1,0:T(8,128)(2,1)S(1)}, u32[]{:S(2)}, u32[]{:S(2)}) %collective-permute-start.25) | collective-permute-done | bytes 557088 | tf_op jit(solution)/shard_map/ppermute | solution.py:53
  105.4 2.6 %second_half.1 = (bf16[272,1024]{1,0:T(8,128)(2,1)S(1)}, bf16[272,1024]{1,0:T(8,128)(2,1)S(1)}) custom-call(bf16[272,1024]{1,0:T(8,128)(2,1)S(1)} %pair_sum.1.part, bf16[2,512,512]{2,1,0:T(8,128)(2,1)S(1)} %get-tuple-element.57.refs_7_.weight, bf16[2,128,512]{2,1,0:T(8,128)(2,1)S(1)} %get-tuple-element.62.entering, ...), custom_call_target="tpu_custom_call" | custom-call | flops 17179869184 | bytes 4194304 | tf_op jit(solution)/shard_map/second_half/pallas_call | solution.py:61
  108.4 1.6 %collective-permute-done.26.came = bf16[272,1024]{1,0:T(8,128)(2,1)S(1)} collective-permute-done((bf16[272,1024]{1,0:T(8,128)(2,1)S(1)}, bf16[272,1024]{1,0:T(8,128)(2,1)S(1)}, u32[]{:S(2)}, u32[]{:S(2)}) %collective-permute-start.26) | collective-permute-done | bytes 557088 | tf_op jit(solution)/shard_map/ppermute | solution.py:53
  110.0 12.5 %collective-permute-done.27.far = bf16[272,1024]{1,0:T(8,128)(2,1)S(1)} collective-permute-done((bf16[272,1024]{1,0:T(8,128)(2,1)S(1)}, bf16[272,1024]{1,0:T(8,128)(2,1)S(1)}, u32[]{:S(2)}, u32[]{:S(2)}) %collective-permute-start.27) | collective-permute-done | bytes 557088 | tf_op jit(solution)/shard_map/ppermute | solution.py:53
  122.5 1.3 %last_kernel.1 = bf16[128,2048]{1,0:T(8,128)(2,1)} custom-call(bf16[272,1024]{1,0:T(8,128)(2,1)S(1)} %get-tuple-element.63.mine, bf16[272,1024]{1,0:T(8,128)(2,1)S(1)} %collective-permute-done.26.came, bf16[272,1024]{1,0:T(8,128)(2,1)S(1)} %collective-permute-done.27.far), custom_call_target="tpu_custom_call" | custom-call | tf_op jit(solution)/shard_map/last_kernel/pallas_call | solution.py:61
  (51 shorter events, 2.4 us)
Async XLA Ops:
  0.0 1.0 copy-start.5
  1.0 0.8 copy-start.8
  1.8 0.7 copy-start.10
  3.1 22.5 %collective-permute-start = (bf16[256,1024]{1,0:T(8,128)(2,1)S(1)}, bf16[256,1024]{1,0:T(8,128)(2,1)S(1)}, u32[]{:S(2)}, u32[]{:S(2)}) collective-permute-start(bf16[256,1024]{1,0:T(8,128)(2,1)S(1)} %get-tuple-element.35.refs_0_), channel_id=1, source_target_pairs={{0,16},{1,17},{2,18},{3,19},{4,20},{5,21},{6,22},{7,23},{8,24},{9,... | collective-permute-start | bytes 1572872 | tf_op jit(solution)/shard_map/ppermute | solution.py:53
  7.5 28.6 %copy-start.14 = (f32[2304]{0:T(1024)S(1)}, f32[2304]{0:T(1024)}, u32[]{:S(2)}) copy-start(f32[2304]{0:T(1024)} %param.15) | copy-start | bytes 27652
  7.5 28.6 %copy-start.6 = (bf16[256,1024]{1,0:T(8,128)(2,1)S(1)}, bf16[256,1024]{1,0:T(8,128)(2,1)}, u32[]{:S(2)}) copy-start(bf16[256,1024]{1,0:T(8,128)(2,1)} %ow.1) | copy-start | bytes 1572868
  7.5 28.6 %copy-start.7 = (f32[4,2304]{1,0:T(4,128)S(1)}, f32[4,2304]{1,0:T(4,128)}, u32[]{:S(2)}) copy-start(f32[4,2304]{1,0:T(4,128)} %cw.1) | copy-start | bytes 110596
  7.5 28.6 %copy-start.9 = (f32[2048]{0:T(1024)S(1)}, f32[2048]{0:T(1024)}, u32[]{:S(2)}) copy-start(f32[2048]{0:T(1024)} %param.18) | copy-start | bytes 24580
  7.5 28.6 %copy-start.11 = (f32[32]{0:T(128)S(1)}, f32[32]{0:T(128)}, u32[]{:S(2)}) copy-start(f32[32]{0:T(128)} %param.16) | copy-start | bytes 388
  7.5 28.6 %copy-start.12 = (f32[32]{0:T(128)S(1)}, f32[32]{0:T(128)}, u32[]{:S(2)}) copy-start(f32[32]{0:T(128)} %param.17) | copy-start | bytes 388
  7.6 7.0 %collective-permute-start.6 = (bf16[176,512]{1,0:T(8,128)(2,1)S(1)}, bf16[176,512]{1,0:T(8,128)(2,1)S(1)}, u32[]{:S(2)}, u32[]{:S(2)}) collective-permute-start(bf16[176,512]{1,0:T(8,128)(2,1)S(1)} %get-tuple-element.38), channel_id=1, source_target_pairs={{0,20},{1,21},{2,22},{3,23},{4,16},{5,17},{6,18},{7,19},{8,28},{9,... | collective-permute-start | bytes 540680 | tf_op jit(solution)/shard_map/ppermute | solution.py:53
  9.5 7.1 %collective-permute-start.5 = (bf16[176,512]{1,0:T(8,128)(2,1)S(1)}, bf16[176,512]{1,0:T(8,128)(2,1)S(1)}, u32[]{:S(2)}, u32[]{:S(2)}) collective-permute-start(bf16[176,512]{1,0:T(8,128)(2,1)S(1)} %get-tuple-element.37.refs_4_.refs_5_), channel_id=1, source_target_pairs={{0,3},{1,0},{2,1},{3,2},{4,7},{5,4},{6,5},{7,6},{8,11},{9,8},{10,9... | collective-permute-start | bytes 540680 | tf_op jit(solution)/shard_map/ppermute | solution.py:53
  12.0 5.9 %collective-permute-start.4 = (bf16[176,512]{1,0:T(8,128)(2,1)S(1)}, bf16[176,512]{1,0:T(8,128)(2,1)S(1)}, u32[]{:S(2)}, u32[]{:S(2)}) collective-permute-start(bf16[176,512]{1,0:T(8,128)(2,1)S(1)} %get-tuple-element.37.refs_4_.refs_5_), channel_id=1, source_target_pairs={{0,2},{1,3},{2,0},{3,1},{4,6},{5,7},{6,4},{7,5},{8,10},{9,11},{10,... | collective-permute-start | bytes 540680 | tf_op jit(solution)/shard_map/ppermute | solution.py:53
  12.5 0.7 collective-permute-start.2
  13.2 0.7 collective-permute-start.1
  13.9 8.0 %collective-permute-start.3 = (bf16[176,512]{1,0:T(8,128)(2,1)S(1)}, bf16[176,512]{1,0:T(8,128)(2,1)S(1)}, u32[]{:S(2)}, u32[]{:S(2)}) collective-permute-start(bf16[176,512]{1,0:T(8,128)(2,1)S(1)} %get-tuple-element.37.refs_4_.refs_5_), channel_id=1, source_target_pairs={{0,1},{1,2},{2,3},{3,0},{4,5},{5,6},{6,7},{7,4},{8,9},{9,10},{10,1... | collective-permute-start | bytes 540680 | tf_op jit(solution)/shard_map/ppermute | solution.py:53
  14.6 9.5 %collective-permute-start.9 = (bf16[176,512]{1,0:T(8,128)(2,1)S(1)}, bf16[176,512]{1,0:T(8,128)(2,1)S(1)}, u32[]{:S(2)}, u32[]{:S(2)}) collective-permute-start(bf16[176,512]{1,0:T(8,128)(2,1)S(1)} %collective-permute-done.6.refs_8_.refs_9_), channel_id=1, source_target_pairs={{0,3},{1,0},{2,1},{3,2},{4,7},{5,4},{6,5},{7,6},{8,11},{9,8},{10,9... | collective-permute-start | bytes 540680 | tf_op jit(solution)/shard_map/ppermute | solution.py:53
  16.7 7.5 %collective-permute-start.8 = (bf16[176,512]{1,0:T(8,128)(2,1)S(1)}, bf16[176,512]{1,0:T(8,128)(2,1)S(1)}, u32[]{:S(2)}, u32[]{:S(2)}) collective-permute-start(bf16[176,512]{1,0:T(8,128)(2,1)S(1)} %collective-permute-done.6.refs_8_.refs_9_), channel_id=1, source_target_pairs={{0,2},{1,3},{2,0},{3,1},{4,6},{5,7},{6,4},{7,5},{8,10},{9,11},{10,... | collective-permute-start | bytes 540680 | tf_op jit(solution)/shard_map/ppermute | solution.py:53
  17.9 7.7 %collective-permute-start.7 = (bf16[176,512]{1,0:T(8,128)(2,1)S(1)}, bf16[176,512]{1,0:T(8,128)(2,1)S(1)}, u32[]{:S(2)}, u32[]{:S(2)}) collective-permute-start(bf16[176,512]{1,0:T(8,128)(2,1)S(1)} %collective-permute-done.6.refs_8_.refs_9_), channel_id=1, source_target_pairs={{0,1},{1,2},{2,3},{3,0},{4,5},{5,6},{6,7},{7,4},{8,9},{9,10},{10,1... | collective-permute-start | bytes 540680 | tf_op jit(solution)/shard_map/ppermute | solution.py:53
  25.7 22.5 %collective-permute-start.10 = (bf16[720,1024]{1,0:T(8,128)(2,1)S(1)}, bf16[720,1024]{1,0:T(8,128)(2,1)S(1)}, u32[]{:S(2)}, u32[]{:S(2)}) collective-permute-start(bf16[720,1024]{1,0:T(8,128)(2,1)S(1)} %pack_core.1), channel_id=1, source_target_pairs={{0,8},{1,9},{2,10},{3,11},{4,12},{5,13},{6,14},{7,15},{8,0},{9,1},... | collective-permute-start | bytes 4423688 | tf_op jit(solution)/shard_map/ppermute | solution.py:53
  36.9 9.2 %collective-permute-start.21 = (bf16[256,512]{1,0:T(8,128)(2,1)S(1)}, bf16[256,512]{1,0:T(8,128)(2,1)S(1)}, u32[]{:S(2)}, u32[]{:S(2)}) collective-permute-start(bf16[256,512]{1,0:T(8,128)(2,1)S(1)} %get-tuple-element.49), channel_id=1, source_target_pairs={{0,20},{1,21},{2,22},{3,23},{4,16},{5,17},{6,18},{7,19},{8,28},{9,... | collective-permute-start | bytes 786440 | tf_op jit(solution)/shard_map/ppermute | solution.py:53
  39.4 7.6 %collective-permute-start.20 = (bf16[256,512]{1,0:T(8,128)(2,1)S(1)}, bf16[256,512]{1,0:T(8,128)(2,1)S(1)}, u32[]{:S(2)}, u32[]{:S(2)}) collective-permute-start(bf16[256,512]{1,0:T(8,128)(2,1)S(1)} %get-tuple-element.48.refs_3_), channel_id=1, source_target_pairs={{0,3},{1,0},{2,1},{3,2},{4,7},{5,4},{6,5},{7,6},{8,11},{9,8},{10,9... | collective-permute-start | bytes 786440 | tf_op jit(solution)/shard_map/ppermute | solution.py:53
  39.5 19.6 %collective-permute-start.19 = (bf16[256,512]{1,0:T(8,128)(2,1)S(1)}, bf16[256,512]{1,0:T(8,128)(2,1)S(1)}, u32[]{:S(2)}, u32[]{:S(2)}) collective-permute-start(bf16[256,512]{1,0:T(8,128)(2,1)S(1)} %get-tuple-element.48.refs_3_), channel_id=1, source_target_pairs={{0,2},{1,3},{2,0},{3,1},{4,6},{5,7},{6,4},{7,5},{8,10},{9,11},{10,... | collective-permute-start | bytes 786440 | tf_op jit(solution)/shard_map/ppermute | solution.py:53
  40.6 20.2 %collective-permute-start.18 = (bf16[256,512]{1,0:T(8,128)(2,1)S(1)}, bf16[256,512]{1,0:T(8,128)(2,1)S(1)}, u32[]{:S(2)}, u32[]{:S(2)}) collective-permute-start(bf16[256,512]{1,0:T(8,128)(2,1)S(1)} %get-tuple-element.48.refs_3_), channel_id=1, source_target_pairs={{0,1},{1,2},{2,3},{3,0},{4,5},{5,6},{6,7},{7,4},{8,9},{9,10},{10,1... | collective-permute-start | bytes 786440 | tf_op jit(solution)/shard_map/ppermute | solution.py:53
  46.1 18.9 %collective-permute-start.24 = (bf16[256,512]{1,0:T(8,128)(2,1)S(1)}, bf16[256,512]{1,0:T(8,128)(2,1)S(1)}, u32[]{:S(2)}, u32[]{:S(2)}) collective-permute-start(bf16[256,512]{1,0:T(8,128)(2,1)S(1)} %collective-permute-done.21.refs_7_), channel_id=1, source_target_pairs={{0,3},{1,0},{2,1},{3,2},{4,7},{5,4},{6,5},{7,6},{8,11},{9,8},{10,9... | collective-permute-start | bytes 786440 | tf_op jit(solution)/shard_map/ppermute | solution.py:53
  47.0 20.8 %collective-permute-start.23 = (bf16[256,512]{1,0:T(8,128)(2,1)S(1)}, bf16[256,512]{1,0:T(8,128)(2,1)S(1)}, u32[]{:S(2)}, u32[]{:S(2)}) collective-permute-start(bf16[256,512]{1,0:T(8,128)(2,1)S(1)} %collective-permute-done.21.refs_7_), channel_id=1, source_target_pairs={{0,2},{1,3},{2,0},{3,1},{4,6},{5,7},{6,4},{7,5},{8,10},{9,11},{10,... | collective-permute-start | bytes 786440 | tf_op jit(solution)/shard_map/ppermute | solution.py:53
  48.2 1.1 copy-start.3
  48.2 19.9 %collective-permute-start.22 = (bf16[256,512]{1,0:T(8,128)(2,1)S(1)}, bf16[256,512]{1,0:T(8,128)(2,1)S(1)}, u32[]{:S(2)}, u32[]{:S(2)}) collective-permute-start(bf16[256,512]{1,0:T(8,128)(2,1)S(1)} %collective-permute-done.21.refs_7_), channel_id=1, source_target_pairs={{0,1},{1,2},{2,3},{3,0},{4,5},{5,6},{6,7},{7,4},{8,9},{9,10},{10,1... | collective-permute-start | bytes 786440 | tf_op jit(solution)/shard_map/ppermute | solution.py:53
  59.1 13.1 %collective-permute-start.11 = (bf16[144,512]{1,0:T(8,128)(2,1)S(1)}, bf16[144,512]{1,0:T(8,128)(2,1)S(1)}, u32[]{:S(2)}, u32[]{:S(2)}) collective-permute-start(bf16[144,512]{1,0:T(8,128)(2,1)S(1)} %get-tuple-element.41), channel_id=1, source_target_pairs={{0,32},{1,33},{2,34},{3,35},{4,36},{5,37},{6,38},{7,39},{8,40},{9,... | collective-permute-start | bytes 442376 | tf_op jit(solution)/shard_map/ppermute | solution.py:53
  60.8 14.4 %collective-permute-start.12 = (bf16[144,512]{1,0:T(8,128)(2,1)S(1)}, bf16[144,512]{1,0:T(8,128)(2,1)S(1)}, u32[]{:S(2)}, u32[]{:S(2)}) collective-permute-start(bf16[144,512]{1,0:T(8,128)(2,1)S(1)} %get-tuple-element.42), channel_id=1, source_target_pairs={{0,64},{1,65},{2,66},{3,67},{4,68},{5,69},{6,70},{7,71},{8,72},{9,... | collective-permute-start | bytes 442376 | tf_op jit(solution)/shard_map/ppermute | solution.py:53
  65.0 26.2 %collective-permute-start.13 = (bf16[144,512]{1,0:T(8,128)(2,1)S(1)}, bf16[144,512]{1,0:T(8,128)(2,1)S(1)}, u32[]{:S(2)}, u32[]{:S(2)}) collective-permute-start(bf16[144,512]{1,0:T(8,128)(2,1)S(1)} %get-tuple-element.43), channel_id=1, source_target_pairs={{0,96},{1,97},{2,98},{3,99},{4,100},{5,101},{6,102},{7,103},{8,104... | collective-permute-start | bytes 442376 | tf_op jit(solution)/shard_map/ppermute | solution.py:53
  67.9 23.3 %collective-permute-start.14 = (bf16[144,512]{1,0:T(8,128)(2,1)S(1)}, bf16[144,512]{1,0:T(8,128)(2,1)S(1)}, u32[]{:S(2)}, u32[]{:S(2)}) collective-permute-start(bf16[144,512]{1,0:T(8,128)(2,1)S(1)} %get-tuple-element.44), channel_id=1, source_target_pairs={{0,128},{1,129},{2,130},{3,131},{4,132},{5,133},{6,134},{7,135},{8... | collective-permute-start | bytes 442376 | tf_op jit(solution)/shard_map/ppermute | solution.py:53
  68.1 23.1 %collective-permute-start.15 = (bf16[144,512]{1,0:T(8,128)(2,1)S(1)}, bf16[144,512]{1,0:T(8,128)(2,1)S(1)}, u32[]{:S(2)}, u32[]{:S(2)}) collective-permute-start(bf16[144,512]{1,0:T(8,128)(2,1)S(1)} %get-tuple-element.45), channel_id=1, source_target_pairs={{0,160},{1,161},{2,162},{3,163},{4,164},{5,165},{6,166},{7,167},{8... | collective-permute-start | bytes 442376 | tf_op jit(solution)/shard_map/ppermute | solution.py:53
  72.1 22.1 %collective-permute-start.16 = (bf16[144,512]{1,0:T(8,128)(2,1)S(1)}, bf16[144,512]{1,0:T(8,128)(2,1)S(1)}, u32[]{:S(2)}, u32[]{:S(2)}) collective-permute-start(bf16[144,512]{1,0:T(8,128)(2,1)S(1)} %get-tuple-element.46), channel_id=1, source_target_pairs={{0,192},{1,193},{2,194},{3,195},{4,196},{5,197},{6,198},{7,199},{8... | collective-permute-start | bytes 442376 | tf_op jit(solution)/shard_map/ppermute | solution.py:53
  75.2 20.6 %collective-permute-start.17 = (bf16[144,512]{1,0:T(8,128)(2,1)S(1)}, bf16[144,512]{1,0:T(8,128)(2,1)S(1)}, u32[]{:S(2)}, u32[]{:S(2)}) collective-permute-start(bf16[144,512]{1,0:T(8,128)(2,1)S(1)} %get-tuple-element.47), channel_id=1, source_target_pairs={{0,224},{1,225},{2,226},{3,227},{4,228},{5,229},{6,230},{7,231},{8... | collective-permute-start | bytes 442376 | tf_op jit(solution)/shard_map/ppermute | solution.py:53
  76.1 1.2 copy-start.13
  77.3 7.6 %copy-start.4 = (bf16[720,1024]{1,0:T(8,128)(2,1)S(1)}, bf16[720,1024]{1,0:T(8,128)(2,1)}, u32[]{:S(2)}) copy-start(bf16[720,1024]{1,0:T(8,128)(2,1)} %copy-done.3) | copy-start | bytes 4423684
  83.6 1.3 %copy-start.2 = (f32[2,512,512]{2,1,0:T(8,128)}, f32[2,512,512]{2,1,0:T(8,128)S(1)}, u32[]{:S(2)}) copy-start(f32[2,512,512]{2,1,0:T(8,128)S(1)} %get-tuple-element.55.refs_11_) | copy-start | bytes 6291460
  95.8 1.6 %copy-start = (f32[2,512,512]{2,1,0:T(8,128)S(1)}, f32[2,512,512]{2,1,0:T(8,128)}, u32[]{:S(2)}) copy-start(f32[2,512,512]{2,1,0:T(8,128)} %get-tuple-element.58.refs_10_.local) | copy-start | bytes 6291460
  97.4 8.0 %copy-start.1 = (f32[2,512,512]{2,1,0:T(8,128)S(1)}, f32[2,512,512]{2,1,0:T(8,128)}, u32[]{:S(2)}) copy-start(f32[2,512,512]{2,1,0:T(8,128)} %get-tuple-element.58.refs_10_.local) | copy-start | bytes 6291460
  100.6 4.7 %collective-permute-start.25 = (bf16[272,1024]{1,0:T(8,128)(2,1)S(1)}, bf16[272,1024]{1,0:T(8,128)(2,1)S(1)}, u32[]{:S(2)}, u32[]{:S(2)}) collective-permute-start(bf16[272,1024]{1,0:T(8,128)(2,1)S(1)} %get-tuple-element.61), channel_id=1, source_target_pairs={{0,8},{1,9},{2,10},{3,11},{4,12},{5,13},{6,14},{7,15},{8,0},{9,1},... | collective-permute-start | bytes 1671176 | tf_op jit(solution)/shard_map/ppermute | solution.py:53
  108.0 2.0 %collective-permute-start.26 = (bf16[272,1024]{1,0:T(8,128)(2,1)S(1)}, bf16[272,1024]{1,0:T(8,128)(2,1)S(1)}, u32[]{:S(2)}, u32[]{:S(2)}) collective-permute-start(bf16[272,1024]{1,0:T(8,128)(2,1)S(1)} %get-tuple-element.64), channel_id=1, source_target_pairs={{0,8},{1,9},{2,10},{3,11},{4,12},{5,13},{6,14},{7,15},{8,0},{9,1},... | collective-permute-start | bytes 1671176 | tf_op jit(solution)/shard_map/ppermute | solution.py:53
  108.4 14.1 %collective-permute-start.27 = (bf16[272,1024]{1,0:T(8,128)(2,1)S(1)}, bf16[272,1024]{1,0:T(8,128)(2,1)S(1)}, u32[]{:S(2)}, u32[]{:S(2)}) collective-permute-start(bf16[272,1024]{1,0:T(8,128)(2,1)S(1)} %pair_sum.1.part), channel_id=1, source_target_pairs={{0,16},{1,17},{2,18},{3,19},{4,20},{5,21},{6,22},{7,23},{8,24},{9,... | collective-permute-start | bytes 1671176 | tf_op jit(solution)/shard_map/ppermute | solution.py:53

commit v3 on v2

v3 whole, which is shorter than its diff:
```python
import jax
import jax.numpy as jnp
from jax import lax
from jax.experimental import pallas as pl
from jax.experimental.pallas import tpu as pltpu
from jax.sharding import PartitionSpec as P

D = 1024
HEADS = 32
HEADDIM = 64
STATE = 128
CONV = 4
GROUP = 128
E = 2048
WIDE = 4384
ROWS = 128
SPAN = 512
GROUPS = SPAN // GROUP
OWN = 512
MINE = 8
HALO = 16
PAD = HALO + SPAN
CONVED = OWN + 2 * STATE
WA = CONVED + 128
UNIT = OWN + STATE + HEADS
LATE = 2 * HEADDIM
Z = 8
PAYLOAD = 4 * ROWS + HALO + STATE

F32 = jnp.float32
BF16 = jnp.bfloat16
EXACT = lax.Precision.HIGHEST
ANY = pl.BlockSpec(memory_space=pl.ANY)
VMEM = pl.BlockSpec(memory_space=pltpu.VMEM)


def place():
    s, f = lax.axis_index("seq"), lax.axis_index("fsdp")
    t = lax.rem(s, 4)
    return s // 4, t // 2, lax.rem(t, 2), f // 4, lax.rem(f, 4), t


def move(value, to):
    pairs = []
    for s in range(32):
        for f in range(8):
            here = dict(z=s // 4, yl=(s // 2) % 2, c=s % 2, yh=f // 4, x=f % 4)
            change = to(**here)
            if change is None:
                continue
            there = {**here, **change}
            target = (there["z"] * 4 + there["yl"] * 2 + there["c"]) * 8 + there["yh"] * 4 + there["x"]
            pairs.append((s * 8 + f, target))
    return lax.ppermute(value, ("seq", "fsdp"), pairs)


def shape(*dims, dtype=BF16):
    return jax.ShapeDtypeStruct(dims, dtype)


def call(kernel, name, outs, ins, operands, scratch=(), mb=48, flops=0, bytes_accessed=0, out_specs=None):
    return pl.pallas_call(
        kernel,
        out_shape=outs,
        in_specs=ins,
        out_specs=jax.tree.map(lambda _: VMEM, outs) if out_specs is None else out_specs,
        scratch_shapes=scratch,
        name=name,
        compiler_params=pltpu.CompilerParams(vmem_limit_bytes=mb << 20),
        cost_estimate=pl.CostEstimate(flops=flops, bytes_accessed=bytes_accessed, transcendentals=0),
    )(*operands)


def iota2(dims, dim):
    return lax.broadcasted_iota(jnp.int32, dims, dim)


def ones_at(where):
    return jnp.where(where, 1.0, 0.0)


def anti_identity():
    return ones_at(iota2((128, 128), 0) + iota2((128, 128), 1) == 127).astype(BF16)


def flipped(block):
    anti = anti_identity()
    rows = jnp.dot(anti, block, preferred_element_type=F32).astype(BF16)
    parts = [
        jnp.dot(rows[:, 128 * j : 128 * j + 128], anti, preferred_element_type=F32).astype(BF16)
        for j in range(D // 128)
    ]
    return jnp.concatenate(parts[::-1], axis=1)


def head_pick():
    _, _, _, _, _, t = place()
    row, col = iota2((512, 128), 0), iota2((512, 128), 1)
    return ones_at(row == 256 * (col // 64) + 64 * t + lax.rem(col, 64))


def start_kernel(hidden, tokens, base_bias, iw, ow, act, halo, ua, ua_other, ub, ub_other, rows_in, ids_in, bias_in, iw_in, ow_in, sem):
    _, yl, c, _, _, t = place()
    copies = [
        pltpu.make_async_copy(tokens, ids_in, sem.at[0]),
        pltpu.make_async_copy(base_bias, bias_in, sem.at[1]),
        pltpu.make_async_copy(hidden, rows_in, sem.at[2]),
        pltpu.make_async_copy(iw.at[pl.ds(E, WIDE - E)], iw_in.at[pl.ds(E, WIDE - E)], sem.at[3]),
        pltpu.make_async_copy(iw.at[pl.ds(0, E)], iw_in.at[pl.ds(0, E)], sem.at[4]),
        pltpu.make_async_copy(ow, ow_in, sem.at[5]),
    ]
    for copy in copies:
        copy.start()
    for copy in copies[:3]:
        copy.wait()
    ids = ids_in[...]
    letter = iota2((5, ROWS), 0)
    paired = jnp.where(ids == 4, 4, 3 - ids)
    for strand, chosen in ((0, ids), (1, paired)):
        onehot = ones_at(letter == chosen).astype(BF16)
        bias = lax.dot_general(
            onehot, bias_in[:, D * strand : D * strand + D], (((0,), (0,)), ((), ())), preferred_element_type=F32
        )
        block = (rows_in[:, D * strand : D * strand + D].astype(F32) + bias).astype(BF16)
        if strand:
            block = flipped(block)
        act[ROWS * strand : ROWS * strand + ROWS, :] = block
    halo[...] = jnp.where(c == 1, act[ROWS - HALO : ROWS, :], act[2 * ROWS - HALO :, :])
    for copy in copies[3:]:
        copy.wait()
    for early, late, which in ((ua, ub, t), (ua_other, ub_other, (1 - yl) * 2 + c)):
        for j in range(MINE):
            row = pl.multiple_of(256 * j + 64 * which, 64)
            early[64 * j : 64 * j + 64, :] = iw_in[pl.ds(E + row, 64), :]
            late[:HEADDIM, 128 * j : 128 * j + 128] = iw_in[pl.ds(row, 64), :]
        early[OWN : OWN + STATE, :] = iw_in[pl.ds(pl.multiple_of(2 * E + STATE * c, STATE), STATE), :]
        early[OWN + STATE :, :] = iw_in[2 * E + 2 * STATE :, :]
        late[HEADDIM:, :] = ow_in[pl.ds(pl.multiple_of(64 * which, 64), 64), :]


def hold(*refs):
    count = (len(refs) - 1) // 2
    for n in range(count):
        refs[count + 1 + n][...] = refs[n][...]


def pack_params(cw, cb, dtb, rate, gain, prm, heads, stack):
    _, _, _, _, _, t = place()
    pick = head_pick()
    stack[...] = jnp.zeros_like(stack)
    stack[0:4, :] = cw[:, :E]
    stack[4:5, :] = cb[:, :E]
    stack[5:6, :] = gain[...]
    prm[...] = jnp.zeros_like(prm)
    for j in range(4):
        prm[:, 128 * j : 128 * j + 128] = jnp.dot(
            stack[:, 512 * j : 512 * j + 512], pick, precision=EXACT, preferred_element_type=F32
        )
    prm[0:4, OWN:] = cw[:, E:]
    prm[4:5, OWN:] = cb[:, E:]
    chosen = iota2((MINE, HEADS), 1) == 4 * iota2((MINE, HEADS), 0) + t
    for n, ref in enumerate((dtb, rate)):
        column = jnp.sum(jnp.where(chosen, ref[...], 0.0), axis=1, keepdims=True)
        heads[n] = jnp.broadcast_to(column, (MINE, 128))


def pack_core(*refs):
    act, act_y, halo_a, halo_b, ub, ub_far = refs[:6]
    units, out, out_b = refs[6:14], refs[14], refs[15]
    out_b[:LATE, :] = ub[...]
    out_b[LATE:, :] = ub_far[...]
    out[: 2 * ROWS, :] = act[...]
    out[2 * ROWS : 4 * ROWS, :] = act_y[...]
    out[4 * ROWS : 4 * ROWS + HALO, :] = halo_a[...] + halo_b[...]
    for n, unit in enumerate(units):
        out[4 * ROWS + HALO :, 128 * n : 128 * n + 128] = unit[OWN : OWN + STATE, :]


def weight_rows():
    _, _, _, yh, x, _ = place()
    return [which * 4 + lax.rem(x - k + 4, 4) for which in (yh, 1 - yh) for k in range(4)]


def place_act(act, blocks):
    _, _, _, _, _, t = place()
    for (ref, first), other in zip(blocks, (0, 2, 1, 3)):
        at = t ^ other
        for strand, row in ((0, at), (1, 3 - at)):
            act[strand, pl.ds(pl.multiple_of(HALO + ROWS * row, 16), ROWS), :] = ref[
                first + ROWS * strand : first + ROWS * strand + ROWS, :
            ]


def spread_heads(count):
    return ones_at(lax.rem(iota2((MINE * count, OWN), 0), MINE) == iota2((MINE * count, OWN), 1) // HEADDIM)


def hi_lo(v):
    hi = v.astype(BF16).astype(F32)
    return hi, v - hi


def spread_columns(rows):
    both = jnp.concatenate(hi_lo(rows), axis=0).astype(BF16)
    return lax.dot_general(
        both, spread_heads(2).astype(BF16), (((0,), (0,)), ((), ())), preferred_element_type=F32
    )


def spread_row(column):
    return jnp.sum(spread_heads(1) * column, axis=0, keepdims=True)


def running_sum(rows):
    count = rows.shape[0]
    hi, rest = hi_lo(rows)
    mid, low = hi_lo(rest)
    upper = ones_at(iota2((GROUP, GROUP), 0) <= iota2((GROUP, GROUP), 1)).astype(BF16)
    pieces = jnp.concatenate([hi, mid, low], axis=0).astype(BF16)
    sums = jnp.dot(pieces, upper, preferred_element_type=F32)
    return sums[:count] + sums[count : 2 * count] + sums[2 * count :]


def times_turned(a, b):
    return lax.dot_general(a, b, (((1,), (1,)), ((), ())), preferred_element_type=F32)


def scan_kernel(*refs):
    act_own, act_y, halo_a, halo_b, swapped = refs[:5]
    units, refs = refs[5:13], refs[13:]
    prm, heads, refs = refs[0], refs[1], refs[2:]
    xs, maps, sizes, sums, starts, act, kept, given = refs[:8]
    weight, proj, ends = refs[8:]
    z, _, c, _, _, t = place()
    weight[CONVED + HEADS :, :] = jnp.zeros((WA - CONVED - HEADS, D), BF16)
    for n, (unit, f) in enumerate(zip(units, weight_rows())):
        lanes = pl.ds(pl.multiple_of(128 * f, 128), 128)
        weight[:OWN, lanes] = unit[:OWN, :]
        weight[pl.ds(pl.multiple_of(OWN + STATE * c, STATE), STATE), lanes] = unit[OWN : OWN + STATE, :]
        weight[pl.ds(pl.multiple_of(OWN + STATE * (1 - c), STATE), STATE), lanes] = swapped[
            4 * ROWS + HALO :, 128 * n : 128 * n + 128
        ]
        weight[CONVED : CONVED + HEADS, lanes] = unit[OWN + STATE :, :]
    place_act(act, ((act_own, 0), (act_y, 0), (swapped, 0), (swapped, 2 * ROWS)))
    near = halo_a[...] + halo_b[...]
    far = swapped[4 * ROWS : 4 * ROWS + HALO, :]
    act[0, :HALO, :] = jnp.where(c == 1, near, far)
    act[1, :HALO, :] = jnp.where(c == 1, far, near)

    choose = ones_at(iota2((MINE, HEADS), 1) == 4 * iota2((MINE, HEADS), 0) + t).astype(BF16)

    def one_strand(strand, _):
        proj[...] = times_turned(act[strand], weight[...]).astype(BF16).astype(F32)
        turned = []
        for g in range(GROUPS):
            steps = proj[HALO + GROUP * g : HALO + GROUP * g + GROUP, CONVED:].T[:HEADS].astype(BF16)
            turned.append(jnp.dot(choose, steps, preferred_element_type=F32))
        raw = jnp.concatenate(turned, axis=0) + jnp.concatenate([heads[0]] * GROUPS, axis=0)
        size = jnp.maximum(raw, 0.0) + jnp.log1p(jnp.exp(-jnp.abs(raw)))
        decay = -size * jnp.concatenate([heads[1]] * GROUPS, axis=0)
        cumulated = running_sum(decay)
        sizes[strand] = size
        sums[strand] = cumulated
        state = jnp.zeros((STATE, OWN), F32)
        total = jnp.zeros((MINE, 1), F32)
        for g in range(GROUPS):
            rows = slice(GROUP * g, GROUP * g + GROUP)
            for j in range(6):
                cols = slice(128 * j, 128 * j + 128)
                first = HALO - 3 + GROUP * g
                acc = prm[4:5, cols] + prm[0:1, cols] * proj[first : first + GROUP, cols]
                for k in range(1, CONV):
                    acc = acc + prm[k : k + 1, cols] * proj[first + k : first + k + GROUP, cols]
                half = 0.5 * acc
                done = (half + half * jnp.tanh(half)).astype(BF16)
                if j < 4:
                    xs[strand, rows, cols] = done
                else:
                    maps[strand, rows, 128 * (j - 4) : 128 * (j - 4) + 128] = done
            part = slice(MINE * g, MINE * g + MINE)
            last = cumulated[part, GROUP - 1 :]
            total = total + last
            remaining = spread_columns(jnp.exp(last - cumulated[part]) * size[part])
            weighted = (xs[strand, rows, :].astype(F32) * remaining).astype(BF16)
            starts[strand, g] = state.astype(BF16)
            added = lax.dot_general(
                maps[strand, rows, :STATE], weighted, (((0,), (0,)), ((), ())), preferred_element_type=F32
            )
            state = state * spread_row(jnp.exp(last)) + added
        ends[strand, :STATE, :] = state.astype(BF16)
        hi, lo = hi_lo(spread_row(total))
        line = iota2((HALO, OWN), 0)
        ends[strand, STATE:, :] = jnp.where(line == 0, hi, jnp.where(line == 1, lo, 0.0)).astype(BF16)
        return 0

    lax.fori_loop(0, 2, one_strand, 0)
    role = chain(z)
    kept[...] = ends[role]
    given[...] = ends[1 - role]


def chain(z):
    return 1 - lax.rem(z, 2)


def decay_of(ref):
    rows = ref[STATE:, :].astype(F32)
    return rows[0:1] + rows[1:2]


def pair_state(kept, mate, out):
    decay = decay_of(kept)
    out[:STATE, :] = (kept[:STATE, :].astype(F32) + jnp.exp(decay) * mate[:STATE, :].astype(F32)).astype(BF16)
    hi, lo = hi_lo(decay + decay_of(mate))
    line = iota2((HALO, OWN), 0)
    out[STATE:, :] = jnp.where(line == 0, hi, jnp.where(line == 1, lo, 0.0)).astype(BF16)


def earlier_pairs(*refs):
    *pairs, out = refs
    total = jnp.zeros((STATE, OWN), F32)
    gone = jnp.zeros((1, OWN), F32)
    for pair in pairs:
        total = total + jnp.exp(gone) * pair[:STATE, :].astype(F32)
        gone = gone + decay_of(pair)
    out[...] = total.astype(BF16)


def local_kernel(*refs):
    xs, maps, sizes, sums, starts, _, local, carry = refs
    causal = ones_at(iota2((GROUP, GROUP), 0) >= iota2((GROUP, GROUP), 1))
    left = iota2((GROUP, 128), 1) < HEADDIM

    def one_strand(strand, _):
        def one_group(g, before):
            rows = pl.ds(pl.multiple_of(GROUP * g, GROUP), GROUP)
            part = pl.ds(pl.multiple_of(MINE * g, MINE), MINE)
            size = sizes[strand, part, :]
            cumulated = sums[strand, part, :]
            columns = jnp.concatenate([cumulated, jnp.zeros((GROUP - MINE, GROUP), F32)], axis=0).T
            in_map = maps[strand, rows, :STATE]
            out_map = maps[strand, rows, STATE:]
            affinity = lax.dot_general(
                out_map, in_map, (((1,), (1,)), ((), ())), preferred_element_type=F32
            ) * causal
            parts = []
            for pair in range(4):
                mixes = []
                for h in (2 * pair, 2 * pair + 1):
                    gap = jnp.minimum(columns[:, h : h + 1] - cumulated[h : h + 1, :], 0.0)
                    mixes.append((affinity * jnp.exp(gap) * size[h : h + 1, :]).astype(BF16))
                x = xs[strand, rows, 128 * pair : 128 * pair + 128]
                zero = jnp.zeros_like(x)
                tall = jnp.concatenate([jnp.where(left, x, zero), jnp.where(left, zero, x)], axis=0)
                parts.append(jnp.dot(jnp.concatenate(mixes, axis=1), tall, preferred_element_type=F32))
            within = jnp.concatenate(parts, axis=1)
            grown = spread_columns(jnp.exp(cumulated))
            local[strand, rows, :] = within + jnp.dot(out_map, starts[strand, g], preferred_element_type=F32) * grown
            carry[strand, rows, :] = grown * spread_row(jnp.exp(before))
            return before + cumulated[:, GROUP - 1 :]

        lax.fori_loop(0, GROUPS, one_group, jnp.zeros((MINE, 1), F32))
        return 0

    lax.fori_loop(0, 2, one_strand, 0)


def gate_kernel(act, *refs):
    received, refs = refs[:4], refs[4:]
    gate, out_weight, weight = refs
    _, _, _, yh, x, _ = place()
    units = []
    for k, unit in enumerate(received):
        for n, which in enumerate((yh, 1 - yh)):
            units.append((unit, LATE * n, which * 4 + lax.rem(x - k + 4, 4)))
    for unit, first, f in units:
        lanes = pl.ds(pl.multiple_of(128 * f, 128), 128)
        for j in range(MINE):
            weight[64 * j : 64 * j + 64, lanes] = unit[first : first + 64, 128 * j : 128 * j + 128]
        rows = pl.ds(pl.multiple_of(64 * f, 64), 64)
        for half in range(2):
            out_weight[half, rows, :] = unit[first + 64 : first + 128, 512 * half : 512 * half + 512]
    for strand in range(2):
        half = 0.5 * times_turned(act[strand, HALO:, :], weight[...]).astype(BF16).astype(F32)
        gate[strand] = half + half * jnp.tanh(half)


def half_rows(own):
    _, yl, _, _, _, _ = place()
    y = yl if own else 1 - yl
    return 256 * y, 256 * (1 - y)


def project_half(own, weight, entering, prm, maps, local, carry, gate, keep, give, normed):
    _, _, c, _, _, _ = place()
    gain = prm[5:6, :OWN]
    tails = []
    for strand, first in enumerate(half_rows(own)):
        for b in range(2):
            rows = pl.ds(pl.multiple_of(first + ROWS * b, ROWS), ROWS)
            held = jnp.dot(maps[strand, rows, STATE:], entering[strand], preferred_element_type=F32)
            gated = (local[strand, rows, :] + held * carry[strand, rows, :]) * gate[strand, rows, :]
            squared = gated * gated
            folded = (squared[:, :128] + squared[:, 128:256]) + (squared[:, 256:384] + squared[:, 384:])
            tails.append(jnp.sum(folded.T, axis=0, keepdims=True))
            normed[2 * strand + b] = (gated * gain).astype(BF16)
    line = iota2((HALO, ROWS), 0)
    for ref, core in ((keep, c), (give, 1 - c)):
        for strand in range(2):
            b = core if strand == 0 else 1 - core
            for half in range(2):
                ref[ROWS * strand : ROWS * strand + ROWS, 512 * half : 512 * half + 512] = jnp.dot(
                    normed[2 * strand + b], weight[half], preferred_element_type=F32
                ).astype(BF16)
            hi, lo = hi_lo(jnp.where(b == 0, tails[2 * strand], tails[2 * strand + 1]))
            tail = jnp.where(line == 0, hi, jnp.where(line == 1, lo, 0.0))
            ref[2 * ROWS :, ROWS * strand : ROWS * strand + ROWS] = tail.astype(BF16)
        ref[2 * ROWS :, 2 * ROWS :] = jnp.zeros((HALO, D - 2 * ROWS), BF16)


def first_half(*refs):
    mate, entered, mate_entered, refs = refs[0], refs[1], refs[2], refs[3:]
    weight, prm, maps, local, carry, gate, entering, keep, give, normed = refs
    z, _, _, _, _, _ = place()
    role = chain(z)
    entering[role] = (
        mate[:STATE, :].astype(F32) + jnp.exp(decay_of(mate)) * entered[...].astype(F32)
    ).astype(BF16)
    entering[1 - role] = mate_entered[...]
    project_half(False, weight, entering, prm, maps, local, carry, gate, keep, give, normed)


def second_half(weight, entering, prm, maps, local, carry, gate, keep, give, normed):
    project_half(True, weight, entering, prm, maps, local, carry, gate, keep, give, normed)


def pair_sum(mine, came, second, out):
    main = mine[: 2 * ROWS, :].astype(F32) + came[: 2 * ROWS, :].astype(F32)
    out[: 2 * ROWS, :] = main.astype(BF16)
    tail = mine[2 * ROWS :, :].astype(F32) + came[2 * ROWS :, :].astype(F32)
    hi, lo = hi_lo(tail[0:1] + tail[1:2])
    line = iota2((HALO, D), 0)
    out[2 * ROWS :, :] = jnp.where(line == 0, hi, jnp.where(line == 1, lo, 0.0)).astype(BF16)


def last_kernel(mine, came, far, out):
    def tail(ref):
        rows = ref[2 * ROWS :, :].astype(F32)
        return rows[0:1] + rows[1:2]

    squares = tail(mine) + tail(came) + tail(far)
    diagonal = iota2((ROWS, ROWS), 0) == iota2((ROWS, ROWS), 1)
    for strand in range(2):
        rows = slice(ROWS * strand, ROWS * strand + ROWS)
        mean = jnp.sum(jnp.where(diagonal, squares[:, rows], 0.0), axis=1, keepdims=True) * (1.0 / E)
        main = mine[rows, :].astype(F32) + came[rows, :].astype(F32) + far[rows, :].astype(F32)
        block = (main * lax.rsqrt(mean + 1e-05)).astype(BF16)
        if strand:
            block = flipped(block)
        out[:, D * strand : D * strand + D] = block


def swap_core(value):
    return move(value, lambda z, yl, c, yh, x: dict(c=1 - c))


def swap_y(value):
    return move(value, lambda z, yl, c, yh, x: dict(yl=1 - yl))


def swap_diagonal(value, k=0):
    return move(value, lambda z, yl, c, yh, x: dict(yl=1 - yl, yh=1 - yh, x=(x + k) % 4))


def along_x(value, k):
    return move(value, lambda z, yl, c, yh, x: dict(x=(x + k) % 4))


def pair_step(m):
    def to(z, yl, c, yh, x):
        target = z + 2 * m if z % 2 else z - 2 * m
        return dict(z=target) if 0 <= target < Z else None

    return to


def halo_step(same):
    def to(z, yl, c, yh, x):
        t = 2 * yl + c
        if t == 3 and z < Z - 1:
            return dict(z=z + 1, yl=1 if same else 0)
        if t == 0 and z > 0:
            return dict(z=z - 1, yl=0 if same else 1)
        return None

    return to


def body(hidden, tokens, base_bias, in_weight, conv_weight, conv_bias, dt_bias, decay_rate, norm_gain, out_weight):
    act, halo, ua, ua_other, ub, ub_other = call(
        start_kernel,
        "start_kernel",
        [shape(2 * ROWS, D), shape(HALO, D)] + [shape(UNIT, 128)] * 2 + [shape(LATE, D)] * 2,
        [ANY] * 5,
        tuple(
            pltpu.with_memory_space_constraint(value, pltpu.HBM)
            for value in (hidden[0], tokens, base_bias, in_weight.T, out_weight)
        ),
        scratch=[
            pltpu.VMEM((ROWS, 2 * D), BF16),
            pltpu.VMEM((1, ROWS), jnp.int32),
            pltpu.VMEM((5, 2 * D), BF16),
            pltpu.VMEM((WIDE, ROWS), BF16),
            pltpu.VMEM((2 * ROWS, D), BF16),
            pltpu.SemaphoreType.DMA((6,)),
        ],
        mb=16,
    )
    act_y = swap_y(act)
    far = swap_diagonal(ua_other)
    own_1, own_3 = along_x(ua, 1), along_x(ua, 3)
    halo_a = move(halo, halo_step(True))
    halo, ub_other, ua_late = call(
        hold,
        "hold",
        [shape(HALO, D), shape(LATE, D), shape(UNIT, 128)],
        [VMEM] * 4,
        (halo, ub_other, ua, far),
        mb=8,
    )
    own_2 = along_x(ua_late, 2)
    far_1, far_3, far_2 = along_x(far, 1), along_x(far, 3), along_x(far, 2)
    units = (ua, own_1, own_2, own_3, far, far_1, far_2, far_3)
    halo_b = move(halo, halo_step(False))
    ub_far = swap_diagonal(ub_other)
    payload, late = call(
        pack_core,
        "pack_core",
        [shape(PAYLOAD, D), shape(2 * LATE, D)],
        [VMEM] * 14,
        (act, act_y, halo_a, halo_b, ub, ub_far, *units),
        mb=12,
    )
    swapped = swap_core(payload)
    late = (late, *[along_x(late, k) for k in (1, 2, 3)])
    prm, heads = call(
        pack_params,
        "pack_params",
        [shape(8, CONVED, dtype=F32), shape(2, MINE, 128, dtype=F32)],
        [VMEM] * 5,
        (conv_weight, conv_bias[None], dt_bias[None], decay_rate[None], norm_gain[None]),
        scratch=[pltpu.VMEM((8, E), F32)],
        mb=12,
    )
    xs, maps, sizes, sums, starts, act, kept, given = call(
        scan_kernel,
        "scan_kernel",
        [
            shape(2, SPAN, OWN),
            shape(2, SPAN, 2 * STATE),
            shape(2, MINE * GROUPS, GROUP, dtype=F32),
            shape(2, MINE * GROUPS, GROUP, dtype=F32),
            shape(2, GROUPS, STATE, OWN),
            shape(2, PAD, D),
        ]
        + [shape(STATE + HALO, OWN)] * 2,
        [VMEM] * 15,
        (act, act_y, halo_a, halo_b, swapped, *units, prm, heads),
        scratch=[
            pltpu.VMEM((WA, D), BF16),
            pltpu.VMEM((PAD, WA), F32),
            pltpu.VMEM((2, STATE + HALO, OWN), BF16),
        ],
        mb=24,
        flops=2 * 1056 * D * WA,
        bytes_accessed=8 << 20,
    )
    mate = move(given, lambda z, yl, c, yh, x: dict(z=z ^ 1))
    pair = call(pair_state, "pair_state", shape(STATE + HALO, OWN), [VMEM] * 2, (kept, mate), mb=8)
    earlier = [move(pair, pair_step(m)) for m in (1, 2, 3)]
    entered = call(earlier_pairs, "earlier_pairs", shape(STATE, OWN), [VMEM] * 3, earlier, mb=8)
    mate_entered = move(entered, lambda z, yl, c, yh, x: dict(z=z ^ 1))
    local, carry = call(
        local_kernel,
        "local_kernel",
        [shape(2, SPAN, OWN, dtype=F32)] * 2,
        [VMEM] * 6,
        (xs, maps, sizes, sums, starts, pair),
        mb=16,
        flops=8 * 1024 * D * OWN,
        bytes_accessed=16 << 20,
    )
    gate, weight = call(
        gate_kernel,
        "gate_kernel",
        [shape(2, SPAN, OWN, dtype=F32), shape(2, OWN, 512)],
        [VMEM] * (1 + len(late)),
        (act, *late),
        scratch=[pltpu.VMEM((OWN, D), BF16)],
        mb=16,
        flops=2 * 1024 * D * OWN,
        bytes_accessed=8 << 20,
    )
    half_out = [shape(2 * ROWS + HALO, D)] * 2
    half_scratch = [pltpu.VMEM((4, ROWS, OWN), BF16)]
    entering, keep, give = call(
        first_half,
        "first_half",
        [shape(2, STATE, OWN)] + half_out,
        [VMEM] * 9,
        (mate, entered, mate_entered, weight, prm, maps, local, carry, gate),
        scratch=half_scratch,
        mb=16,
        flops=1024 * D * OWN,
        bytes_accessed=4 << 20,
    )
    keep_2, give_2 = call(
        second_half,
        "second_half",
        half_out,
        [VMEM] * 7,
        (weight, entering, prm, maps, local, carry, gate),
        scratch=half_scratch,
        mb=16,
        flops=1024 * D * OWN,
        bytes_accessed=4 << 20,
    )
    part = call(
        pair_sum, "pair_sum", shape(2 * ROWS + HALO, D), [VMEM] * 3, (keep, swap_core(give), keep_2), mb=8
    )
    far_part = swap_y(part)
    out = call(last_kernel, "last_kernel", shape(ROWS, 2 * D), [VMEM] * 3, (keep_2, swap_core(give_2), far_part), mb=8)
    return out[None]


def solution(mesh):
    placed = (
        P("fsdp", "seq", None),
        P("fsdp", "seq"),
        P(),
        P("fsdp", None),
        P(),
        P(),
        P(),
        P(),
        P(),
        P("fsdp", None),
    )
    return jax.shard_map(
        body, mesh=mesh, in_specs=placed, out_specs=P("fsdp", "seq", None), check_vma=False
    )
```

time: 126 us -> 102 us (0.81); the launches traced: 124 us -> 102 us
  starting transfers between devices: 53 us -> 37.3 us
  waiting for transfers between devices: 30.4 us -> 43.5 us
  Pallas kernels: 31.4 us -> 21 us
  local copies, waits for them, and re-layouts: 8.83 us -> 0.04 us
    ppermute x28 -> x23, starting transfers between devices: 53 us -> 37.3 us  [move(): return lax.ppermute(value, ('seq', 'fsdp'), pairs)]
    ppermute x28 -> x23, waiting for transfers between devices: 30.4 us -> 43.5 us  [move(): return lax.ppermute(value, ('seq', 'fsdp'), pairs)]
    pallas_call x11 -> x13, Pallas kernels: 31.4 us -> 21 us  [call(): pl.pallas_call(kernel, out_shape=outs, in_specs=ins, out_specs=jax.tree.m...]
    unnamed x31 -> x10, local copies, waits for them, and re-layouts: 8.82 us -> 0.03 us
  transfers between devices with their start and end apart: 28 -> 23, of which waited for: 10 -> 12; matrix products, arithmetic and copies ran while one was open for 1% -> 0% of each run, Pallas kernels for 19% -> 16%
where the time goes in v3:
time: 102 us
  waiting for transfers between devices  43.5 us (43%)
  starting transfers between devices  37.3 us (37%)
  Pallas kernels  21 us (21%)
    ppermute x23, waiting for transfers between devices, move(): return lax.ppermute(value, ('seq', 'fsdp'), pairs)  43.5 us
    ppermute x23, starting transfers between devices, move(): return lax.ppermute(value, ('seq', 'fsdp'), pairs)  37.3 us
    pallas_call x13, Pallas kernels, call(): pl.pallas_call(kernel, out_shape=outs, in_specs=ins, out_specs=jax.tree.m...  21 us
  transfers between devices with their start and end apart: 23, of which 12 were waited for; matrix products, arithmetic and copies ran while one was open for 0% of the time, Pallas kernels for 16%

profile of v3, /device:TPU:1, one launch (start us, length us, event | category | flops | bytes accessed | tf_op | source)
XLA Modules:
  0.0 102.1 jit_solution(14230007858949304529)
XLA Ops:
  0.0 1.9 %start_kernel.1 = (bf16[256,1024]{1,0:T(8,128)(2,1)S(1)}, bf16[16,1024]{1,0:T(8,128)(2,1)S(1)}, bf16[672,128]{1,0:T(8,128)(2,1)S(1)}, bf16[672,128]{1,0:T(8,128)...) custom-call(bf16[128,2048]{1,0:T(8,128)(2,1)} %bitcast.10, s32[1,128]{1,0:T(1,128)} %tokens.1, ...), custom_call_target="tpu_custom_call" | custom-call | tf_op jit(solution)/shard_map/start_kernel/pallas_call | solution.py:62
  1.9 0.0 copy-start.4
  1.9 0.0 copy-start.2
  1.9 2.2 %collective-permute-start = (bf16[256,1024]{1,0:T(8,128)(2,1)S(1)}, bf16[256,1024]{1,0:T(8,128)(2,1)S(1)}, u32[]{:S(2)}, u32[]{:S(2)}) collective-permute-start(bf16[256,1024]{1,0:T(8,128)(2,1)S(1)} %get-tuple-element.35.refs_0_), channel_id=1, source_target_pairs={{0,16},{1,17},{2,18},{3,19},{4,20},{5,21},{6,22},{7,23},{8,24},{9,... | collective-permute-start | bytes 1572872 | tf_op jit(solution)/shard_map/ppermute | solution.py:54
  4.2 1.9 %collective-permute-start.2 = (bf16[672,128]{1,0:T(8,128)(2,1)S(1)}, bf16[672,128]{1,0:T(8,128)(2,1)S(1)}, u32[]{:S(2)}, u32[]{:S(2)}) collective-permute-start(bf16[672,128]{1,0:T(8,128)(2,1)S(1)} %get-tuple-element.39), channel_id=1, source_target_pairs={{0,20},{1,21},{2,22},{3,23},{4,16},{5,17},{6,18},{7,19},{8,28},{9,... | collective-permute-start | bytes 516104 | tf_op jit(solution)/shard_map/ppermute | solution.py:54
  6.1 1.2 %collective-permute-start.5 = (bf16[672,128]{1,0:T(8,128)(2,1)S(1)}, bf16[672,128]{1,0:T(8,128)(2,1)S(1)}, u32[]{:S(2)}, u32[]{:S(2)}) collective-permute-start(bf16[672,128]{1,0:T(8,128)(2,1)S(1)} %get-tuple-element.38.refs_2_.refs_6_.refs_5_), channel_id=1, source_target_pairs={{0,1},{1,2},{2,3},{3,0},{4,5},{5,6},{6,7},{7,4},{8,9},{9,10},{10,1... | collective-permute-start | bytes 516104 | tf_op jit(solution)/shard_map/ppermute | solution.py:54
  7.3 1.5 %collective-permute-start.7 = (bf16[672,128]{1,0:T(8,128)(2,1)S(1)}, bf16[672,128]{1,0:T(8,128)(2,1)S(1)}, u32[]{:S(2)}, u32[]{:S(2)}) collective-permute-start(bf16[672,128]{1,0:T(8,128)(2,1)S(1)} %get-tuple-element.38.refs_2_.refs_6_.refs_5_), channel_id=1, source_target_pairs={{0,3},{1,0},{2,1},{3,2},{4,7},{5,4},{6,5},{7,6},{8,11},{9,8},{10,9... | collective-permute-start | bytes 516104 | tf_op jit(solution)/shard_map/ppermute | solution.py:54
  8.7 1.3 %collective-permute-done.2.refs_3_.refs_10_.refs_9_ = bf16[672,128]{1,0:T(8,128)(2,1)S(1)} collective-permute-done((bf16[672,128]{1,0:T(8,128)(2,1)S(1)}, bf16[672,128]{1,0:T(8,128)(2,1)S(1)}, u32[]{:S(2)}, u32[]{:S(2)}) %collective-permute-start.2) | collective-permute-done | bytes 172064 | tf_op jit(solution)/shard_map/ppermute | solution.py:54
  10.0 3.1 %collective-permute-start.6 = (bf16[672,128]{1,0:T(8,128)(2,1)S(1)}, bf16[672,128]{1,0:T(8,128)(2,1)S(1)}, u32[]{:S(2)}, u32[]{:S(2)}) collective-permute-start(bf16[672,128]{1,0:T(8,128)(2,1)S(1)} %get-tuple-element.43), channel_id=1, source_target_pairs={{0,2},{1,3},{2,0},{3,1},{4,6},{5,7},{6,4},{7,5},{8,10},{9,11},{10,... | collective-permute-start | bytes 516104 | tf_op jit(solution)/shard_map/ppermute | solution.py:54
  13.2 0.7 collective-permute-start.1
  13.8 5.8 %collective-permute-start.4 = (bf16[128,1024]{1,0:T(8,128)(2,1)S(1)}, bf16[128,1024]{1,0:T(8,128)(2,1)S(1)}, u32[]{:S(2)}, u32[]{:S(2)}) collective-permute-start(bf16[128,1024]{1,0:T(8,128)(2,1)S(1)} %get-tuple-element.42), channel_id=1, source_target_pairs={{0,20},{1,21},{2,22},{3,23},{4,16},{5,17},{6,18},{7,19},{8,28},{9,... | collective-permute-start | bytes 786440 | tf_op jit(solution)/shard_map/ppermute | solution.py:54
  19.6 0.7 collective-permute-start.3
  20.3 0.4 collective-permute-start.8
  20.7 1.8 %collective-permute-start.9 = (bf16[672,128]{1,0:T(8,128)(2,1)S(1)}, bf16[672,128]{1,0:T(8,128)(2,1)S(1)}, u32[]{:S(2)}, u32[]{:S(2)}) collective-permute-start(bf16[672,128]{1,0:T(8,128)(2,1)S(1)} %collective-permute-done.2.refs_3_.refs_10_.refs_9_), channel_id=1, source_target_pairs={{0,2},{1,3},{2,0},{3,1},{4,6},{5,7},{6,4},{7,5},{8,10},{9,11},{10,... | collective-permute-start | bytes 516104 | tf_op jit(solution)/shard_map/ppermute | solution.py:54
  22.4 0.8 collective-permute-start.10
  23.2 4.3 %collective-permute-done.8.refs_11_.refs_10_ = bf16[672,128]{1,0:T(8,128)(2,1)S(1)} collective-permute-done((bf16[672,128]{1,0:T(8,128)(2,1)S(1)}, bf16[672,128]{1,0:T(8,128)(2,1)S(1)}, u32[]{:S(2)}, u32[]{:S(2)}) %collective-permute-start.8) | collective-permute-done | bytes 172064 | tf_op jit(solution)/shard_map/ppermute | solution.py:54
  27.5 1.2 %collective-permute-done.9.refs_12_.refs_11_ = bf16[672,128]{1,0:T(8,128)(2,1)S(1)} collective-permute-done((bf16[672,128]{1,0:T(8,128)(2,1)S(1)}, bf16[672,128]{1,0:T(8,128)(2,1)S(1)}, u32[]{:S(2)}, u32[]{:S(2)}) %collective-permute-start.9) | collective-permute-done | bytes 172064 | tf_op jit(solution)/shard_map/ppermute | solution.py:54
  28.7 1.7 %collective-permute-done.10.refs_13_.refs_12_ = bf16[672,128]{1,0:T(8,128)(2,1)S(1)} collective-permute-done((bf16[672,128]{1,0:T(8,128)(2,1)S(1)}, bf16[672,128]{1,0:T(8,128)(2,1)S(1)}, u32[]{:S(2)}, u32[]{:S(2)}) %collective-permute-start.10) | collective-permute-done | bytes 172064 | tf_op jit(solution)/shard_map/ppermute | solution.py:54
  30.4 0.2 pack_core.1
  30.6 2.3 %collective-permute-start.11 = (bf16[656,1024]{1,0:T(8,128)(2,1)S(1)}, bf16[656,1024]{1,0:T(8,128)(2,1)S(1)}, u32[]{:S(2)}, u32[]{:S(2)}) collective-permute-start(bf16[656,1024]{1,0:T(8,128)(2,1)S(1)} %get-tuple-element.44), channel_id=1, source_target_pairs={{0,8},{1,9},{2,10},{3,11},{4,12},{5,13},{6,14},{7,15},{8,0},{9,1},... | collective-permute-start | bytes 4030472 | tf_op jit(solution)/shard_map/ppermute | solution.py:54
  32.9 0.1 collective-permute-start.12
  33.0 3.3 %collective-permute-start.13 = (bf16[256,1024]{1,0:T(8,128)(2,1)S(1)}, bf16[256,1024]{1,0:T(8,128)(2,1)S(1)}, u32[]{:S(2)}, u32[]{:S(2)}) collective-permute-start(bf16[256,1024]{1,0:T(8,128)(2,1)S(1)} %get-tuple-element.48.refs_0_), channel_id=1, source_target_pairs={{0,2},{1,3},{2,0},{3,1},{4,6},{5,7},{6,4},{7,5},{8,10},{9,11},{10,... | collective-permute-start | bytes 1572872 | tf_op jit(solution)/shard_map/ppermute | solution.py:54
  36.4 0.6 pack_params.1
  36.9 7.9 %scan_kernel.1 = (bf16[2,512,512]{2,1,0:T(8,128)(2,1)S(1)}, bf16[2,512,256]{2,1,0:T(8,128)(2,1)S(1)}, f32[2,32,128]{2,1,0:T(8,128)S(1)}, f32[2,32,128]{2,1,0:T(8...) custom-call(bf16[256,1024]{1,0:T(8,128)(2,1)S(1)} %get-tuple-element, ...), custom_call_target="tpu_custom_call" | custom-call | flops 1937768448 | bytes 8388608 | tf_op jit(solution)/shard_map/scan_kernel/pallas_call | solution.py:62
  44.9 6.5 %collective-permute-start.15 = (bf16[144,512]{1,0:T(8,128)(2,1)S(1)}, bf16[144,512]{1,0:T(8,128)(2,1)S(1)}, u32[]{:S(2)}, u32[]{:S(2)}) collective-permute-start(bf16[144,512]{1,0:T(8,128)(2,1)S(1)} %get-tuple-element.50), channel_id=1, source_target_pairs={{0,32},{1,33},{2,34},{3,35},{4,36},{5,37},{6,38},{7,39},{8,40},{9,... | collective-permute-start | bytes 442376 | tf_op jit(solution)/shard_map/ppermute | solution.py:54
  51.4 3.3 %collective-permute-done.15.mate.refs_0_ = bf16[144,512]{1,0:T(8,128)(2,1)S(1)} collective-permute-done((bf16[144,512]{1,0:T(8,128)(2,1)S(1)}, bf16[144,512]{1,0:T(8,128)(2,1)S(1)}, u32[]{:S(2)}, u32[]{:S(2)}) %collective-permute-start.15) | collective-permute-done | bytes 147488 | tf_op jit(solution)/shard_map/ppermute | solution.py:54
  54.7 0.1 pair_state.1.refs_5_
  54.8 1.3 %collective-permute-start.16 = (bf16[144,512]{1,0:T(8,128)(2,1)S(1)}, bf16[144,512]{1,0:T(8,128)(2,1)S(1)}, u32[]{:S(2)}, u32[]{:S(2)}) collective-permute-start(bf16[144,512]{1,0:T(8,128)(2,1)S(1)} %pair_state.1.refs_5_), channel_id=1, source_target_pairs={{32,96},{33,97},{34,98},{35,99},{36,100},{37,101},{38,102},{39,103... | collective-permute-start | bytes 442376 | tf_op jit(solution)/shard_map/ppermute | solution.py:54
  56.1 1.3 %collective-permute-start.17 = (bf16[144,512]{1,0:T(8,128)(2,1)S(1)}, bf16[144,512]{1,0:T(8,128)(2,1)S(1)}, u32[]{:S(2)}, u32[]{:S(2)}) collective-permute-start(bf16[144,512]{1,0:T(8,128)(2,1)S(1)} %pair_state.1.refs_5_), channel_id=1, source_target_pairs={{32,160},{33,161},{34,162},{35,163},{36,164},{37,165},{38,166},{39... | collective-permute-start | bytes 442376 | tf_op jit(solution)/shard_map/ppermute | solution.py:54
  57.4 1.3 %collective-permute-start.18 = (bf16[144,512]{1,0:T(8,128)(2,1)S(1)}, bf16[144,512]{1,0:T(8,128)(2,1)S(1)}, u32[]{:S(2)}, u32[]{:S(2)}) collective-permute-start(bf16[144,512]{1,0:T(8,128)(2,1)S(1)} %pair_state.1.refs_5_), channel_id=1, source_target_pairs={{32,224},{33,225},{34,226},{35,227},{36,228},{37,229},{38,230},{39... | collective-permute-start | bytes 442376 | tf_op jit(solution)/shard_map/ppermute | solution.py:54
  58.7 0.9 collective-permute-done.13.refs_2_
  59.6 1.8 %gate_kernel.1 = (f32[2,512,512]{2,1,0:T(8,128)S(1)}, bf16[2,512,512]{2,1,0:T(8,128)(2,1)S(1)}) custom-call(bf16[2,528,1024]{2,1,0:T(8,128)(2,1)S(1)} %get-tuple-element.47.act, bf16[256,1024]{1,0:T(8,128)(2,1)S(1)} %get-tuple-element.48.refs_0_, bf16[256,1024]{1,0:T(8,128)(2,1)S(1)} %collective-permute-done.12.refs_1_, ...), custom_call_target="tpu_custom_call" | custom-call | flops 1073741824 | bytes 8388608 | tf_op jit(solution)/shard_map/gate_kernel/pallas_call | solution.py:62
  61.4 1.0 %collective-permute-done.16.refs_0_ = bf16[144,512]{1,0:T(8,128)(2,1)S(1)} collective-permute-done((bf16[144,512]{1,0:T(8,128)(2,1)S(1)}, bf16[144,512]{1,0:T(8,128)(2,1)S(1)}, u32[]{:S(2)}, u32[]{:S(2)}) %collective-permute-start.16) | collective-permute-done | bytes 147488 | tf_op jit(solution)/shard_map/ppermute | solution.py:54
  62.4 9.5 %collective-permute-done.17.refs_1_ = bf16[144,512]{1,0:T(8,128)(2,1)S(1)} collective-permute-done((bf16[144,512]{1,0:T(8,128)(2,1)S(1)}, bf16[144,512]{1,0:T(8,128)(2,1)S(1)}, u32[]{:S(2)}, u32[]{:S(2)}) %collective-permute-start.17) | collective-permute-done | bytes 147488 | tf_op jit(solution)/shard_map/ppermute | solution.py:54
  71.9 5.9 %collective-permute-done.18.refs_2_ = bf16[144,512]{1,0:T(8,128)(2,1)S(1)} collective-permute-done((bf16[144,512]{1,0:T(8,128)(2,1)S(1)}, bf16[144,512]{1,0:T(8,128)(2,1)S(1)}, u32[]{:S(2)}, u32[]{:S(2)}) %collective-permute-start.18) | collective-permute-done | bytes 147488 | tf_op jit(solution)/shard_map/ppermute | solution.py:54
  77.8 0.1 earlier_pairs.1.refs_1_
  77.9 0.1 collective-permute-start.19
  78.0 5.0 %local_kernel.1 = (f32[2,512,512]{2,1,0:T(8,128)S(1)}, f32[2,512,512]{2,1,0:T(8,128)S(1)}) custom-call(bf16[2,512,512]{2,1,0:T(8,128)(2,1)S(1)} %get-tuple-element.53.refs_0_, bf16[2,512,256]{2,1,0:T(8,128)(2,1)S(1)} %get-tuple-element.52.refs_1_.refs_5_.maps, f32[2,32,128]{2,1,0:T(8,128)S(1)} %get-tuple-element.54.refs_2_, ...), custom_call_target="tpu_custom_call" | custom-call | flops 4294967296 | bytes 16777216 | tf_op jit(solution)/shard_map/local_kernel/pallas_call | solution.py:62
  83.0 1.1 %first_half.1 = (bf16[2,128,512]{2,1,0:T(8,128)(2,1)S(1)}, bf16[272,1024]{1,0:T(8,128)(2,1)S(1)}, bf16[272,1024]{1,0:T(8,128)(2,1)S(1)}) custom-call(bf16[144,512]{1,0:T(8,128)(2,1)S(1)} %collective-permute-done.15.mate.refs_0_, bf16[128,512]{1,0:T(8,128)(2,1)S(1)} %earlier_pairs.1.refs_1_, bf16[128,512]{1,0:T(8,128)(2,1)S(1)} %collective-permute-done.19.refs_2_, ...), custom_call_target="tpu_custom_call" | custom-call | flops 536870912 | bytes 4194304 | tf_op jit(solution)/shard_map/first_half/pallas_call | solution.py:62
  84.1 1.0 collective-permute-start.21
  85.1 1.0 %second_half.1 = (bf16[272,1024]{1,0:T(8,128)(2,1)S(1)}, bf16[272,1024]{1,0:T(8,128)(2,1)S(1)}) custom-call(bf16[2,512,512]{2,1,0:T(8,128)(2,1)S(1)} %get-tuple-element.49.refs_3_.weight, bf16[2,128,512]{2,1,0:T(8,128)(2,1)S(1)} %get-tuple-element.60.entering, f32[8,768]{1,0:T(8,128)S(1)} %get-tuple-element.45.refs_13_.refs_4_.prm, ...), custom_call_target="tpu_custom_call" | custom-call | flops 536870912 | bytes 4194304 | tf_op jit(solution)/shard_map/second_half/pallas_call | solution.py:62
  86.2 0.1 collective-permute-start.20
  86.3 0.4 collective-permute-done.21.came
  86.7 0.1 pair_sum.1
  86.9 0.1 collective-permute-start.22
  87.0 1.3 %collective-permute-done.20.came = bf16[272,1024]{1,0:T(8,128)(2,1)S(1)} collective-permute-done((bf16[272,1024]{1,0:T(8,128)(2,1)S(1)}, bf16[272,1024]{1,0:T(8,128)(2,1)S(1)}, u32[]{:S(2)}, u32[]{:S(2)}) %collective-permute-start.20) | collective-permute-done | bytes 557088 | tf_op jit(solution)/shard_map/ppermute | solution.py:54
  88.2 12.6 %collective-permute-done.22.far = bf16[272,1024]{1,0:T(8,128)(2,1)S(1)} collective-permute-done((bf16[272,1024]{1,0:T(8,128)(2,1)S(1)}, bf16[272,1024]{1,0:T(8,128)(2,1)S(1)}, u32[]{:S(2)}, u32[]{:S(2)}) %collective-permute-start.22) | collective-permute-done | bytes 557088 | tf_op jit(solution)/shard_map/ppermute | solution.py:54
  100.8 1.3 %last_kernel.1 = bf16[128,2048]{1,0:T(8,128)(2,1)} custom-call(bf16[272,1024]{1,0:T(8,128)(2,1)S(1)} %get-tuple-element.61.second.mine, bf16[272,1024]{1,0:T(8,128)(2,1)S(1)} %collective-permute-done.20.came, bf16[272,1024]{1,0:T(8,128)(2,1)S(1)} %collective-permute-done.22.far), custom_call_target="tpu_custom_call" | custom-call | tf_op jit(solution)/shard_map/last_kernel/pallas_call | solution.py:62
  (22 shorter events, 0.1 us)
Async XLA Ops:
  1.9 34.4 %copy-start.4 = (f32[2304]{0:T(1024)S(1)}, f32[2304]{0:T(1024)}, u32[]{:S(2)}) copy-start(f32[2304]{0:T(1024)} %param.15) | copy-start | bytes 27652
  1.9 34.4 %copy-start = (f32[4,2304]{1,0:T(4,128)S(1)}, f32[4,2304]{1,0:T(4,128)}, u32[]{:S(2)}) copy-start(f32[4,2304]{1,0:T(4,128)} %cw.1) | copy-start | bytes 110596
  1.9 34.4 %copy-start.1 = (f32[2048]{0:T(1024)S(1)}, f32[2048]{0:T(1024)}, u32[]{:S(2)}) copy-start(f32[2048]{0:T(1024)} %param.18) | copy-start | bytes 24580
  1.9 34.4 %copy-start.2 = (f32[32]{0:T(128)S(1)}, f32[32]{0:T(128)}, u32[]{:S(2)}) copy-start(f32[32]{0:T(128)} %param.16) | copy-start | bytes 388
  1.9 34.4 %copy-start.3 = (f32[32]{0:T(128)S(1)}, f32[32]{0:T(128)}, u32[]{:S(2)}) copy-start(f32[32]{0:T(128)} %param.17) | copy-start | bytes 388
  1.9 28.5 %collective-permute-start = (bf16[256,1024]{1,0:T(8,128)(2,1)S(1)}, bf16[256,1024]{1,0:T(8,128)(2,1)S(1)}, u32[]{:S(2)}, u32[]{:S(2)}) collective-permute-start(bf16[256,1024]{1,0:T(8,128)(2,1)S(1)} %get-tuple-element.35.refs_0_), channel_id=1, source_target_pairs={{0,16},{1,17},{2,18},{3,19},{4,20},{5,21},{6,22},{7,23},{8,24},{9,... | collective-permute-start | bytes 1572872 | tf_op jit(solution)/shard_map/ppermute | solution.py:54
  4.2 5.9 %collective-permute-start.2 = (bf16[672,128]{1,0:T(8,128)(2,1)S(1)}, bf16[672,128]{1,0:T(8,128)(2,1)S(1)}, u32[]{:S(2)}, u32[]{:S(2)}) collective-permute-start(bf16[672,128]{1,0:T(8,128)(2,1)S(1)} %get-tuple-element.39), channel_id=1, source_target_pairs={{0,20},{1,21},{2,22},{3,23},{4,16},{5,17},{6,18},{7,19},{8,28},{9,... | collective-permute-start | bytes 516104 | tf_op jit(solution)/shard_map/ppermute | solution.py:54
  6.1 13.6 %collective-permute-start.5 = (bf16[672,128]{1,0:T(8,128)(2,1)S(1)}, bf16[672,128]{1,0:T(8,128)(2,1)S(1)}, u32[]{:S(2)}, u32[]{:S(2)}) collective-permute-start(bf16[672,128]{1,0:T(8,128)(2,1)S(1)} %get-tuple-element.38.refs_2_.refs_6_.refs_5_), channel_id=1, source_target_pairs={{0,1},{1,2},{2,3},{3,0},{4,5},{5,6},{6,7},{7,4},{8,9},{9,10},{10,1... | collective-permute-start | bytes 516104 | tf_op jit(solution)/shard_map/ppermute | solution.py:54
  7.3 13.0 %collective-permute-start.7 = (bf16[672,128]{1,0:T(8,128)(2,1)S(1)}, bf16[672,128]{1,0:T(8,128)(2,1)S(1)}, u32[]{:S(2)}, u32[]{:S(2)}) collective-permute-start(bf16[672,128]{1,0:T(8,128)(2,1)S(1)} %get-tuple-element.38.refs_2_.refs_6_.refs_5_), channel_id=1, source_target_pairs={{0,3},{1,0},{2,1},{3,2},{4,7},{5,4},{6,5},{7,6},{8,11},{9,8},{10,9... | collective-permute-start | bytes 516104 | tf_op jit(solution)/shard_map/ppermute | solution.py:54
  10.0 12.4 %collective-permute-start.6 = (bf16[672,128]{1,0:T(8,128)(2,1)S(1)}, bf16[672,128]{1,0:T(8,128)(2,1)S(1)}, u32[]{:S(2)}, u32[]{:S(2)}) collective-permute-start(bf16[672,128]{1,0:T(8,128)(2,1)S(1)} %get-tuple-element.43), channel_id=1, source_target_pairs={{0,2},{1,3},{2,0},{3,1},{4,6},{5,7},{6,4},{7,5},{8,10},{9,11},{10,... | collective-permute-start | bytes 516104 | tf_op jit(solution)/shard_map/ppermute | solution.py:54
  13.2 0.7 collective-permute-start.1
  13.8 16.6 %collective-permute-start.4 = (bf16[128,1024]{1,0:T(8,128)(2,1)S(1)}, bf16[128,1024]{1,0:T(8,128)(2,1)S(1)}, u32[]{:S(2)}, u32[]{:S(2)}) collective-permute-start(bf16[128,1024]{1,0:T(8,128)(2,1)S(1)} %get-tuple-element.42), channel_id=1, source_target_pairs={{0,20},{1,21},{2,22},{3,23},{4,16},{5,17},{6,18},{7,19},{8,28},{9,... | collective-permute-start | bytes 786440 | tf_op jit(solution)/shard_map/ppermute | solution.py:54
  19.6 1.0 %collective-permute-start.3 = (bf16[16,1024]{1,0:T(8,128)(2,1)S(1)}, bf16[16,1024]{1,0:T(8,128)(2,1)S(1)}, u32[]{:S(2)}, u32[]{:S(2)}) collective-permute-start(bf16[16,1024]{1,0:T(8,128)(2,1)S(1)} %get-tuple-element.40), channel_id=1, source_target_pairs={{24,40},{25,41},{26,42},{27,43},{28,44},{29,45},{30,46},{31,47},{3... | collective-permute-start | bytes 98312 | tf_op jit(solution)/shard_map/ppermute | solution.py:54
  20.3 7.2 %collective-permute-start.8 = (bf16[672,128]{1,0:T(8,128)(2,1)S(1)}, bf16[672,128]{1,0:T(8,128)(2,1)S(1)}, u32[]{:S(2)}, u32[]{:S(2)}) collective-permute-start(bf16[672,128]{1,0:T(8,128)(2,1)S(1)} %collective-permute-done.2.refs_3_.refs_10_.refs_9_), channel_id=1, source_target_pairs={{0,1},{1,2},{2,3},{3,0},{4,5},{5,6},{6,7},{7,4},{8,9},{9,10},{10,1... | collective-permute-start | bytes 516104 | tf_op jit(solution)/shard_map/ppermute | solution.py:54
  20.7 8.0 %collective-permute-start.9 = (bf16[672,128]{1,0:T(8,128)(2,1)S(1)}, bf16[672,128]{1,0:T(8,128)(2,1)S(1)}, u32[]{:S(2)}, u32[]{:S(2)}) collective-permute-start(bf16[672,128]{1,0:T(8,128)(2,1)S(1)} %collective-permute-done.2.refs_3_.refs_10_.refs_9_), channel_id=1, source_target_pairs={{0,2},{1,3},{2,0},{3,1},{4,6},{5,7},{6,4},{7,5},{8,10},{9,11},{10,... | collective-permute-start | bytes 516104 | tf_op jit(solution)/shard_map/ppermute | solution.py:54
  22.4 8.0 %collective-permute-start.10 = (bf16[672,128]{1,0:T(8,128)(2,1)S(1)}, bf16[672,128]{1,0:T(8,128)(2,1)S(1)}, u32[]{:S(2)}, u32[]{:S(2)}) collective-permute-start(bf16[672,128]{1,0:T(8,128)(2,1)S(1)} %collective-permute-done.2.refs_3_.refs_10_.refs_9_), channel_id=1, source_target_pairs={{0,3},{1,0},{2,1},{3,2},{4,7},{5,4},{6,5},{7,6},{8,11},{9,8},{10,9... | collective-permute-start | bytes 516104 | tf_op jit(solution)/shard_map/ppermute | solution.py:54
  30.6 6.3 %collective-permute-start.11 = (bf16[656,1024]{1,0:T(8,128)(2,1)S(1)}, bf16[656,1024]{1,0:T(8,128)(2,1)S(1)}, u32[]{:S(2)}, u32[]{:S(2)}) collective-permute-start(bf16[656,1024]{1,0:T(8,128)(2,1)S(1)} %get-tuple-element.44), channel_id=1, source_target_pairs={{0,8},{1,9},{2,10},{3,11},{4,12},{5,13},{6,14},{7,15},{8,0},{9,1},... | collective-permute-start | bytes 4030472 | tf_op jit(solution)/shard_map/ppermute | solution.py:54
  32.9 24.4 %collective-permute-start.12 = (bf16[256,1024]{1,0:T(8,128)(2,1)S(1)}, bf16[256,1024]{1,0:T(8,128)(2,1)S(1)}, u32[]{:S(2)}, u32[]{:S(2)}) collective-permute-start(bf16[256,1024]{1,0:T(8,128)(2,1)S(1)} %get-tuple-element.48.refs_0_), channel_id=1, source_target_pairs={{0,1},{1,2},{2,3},{3,0},{4,5},{5,6},{6,7},{7,4},{8,9},{9,10},{10,1... | collective-permute-start | bytes 1572872 | tf_op jit(solution)/shard_map/ppermute | solution.py:54
  33.0 26.5 %collective-permute-start.13 = (bf16[256,1024]{1,0:T(8,128)(2,1)S(1)}, bf16[256,1024]{1,0:T(8,128)(2,1)S(1)}, u32[]{:S(2)}, u32[]{:S(2)}) collective-permute-start(bf16[256,1024]{1,0:T(8,128)(2,1)S(1)} %get-tuple-element.48.refs_0_), channel_id=1, source_target_pairs={{0,2},{1,3},{2,0},{3,1},{4,6},{5,7},{6,4},{7,5},{8,10},{9,11},{10,... | collective-permute-start | bytes 1572872 | tf_op jit(solution)/shard_map/ppermute | solution.py:54
  36.3 23.2 %collective-permute-start.14 = (bf16[256,1024]{1,0:T(8,128)(2,1)S(1)}, bf16[256,1024]{1,0:T(8,128)(2,1)S(1)}, u32[]{:S(2)}, u32[]{:S(2)}) collective-permute-start(bf16[256,1024]{1,0:T(8,128)(2,1)S(1)} %get-tuple-element.48.refs_0_), channel_id=1, source_target_pairs={{0,3},{1,0},{2,1},{3,2},{4,7},{5,4},{6,5},{7,6},{8,11},{9,8},{10,9... | collective-permute-start | bytes 1572872 | tf_op jit(solution)/shard_map/ppermute | solution.py:54
  44.9 9.8 %collective-permute-start.15 = (bf16[144,512]{1,0:T(8,128)(2,1)S(1)}, bf16[144,512]{1,0:T(8,128)(2,1)S(1)}, u32[]{:S(2)}, u32[]{:S(2)}) collective-permute-start(bf16[144,512]{1,0:T(8,128)(2,1)S(1)} %get-tuple-element.50), channel_id=1, source_target_pairs={{0,32},{1,33},{2,34},{3,35},{4,36},{5,37},{6,38},{7,39},{8,40},{9,... | collective-permute-start | bytes 442376 | tf_op jit(solution)/shard_map/ppermute | solution.py:54
  54.8 7.6 %collective-permute-start.16 = (bf16[144,512]{1,0:T(8,128)(2,1)S(1)}, bf16[144,512]{1,0:T(8,128)(2,1)S(1)}, u32[]{:S(2)}, u32[]{:S(2)}) collective-permute-start(bf16[144,512]{1,0:T(8,128)(2,1)S(1)} %pair_state.1.refs_5_), channel_id=1, source_target_pairs={{32,96},{33,97},{34,98},{35,99},{36,100},{37,101},{38,102},{39,103... | collective-permute-start | bytes 442376 | tf_op jit(solution)/shard_map/ppermute | solution.py:54
  56.1 15.8 %collective-permute-start.17 = (bf16[144,512]{1,0:T(8,128)(2,1)S(1)}, bf16[144,512]{1,0:T(8,128)(2,1)S(1)}, u32[]{:S(2)}, u32[]{:S(2)}) collective-permute-start(bf16[144,512]{1,0:T(8,128)(2,1)S(1)} %pair_state.1.refs_5_), channel_id=1, source_target_pairs={{32,160},{33,161},{34,162},{35,163},{36,164},{37,165},{38,166},{39... | collective-permute-start | bytes 442376 | tf_op jit(solution)/shard_map/ppermute | solution.py:54
  57.4 20.5 %collective-permute-start.18 = (bf16[144,512]{1,0:T(8,128)(2,1)S(1)}, bf16[144,512]{1,0:T(8,128)(2,1)S(1)}, u32[]{:S(2)}, u32[]{:S(2)}) collective-permute-start(bf16[144,512]{1,0:T(8,128)(2,1)S(1)} %pair_state.1.refs_5_), channel_id=1, source_target_pairs={{32,224},{33,225},{34,226},{35,227},{36,228},{37,229},{38,230},{39... | collective-permute-start | bytes 442376 | tf_op jit(solution)/shard_map/ppermute | solution.py:54
  77.9 5.1 %collective-permute-start.19 = (bf16[128,512]{1,0:T(8,128)(2,1)S(1)}, bf16[128,512]{1,0:T(8,128)(2,1)S(1)}, u32[]{:S(2)}, u32[]{:S(2)}) collective-permute-start(bf16[128,512]{1,0:T(8,128)(2,1)S(1)} %earlier_pairs.1.refs_1_), channel_id=1, source_target_pairs={{0,32},{1,33},{2,34},{3,35},{4,36},{5,37},{6,38},{7,39},{8,40},{9,... | collective-permute-start | bytes 393224 | tf_op jit(solution)/shard_map/ppermute | solution.py:54
  84.1 2.6 %collective-permute-start.21 = (bf16[272,1024]{1,0:T(8,128)(2,1)S(1)}, bf16[272,1024]{1,0:T(8,128)(2,1)S(1)}, u32[]{:S(2)}, u32[]{:S(2)}) collective-permute-start(bf16[272,1024]{1,0:T(8,128)(2,1)S(1)} %get-tuple-element.64), channel_id=1, source_target_pairs={{0,8},{1,9},{2,10},{3,11},{4,12},{5,13},{6,14},{7,15},{8,0},{9,1},... | collective-permute-start | bytes 1671176 | tf_op jit(solution)/shard_map/ppermute | solution.py:54
  86.2 2.0 %collective-permute-start.20 = (bf16[272,1024]{1,0:T(8,128)(2,1)S(1)}, bf16[272,1024]{1,0:T(8,128)(2,1)S(1)}, u32[]{:S(2)}, u32[]{:S(2)}) collective-permute-start(bf16[272,1024]{1,0:T(8,128)(2,1)S(1)} %get-tuple-element.62), channel_id=1, source_target_pairs={{0,8},{1,9},{2,10},{3,11},{4,12},{5,13},{6,14},{7,15},{8,0},{9,1},... | collective-permute-start | bytes 1671176 | tf_op jit(solution)/shard_map/ppermute | solution.py:54
  86.9 13.9 %collective-permute-start.22 = (bf16[272,1024]{1,0:T(8,128)(2,1)S(1)}, bf16[272,1024]{1,0:T(8,128)(2,1)S(1)}, u32[]{:S(2)}, u32[]{:S(2)}) collective-permute-start(bf16[272,1024]{1,0:T(8,128)(2,1)S(1)} %pair_sum.1), channel_id=1, source_target_pairs={{0,16},{1,17},{2,18},{3,19},{4,20},{5,21},{6,22},{7,23},{8,24},{9,... | collective-permute-start | bytes 1671176 | tf_op jit(solution)/shard_map/ppermute | solution.py:54

commit v4 on v3

--- a/solution.py
+++ b/solution.py
@@ -23,7 +23,7 @@
 CONVED = OWN + 2 * STATE
 WA = CONVED + 128
 UNIT = OWN + STATE + HEADS
-LATE = 2 * HEADDIM
+LATE = 2 * OWN
 Z = 8
 PAYLOAD = 4 * ROWS + HALO + STATE
 
@@ -99,7 +99,7 @@
     return ones_at(row == 256 * (col // 64) + 64 * t + lax.rem(col, 64))
 
 
-def start_kernel(hidden, tokens, base_bias, iw, ow, act, halo, ua, ua_other, ub, ub_other, rows_in, ids_in, bias_in, iw_in, ow_in, sem):
+def start_kernel(hidden, tokens, base_bias, iw, ow, act, ua, ub, other, rows_in, ids_in, bias_in, iw_in, ow_in, sem):
     _, yl, c, _, _, t = place()
     copies = [
         pltpu.make_async_copy(tokens, ids_in, sem.at[0]),
@@ -125,23 +125,30 @@
         if strand:
             block = flipped(block)
         act[ROWS * strand : ROWS * strand + ROWS, :] = block
-    halo[...] = jnp.where(c == 1, act[ROWS - HALO : ROWS, :], act[2 * ROWS - HALO :, :])
     for copy in copies[3:]:
         copy.wait()
-    for early, late, which in ((ua, ub, t), (ua_other, ub_other, (1 - yl) * 2 + c)):
+    for early, first, late, second, which in ((ua, 0, ub, 0, t), (other, 0, other, UNIT, (1 - yl) * 2 + c)):
         for j in range(MINE):
             row = pl.multiple_of(256 * j + 64 * which, 64)
-            early[64 * j : 64 * j + 64, :] = iw_in[pl.ds(E + row, 64), :]
-            late[:HEADDIM, 128 * j : 128 * j + 128] = iw_in[pl.ds(row, 64), :]
-        early[OWN : OWN + STATE, :] = iw_in[pl.ds(pl.multiple_of(2 * E + STATE * c, STATE), STATE), :]
-        early[OWN + STATE :, :] = iw_in[2 * E + 2 * STATE :, :]
-        late[HEADDIM:, :] = ow_in[pl.ds(pl.multiple_of(64 * which, 64), 64), :]
-
-
-def hold(*refs):
-    count = (len(refs) - 1) // 2
-    for n in range(count):
-        refs[count + 1 + n][...] = refs[n][...]
+            early[first + 64 * j : first + 64 * j + 64, :] = iw_in[pl.ds(E + row, 64), :]
+            late[second + 64 * j : second + 64 * j + 64, :] = iw_in[pl.ds(row, 64), :]
+            out_rows = ow_in[pl.ds(pl.multiple_of(64 * which, 64), 64), 128 * j : 128 * j + 128]
+            late[second + OWN + 64 * j : second + OWN + 64 * j + 64, :] = out_rows
+        shared = iw_in[pl.ds(pl.multiple_of(2 * E + STATE * c, STATE), STATE), :]
+        early[first + OWN : first + OWN + STATE, :] = shared
+        early[first + OWN + STATE : first + UNIT, :] = iw_in[2 * E + 2 * STATE :, :]
+
+
+def split_far(both, prm, far):
+    far[...] = both[:UNIT, :]
+
+
+def choose_halo(act, act_y, far, halo, far_out):
+    _, yl, c, _, _, _ = place()
+    forward = jnp.where(yl == 1, act[ROWS - HALO : ROWS, :], act_y[ROWS - HALO : ROWS, :])
+    reverse = jnp.where(yl == 0, act[2 * ROWS - HALO :, :], act_y[2 * ROWS - HALO :, :])
+    halo[...] = jnp.where(c == 1, forward, reverse)
+    far_out[...] = far[...]
 
 
 def pack_params(cw, cb, dtb, rate, gain, prm, heads, stack):
@@ -165,13 +172,13 @@
 
 
 def pack_core(*refs):
-    act, act_y, halo_a, halo_b, ub, ub_far = refs[:6]
-    units, out, out_b = refs[6:14], refs[14], refs[15]
+    act, act_y, halo, ub, both = refs[:5]
+    units, out, out_b = refs[5:13], refs[13], refs[14]
     out_b[:LATE, :] = ub[...]
-    out_b[LATE:, :] = ub_far[...]
+    out_b[LATE:, :] = both[UNIT:, :]
     out[: 2 * ROWS, :] = act[...]
     out[2 * ROWS : 4 * ROWS, :] = act_y[...]
-    out[4 * ROWS : 4 * ROWS + HALO, :] = halo_a[...] + halo_b[...]
+    out[4 * ROWS : 4 * ROWS + HALO, :] = halo[...]
     for n, unit in enumerate(units):
         out[4 * ROWS + HALO :, 128 * n : 128 * n + 128] = unit[OWN : OWN + STATE, :]
 
@@ -225,13 +232,57 @@
     return lax.dot_general(a, b, (((1,), (1,)), ((), ())), preferred_element_type=F32)
 
 
-def scan_kernel(*refs):
-    act_own, act_y, halo_a, halo_b, swapped = refs[:5]
-    units, refs = refs[5:13], refs[13:]
-    prm, heads, refs = refs[0], refs[1], refs[2:]
-    xs, maps, sizes, sums, starts, act, kept, given = refs[:8]
-    weight, proj, ends = refs[8:]
-    z, _, c, _, _, t = place()
+def scan_strand(strand, act, weight, prm, heads, xs, maps, sizes, sums, starts, end, proj):
+    _, _, _, _, _, t = place()
+    choose = ones_at(iota2((MINE, HEADS), 1) == 4 * iota2((MINE, HEADS), 0) + t).astype(BF16)
+    proj[...] = times_turned(act[strand], weight[...]).astype(BF16).astype(F32)
+    turned = []
+    for g in range(GROUPS):
+        steps = proj[HALO + GROUP * g : HALO + GROUP * g + GROUP, CONVED:].T[:HEADS].astype(BF16)
+        turned.append(jnp.dot(choose, steps, preferred_element_type=F32))
+    raw = jnp.concatenate(turned, axis=0) + jnp.concatenate([heads[0]] * GROUPS, axis=0)
+    size = jnp.maximum(raw, 0.0) + jnp.log1p(jnp.exp(-jnp.abs(raw)))
+    decay = -size * jnp.concatenate([heads[1]] * GROUPS, axis=0)
+    cumulated = running_sum(decay)
+    sizes[...] = size
+    sums[...] = cumulated
+    state = jnp.zeros((STATE, OWN), F32)
+    total = jnp.zeros((MINE, 1), F32)
+    for g in range(GROUPS):
+        rows = slice(GROUP * g, GROUP * g + GROUP)
+        for j in range(6):
+            cols = slice(128 * j, 128 * j + 128)
+            first = HALO - 3 + GROUP * g
+            acc = prm[4:5, cols] + prm[0:1, cols] * proj[first : first + GROUP, cols]
+            for k in range(1, CONV):
+                acc = acc + prm[k : k + 1, cols] * proj[first + k : first + k + GROUP, cols]
+            half = 0.5 * acc
+            done = (half + half * jnp.tanh(half)).astype(BF16)
+            if j < 4:
+                xs[rows, cols] = done
+            else:
+                maps[rows, 128 * (j - 4) : 128 * (j - 4) + 128] = done
+        part = slice(MINE * g, MINE * g + MINE)
+        last = cumulated[part, GROUP - 1 :]
+        total = total + last
+        remaining = spread_columns(jnp.exp(last - cumulated[part]) * size[part])
+        weighted = (xs[rows, :].astype(F32) * remaining).astype(BF16)
+        starts[g] = state.astype(BF16)
+        added = lax.dot_general(
+            maps[rows, :STATE], weighted, (((0,), (0,)), ((), ())), preferred_element_type=F32
+        )
+        state = state * spread_row(jnp.exp(last)) + added
+    end[:STATE, :] = state.astype(BF16)
+    hi, lo = hi_lo(spread_row(total))
+    line = iota2((HALO, OWN), 0)
+    end[STATE:, :] = jnp.where(line == 0, hi, jnp.where(line == 1, lo, 0.0)).astype(BF16)
+
+
+def first_scan(*refs):
+    act_own, act_y, halo, swapped = refs[:4]
+    units, refs = refs[4:12], refs[12:]
+    prm, heads, xs, maps, sizes, sums, starts, act, weight, end, proj = refs
+    z, _, c, _, _, _ = place()
     weight[CONVED + HEADS :, :] = jnp.zeros((WA - CONVED - HEADS, D), BF16)
     for n, (unit, f) in enumerate(zip(units, weight_rows())):
         lanes = pl.ds(pl.multiple_of(128 * f, 128), 128)
@@ -242,61 +293,16 @@
         ]
         weight[CONVED : CONVED + HEADS, lanes] = unit[OWN + STATE :, :]
     place_act(act, ((act_own, 0), (act_y, 0), (swapped, 0), (swapped, 2 * ROWS)))
-    near = halo_a[...] + halo_b[...]
+    near = halo[...]
     far = swapped[4 * ROWS : 4 * ROWS + HALO, :]
     act[0, :HALO, :] = jnp.where(c == 1, near, far)
     act[1, :HALO, :] = jnp.where(c == 1, far, near)
-
-    choose = ones_at(iota2((MINE, HEADS), 1) == 4 * iota2((MINE, HEADS), 0) + t).astype(BF16)
-
-    def one_strand(strand, _):
-        proj[...] = times_turned(act[strand], weight[...]).astype(BF16).astype(F32)
-        turned = []
-        for g in range(GROUPS):
-            steps = proj[HALO + GROUP * g : HALO + GROUP * g + GROUP, CONVED:].T[:HEADS].astype(BF16)
-            turned.append(jnp.dot(choose, steps, preferred_element_type=F32))
-        raw = jnp.concatenate(turned, axis=0) + jnp.concatenate([heads[0]] * GROUPS, axis=0)
-        size = jnp.maximum(raw, 0.0) + jnp.log1p(jnp.exp(-jnp.abs(raw)))
-        decay = -size * jnp.concatenate([heads[1]] * GROUPS, axis=0)
-        cumulated = running_sum(decay)
-        sizes[strand] = size
-        sums[strand] = cumulated
-        state = jnp.zeros((STATE, OWN), F32)
-        total = jnp.zeros((MINE, 1), F32)
-        for g in range(GROUPS):
-            rows = slice(GROUP * g, GROUP * g + GROUP)
-            for j in range(6):
-                cols = slice(128 * j, 128 * j + 128)
-                first = HALO - 3 + GROUP * g
-                acc = prm[4:5, cols] + prm[0:1, cols] * proj[first : first + GROUP, cols]
-                for k in range(1, CONV):
-                    acc = acc + prm[k : k + 1, cols] * proj[first + k : first + k + GROUP, cols]
-                half = 0.5 * acc
-                done = (half + half * jnp.tanh(half)).astype(BF16)
-                if j < 4:
-                    xs[strand, rows, cols] = done
-                else:
-                    maps[strand, rows, 128 * (j - 4) : 128 * (j - 4) + 128] = done
-            part = slice(MINE * g, MINE * g + MINE)
-            last = cumulated[part, GROUP - 1 :]
-            total = total + last
-            remaining = spread_columns(jnp.exp(last - cumulated[part]) * size[part])
-            weighted = (xs[strand, rows, :].astype(F32) * remaining).astype(BF16)
-            starts[strand, g] = state.astype(BF16)
-            added = lax.dot_general(
-                maps[strand, rows, :STATE], weighted, (((0,), (0,)), ((), ())), preferred_element_type=F32
-            )
-            state = state * spread_row(jnp.exp(last)) + added
-        ends[strand, :STATE, :] = state.astype(BF16)
-        hi, lo = hi_lo(spread_row(total))
-        line = iota2((HALO, OWN), 0)
-        ends[strand, STATE:, :] = jnp.where(line == 0, hi, jnp.where(line == 1, lo, 0.0)).astype(BF16)
-        return 0
-
-    lax.fori_loop(0, 2, one_strand, 0)
-    role = chain(z)
-    kept[...] = ends[role]
-    given[...] = ends[1 - role]
+    scan_strand(1 - chain(z), act, weight, prm, heads, xs, maps, sizes, sums, starts, end, proj)
+
+
+def second_scan(act, weight, prm, heads, xs, maps, sizes, sums, starts, end, proj):
+    z, _, _, _, _, _ = place()
+    scan_strand(chain(z), act, weight, prm, heads, xs, maps, sizes, sums, starts, end, proj)
 
 
 def chain(z):
@@ -327,42 +333,40 @@
 
 
 def local_kernel(*refs):
-    xs, maps, sizes, sums, starts, _, local, carry = refs
+    scans, refs = (refs[:5], refs[5:10]), refs[11:]
+    local, carry, out_maps = refs
+    z, _, _, _, _, _ = place()
     causal = ones_at(iota2((GROUP, GROUP), 0) >= iota2((GROUP, GROUP), 1))
     left = iota2((GROUP, 128), 1) < HEADDIM
-
-    def one_strand(strand, _):
-        def one_group(g, before):
+    for strand, (xs, maps, sizes, sums, starts) in zip((1 - chain(z), chain(z)), scans):
+        out_maps[strand] = maps[:, STATE:]
+
+        def one_group(g, before, strand=strand, xs=xs, maps=maps, sizes=sizes, sums=sums, starts=starts):
             rows = pl.ds(pl.multiple_of(GROUP * g, GROUP), GROUP)
             part = pl.ds(pl.multiple_of(MINE * g, MINE), MINE)
-            size = sizes[strand, part, :]
-            cumulated = sums[strand, part, :]
+            size = sizes[part, :]
+            cumulated = sums[part, :]
             columns = jnp.concatenate([cumulated, jnp.zeros((GROUP - MINE, GROUP), F32)], axis=0).T
-            in_map = maps[strand, rows, :STATE]
-            out_map = maps[strand, rows, STATE:]
-            affinity = lax.dot_general(
-                out_map, in_map, (((1,), (1,)), ((), ())), preferred_element_type=F32
-            ) * causal
+            in_map = maps[rows, :STATE]
+            out_map = maps[rows, STATE:]
+            affinity = times_turned(out_map, in_map) * causal
             parts = []
             for pair in range(4):
                 mixes = []
                 for h in (2 * pair, 2 * pair + 1):
                     gap = jnp.minimum(columns[:, h : h + 1] - cumulated[h : h + 1, :], 0.0)
                     mixes.append((affinity * jnp.exp(gap) * size[h : h + 1, :]).astype(BF16))
-                x = xs[strand, rows, 128 * pair : 128 * pair + 128]
+                x = xs[rows, 128 * pair : 128 * pair + 128]
                 zero = jnp.zeros_like(x)
                 tall = jnp.concatenate([jnp.where(left, x, zero), jnp.where(left, zero, x)], axis=0)
                 parts.append(jnp.dot(jnp.concatenate(mixes, axis=1), tall, preferred_element_type=F32))
             within = jnp.concatenate(parts, axis=1)
             grown = spread_columns(jnp.exp(cumulated))
-            local[strand, rows, :] = within + jnp.dot(out_map, starts[strand, g], preferred_element_type=F32) * grown
+            local[strand, rows, :] = within + jnp.dot(out_map, starts[g], preferred_element_type=F32) * grown
             carry[strand, rows, :] = grown * spread_row(jnp.exp(before))
             return before + cumulated[:, GROUP - 1 :]
 
         lax.fori_loop(0, GROUPS, one_group, jnp.zeros((MINE, 1), F32))
-        return 0
-
-    lax.fori_loop(0, 2, one_strand, 0)
 
 
 def gate_kernel(act, *refs):
@@ -375,11 +379,11 @@
             units.append((unit, LATE * n, which * 4 + lax.rem(x - k + 4, 4)))
     for unit, first, f in units:
         lanes = pl.ds(pl.multiple_of(128 * f, 128), 128)
-        for j in range(MINE):
-            weight[64 * j : 64 * j + 64, lanes] = unit[first : first + 64, 128 * j : 128 * j + 128]
+        weight[:, lanes] = unit[first : first + OWN, :]
         rows = pl.ds(pl.multiple_of(64 * f, 64), 64)
-        for half in range(2):
-            out_weight[half, rows, :] = unit[first + 64 : first + 128, 512 * half : 512 * half + 512]
+        for j in range(8):
+            line = first + OWN + 64 * j
+            out_weight[j // 4, rows, 128 * (j % 4) : 128 * (j % 4) + 128] = unit[line : line + 64, :]
     for strand in range(2):
         half = 0.5 * times_turned(act[strand, HALO:, :], weight[...]).astype(BF16).astype(F32)
         gate[strand] = half + half * jnp.tanh(half)
@@ -398,7 +402,7 @@
     for strand, first in enumerate(half_rows(own)):
         for b in range(2):
             rows = pl.ds(pl.multiple_of(first + ROWS * b, ROWS), ROWS)
-            held = jnp.dot(maps[strand, rows, STATE:], entering[strand], preferred_element_type=F32)
+            held = jnp.dot(maps[strand, rows, :], entering[strand], preferred_element_type=F32)
             gated = (local[strand, rows, :] + held * carry[strand, rows, :]) * gate[strand, rows, :]
             squared = gated * gated
             folded = (squared[:, :128] + squared[:, 128:256]) + (squared[:, 256:384] + squared[:, 384:])
@@ -484,23 +488,16 @@
     return to
 
 
-def halo_step(same):
-    def to(z, yl, c, yh, x):
-        t = 2 * yl + c
-        if t == 3 and z < Z - 1:
-            return dict(z=z + 1, yl=1 if same else 0)
-        if t == 0 and z > 0:
-            return dict(z=z - 1, yl=0 if same else 1)
-        return None
-
-    return to
+def halo_step(z, yl, c, yh, x):
+    target = z + 1 if c else z - 1
+    return dict(z=target) if 0 <= target < Z else None
 
 
 def body(hidden, tokens, base_bias, in_weight, conv_weight, conv_bias, dt_bias, decay_rate, norm_gain, out_weight):
-    act, halo, ua, ua_other, ub, ub_other = call(
+    act, ua, ub, other = call(
         start_kernel,
         "start_kernel",
-        [shape(2 * ROWS, D), shape(HALO, D)] + [shape(UNIT, 128)] * 2 + [shape(LATE, D)] * 2,
+        [shape(2 * ROWS, D), shape(UNIT, 128), shape(LATE, 128), shape(UNIT + LATE, 128)],
         [ANY] * 5,
         tuple(
             pltpu.with_memory_space_constraint(value, pltpu.HBM)
@@ -517,32 +514,8 @@
         mb=16,
     )
     act_y = swap_y(act)
-    far = swap_diagonal(ua_other)
-    own_1, own_3 = along_x(ua, 1), along_x(ua, 3)
-    halo_a = move(halo, halo_step(True))
-    halo, ub_other, ua_late = call(
-        hold,
-        "hold",
-        [shape(HALO, D), shape(LATE, D), shape(UNIT, 128)],
-        [VMEM] * 4,
-        (halo, ub_other, ua, far),
-        mb=8,
-    )
-    own_2 = along_x(ua_late, 2)
-    far_1, far_3, far_2 = along_x(far, 1), along_x(far, 3), along_x(far, 2)
-    units = (ua, own_1, own_2, own_3, far, far_1, far_2, far_3)
-    halo_b = move(halo, halo_step(False))
-    ub_far = swap_diagonal(ub_other)
-    payload, late = call(
-        pack_core,
-        "pack_core",
-        [shape(PAYLOAD, D), shape(2 * LATE, D)],
-        [VMEM] * 14,
-        (act, act_y, halo_a, halo_b, ub, ub_far, *units),
-        mb=12,
-    )
-    swapped = swap_core(payload)
-    late = (late, *[along_x(late, k) for k in (1, 2, 3)])
+    both = swap_diagonal(other)
+    own_1, own_3, own_2 = along_x(ua, 1), along_x(ua, 3), along_x(ua, 2)
     prm, heads = call(
         pack_params,
         "pack_params",
@@ -552,27 +525,51 @@
         scratch=[pltpu.VMEM((8, E), F32)],
         mb=12,
     )
-    xs, maps, sizes, sums, starts, act, kept, given = call(
-        scan_kernel,
-        "scan_kernel",
-        [
-            shape(2, SPAN, OWN),
-            shape(2, SPAN, 2 * STATE),
-            shape(2, MINE * GROUPS, GROUP, dtype=F32),
-            shape(2, MINE * GROUPS, GROUP, dtype=F32),
-            shape(2, GROUPS, STATE, OWN),
-            shape(2, PAD, D),
-        ]
-        + [shape(STATE + HALO, OWN)] * 2,
-        [VMEM] * 15,
-        (act, act_y, halo_a, halo_b, swapped, *units, prm, heads),
-        scratch=[
-            pltpu.VMEM((WA, D), BF16),
-            pltpu.VMEM((PAD, WA), F32),
-            pltpu.VMEM((2, STATE + HALO, OWN), BF16),
-        ],
-        mb=24,
-        flops=2 * 1056 * D * WA,
+    far = call(split_far, "split_far", shape(UNIT, 128), [VMEM] * 2, (both, prm), mb=8)
+    far_1, far_3 = along_x(far, 1), along_x(far, 3)
+    halo, far_late = call(
+        choose_halo, "choose_halo", [shape(HALO, D), shape(UNIT, 128)], [VMEM] * 3, (act, act_y, far), mb=8
+    )
+    halo = move(halo, halo_step)
+    far_2 = along_x(far_late, 2)
+    units = (ua, own_1, own_2, own_3, far, far_1, far_2, far_3)
+    payload, late = call(
+        pack_core,
+        "pack_core",
+        [shape(PAYLOAD, D), shape(2 * LATE, 128)],
+        [VMEM] * 13,
+        (act, act_y, halo, ub, both, *units),
+        mb=12,
+    )
+    swapped = swap_core(payload)
+    late = (late, *[along_x(late, k) for k in (1, 2, 3)])
+    scanned = [
+        shape(SPAN, OWN),
+        shape(SPAN, 2 * STATE),
+        shape(MINE * GROUPS, GROUP, dtype=F32),
+        shape(MINE * GROUPS, GROUP, dtype=F32),
+        shape(GROUPS, STATE, OWN),
+    ]
+    *first, act, weight, given = call(
+        first_scan,
+        "first_scan",
+        scanned + [shape(2, PAD, D), shape(WA, D), shape(STATE + HALO, OWN)],
+        [VMEM] * 14,
+        (act, act_y, halo, swapped, *units, prm, heads),
+        scratch=[pltpu.VMEM((PAD, WA), F32)],
+        mb=20,
+        flops=1056 * D * WA,
+        bytes_accessed=8 << 20,
+    )
+    *second, kept = call(
+        second_scan,
+        "second_scan",
+        scanned + [shape(STATE + HALO, OWN)],
+        [VMEM] * 4,
+        (act, weight, prm, heads),
+        scratch=[pltpu.VMEM((PAD, WA), F32)],
+        mb=20,
+        flops=16 * 1056 * D * WA,
         bytes_accessed=8 << 20,
     )
     mate = move(given, lambda z, yl, c, yh, x: dict(z=z ^ 1))
@@ -580,12 +577,12 @@
     earlier = [move(pair, pair_step(m)) for m in (1, 2, 3)]
     entered = call(earlier_pairs, "earlier_pairs", shape(STATE, OWN), [VMEM] * 3, earlier, mb=8)
     mate_entered = move(entered, lambda z, yl, c, yh, x: dict(z=z ^ 1))
-    local, carry = call(
+    local, carry, maps = call(
         local_kernel,
         "local_kernel",
-        [shape(2, SPAN, OWN, dtype=F32)] * 2,
-        [VMEM] * 6,
-        (xs, maps, sizes, sums, starts, pair),
+        [shape(2, SPAN, OWN, dtype=F32)] * 2 + [shape(2, SPAN, STATE)],
+        [VMEM] * 11,
+        (*first, *second, pair),
         mb=16,
         flops=8 * 1024 * D * OWN,
         bytes_accessed=16 << 20,

time: 102 us -> 89.7 us (0.88)
  waiting for transfers between devices: 43.5 us -> 37 us
  starting transfers between devices: 37.3 us -> 31 us
    ppermute x23 -> x21, waiting for transfers between devices: 43.5 us -> 37 us  [move(): return lax.ppermute(value, ('seq', 'fsdp'), pairs)]
    ppermute x23 -> x21, starting transfers between devices: 37.3 us -> 31 us  [move(): return lax.ppermute(value, ('seq', 'fsdp'), pairs)]
    pallas_call x13 -> x15, Pallas kernels: 21 us -> 21.2 us  [call(): pl.pallas_call(kernel, out_shape=outs, in_specs=ins, out_specs=jax.tree.m...]
  transfers between devices with their start and end apart: 23 -> 21, of which waited for: 12 -> 10; matrix products, arithmetic and copies ran while one was open for 0% -> 0% of each run, Pallas kernels for 16% -> 19%
where the time goes in v4:
time: 89.7 us; the launch traced here: 89.5 us
  waiting for transfers between devices  37 us (41%)
  starting transfers between devices  31 us (35%)
  Pallas kernels  21.2 us (24%)
    ppermute x21, waiting for transfers between devices, move(): return lax.ppermute(value, ('seq', 'fsdp'), pairs)  37 us
    ppermute x21, starting transfers between devices, move(): return lax.ppermute(value, ('seq', 'fsdp'), pairs)  31 us
    pallas_call x15, Pallas kernels, call(): pl.pallas_call(kernel, out_shape=outs, in_specs=ins, out_specs=jax.tree.m...  21.2 us
  transfers between devices with their start and end apart: 21, of which 10 were waited for; matrix products, arithmetic and copies ran while one was open for 0% of the time, Pallas kernels for 19%

profile of v4, /device:TPU:1, one launch (start us, length us, event | category | flops | bytes accessed | tf_op | source)
XLA Modules:
  0.0 89.5 jit_solution(4841503872837116337)
XLA Ops:
  0.0 1.9 %start_kernel.1 = (bf16[256,1024]{1,0:T(8,128)(2,1)S(1)}, bf16[672,128]{1,0:T(8,128)(2,1)S(1)}, bf16[1024,128]{1,0:T(8,128)(2,1)S(1)}, bf16[1696,128]{1,0:T(8,128)(2,1)S(1)}) custom-call(bf16[128,2048]{1,0:T(8,128)(2,1)} %bitcast.10, s32[1,128]{1,0:T(1,128)} %tokens.1, bf16[5,2048]{1,0:T(8,128)(2,1)} %base_bias.1, bf16[4384,128]{1,0:T(8,128)(2,1)} %bitcast.9, ...), custom_call_target="tpu_custom_call" | custom-call | tf_op jit(solution)/shard_map/start_kernel/pallas_call | solution.py:62
  2.0 2.2 %collective-permute-start = (bf16[256,1024]{1,0:T(8,128)(2,1)S(1)}, bf16[256,1024]{1,0:T(8,128)(2,1)S(1)}, u32[]{:S(2)}, u32[]{:S(2)}) collective-permute-start(bf16[256,1024]{1,0:T(8,128)(2,1)S(1)} %get-tuple-element.39.act.refs_0_), channel_id=1, source_target_pairs={{0,16},{1,17},{2,18},{3,19},{4,20},{5,21},{6,22},{7,23},{8,24},{9,... | collective-permute-start | bytes 1572872 | tf_op jit(solution)/shard_map/ppermute | solution.py:54
  4.2 1.9 %collective-permute-start.1 = (bf16[1696,128]{1,0:T(8,128)(2,1)S(1)}, bf16[1696,128]{1,0:T(8,128)(2,1)S(1)}, u32[]{:S(2)}, u32[]{:S(2)}) collective-permute-start(bf16[1696,128]{1,0:T(8,128)(2,1)S(1)} %get-tuple-element.40), channel_id=1, source_target_pairs={{0,20},{1,21},{2,22},{3,23},{4,16},{5,17},{6,18},{7,19},{8,28},{9,... | collective-permute-start | bytes 1302536 | tf_op jit(solution)/shard_map/ppermute | solution.py:54
  6.1 1.2 %collective-permute-start.3 = (bf16[672,128]{1,0:T(8,128)(2,1)S(1)}, bf16[672,128]{1,0:T(8,128)(2,1)S(1)}, u32[]{:S(2)}, u32[]{:S(2)}) collective-permute-start(bf16[672,128]{1,0:T(8,128)(2,1)S(1)} %get-tuple-element.44.refs_5_.refs_4_), channel_id=1, source_target_pairs={{0,1},{1,2},{2,3},{3,0},{4,5},{5,6},{6,7},{7,4},{8,9},{9,10},{10,1... | collective-permute-start | bytes 516104 | tf_op jit(solution)/shard_map/ppermute | solution.py:54
  7.3 2.5 %collective-permute-start.4 = (bf16[672,128]{1,0:T(8,128)(2,1)S(1)}, bf16[672,128]{1,0:T(8,128)(2,1)S(1)}, u32[]{:S(2)}, u32[]{:S(2)}) collective-permute-start(bf16[672,128]{1,0:T(8,128)(2,1)S(1)} %get-tuple-element.44.refs_5_.refs_4_), channel_id=1, source_target_pairs={{0,2},{1,3},{2,0},{3,1},{4,6},{5,7},{6,4},{7,5},{8,10},{9,11},{10,... | collective-permute-start | bytes 516104 | tf_op jit(solution)/shard_map/ppermute | solution.py:54
  9.7 1.1 %collective-permute-start.5 = (bf16[672,128]{1,0:T(8,128)(2,1)S(1)}, bf16[672,128]{1,0:T(8,128)(2,1)S(1)}, u32[]{:S(2)}, u32[]{:S(2)}) collective-permute-start(bf16[672,128]{1,0:T(8,128)(2,1)S(1)} %get-tuple-element.44.refs_5_.refs_4_), channel_id=1, source_target_pairs={{0,3},{1,0},{2,1},{3,2},{4,7},{5,4},{6,5},{7,6},{8,11},{9,8},{10,9... | collective-permute-start | bytes 516104 | tf_op jit(solution)/shard_map/ppermute | solution.py:54
  10.9 0.6 pack_params.1
  11.5 4.2 %collective-permute-done.1.both.refs_4_ = bf16[1696,128]{1,0:T(8,128)(2,1)S(1)} collective-permute-done((bf16[1696,128]{1,0:T(8,128)(2,1)S(1)}, bf16[1696,128]{1,0:T(8,128)(2,1)S(1)}, u32[]{:S(2)}, u32[]{:S(2)}) %collective-permute-start.1) | collective-permute-done | bytes 434208 | tf_op jit(solution)/shard_map/ppermute | solution.py:54
  15.7 1.6 %collective-permute-start.6 = (bf16[672,128]{1,0:T(8,128)(2,1)S(1)}, bf16[672,128]{1,0:T(8,128)(2,1)S(1)}, u32[]{:S(2)}, u32[]{:S(2)}) collective-permute-start(bf16[672,128]{1,0:T(8,128)(2,1)S(1)} %split_far.1.far.refs_9_.refs_8_), channel_id=1, source_target_pairs={{0,1},{1,2},{2,3},{3,0},{4,5},{5,6},{6,7},{7,4},{8,9},{9,10},{10,1... | collective-permute-start | bytes 516104 | tf_op jit(solution)/shard_map/ppermute | solution.py:54
  17.2 0.0 collective-permute-done.act_y.refs_1_
  17.2 1.4 %collective-permute-start.8 = (bf16[672,128]{1,0:T(8,128)(2,1)S(1)}, bf16[672,128]{1,0:T(8,128)(2,1)S(1)}, u32[]{:S(2)}, u32[]{:S(2)}) collective-permute-start(bf16[672,128]{1,0:T(8,128)(2,1)S(1)} %split_far.1.far.refs_9_.refs_8_), channel_id=1, source_target_pairs={{0,3},{1,0},{2,1},{3,2},{4,7},{5,4},{6,5},{7,6},{8,11},{9,8},{10,9... | collective-permute-start | bytes 516104 | tf_op jit(solution)/shard_map/ppermute | solution.py:54
  18.6 1.7 %collective-permute-start.7 = (bf16[672,128]{1,0:T(8,128)(2,1)S(1)}, bf16[672,128]{1,0:T(8,128)(2,1)S(1)}, u32[]{:S(2)}, u32[]{:S(2)}) collective-permute-start(bf16[672,128]{1,0:T(8,128)(2,1)S(1)} %get-tuple-element.45), channel_id=1, source_target_pairs={{0,2},{1,3},{2,0},{3,1},{4,6},{5,7},{6,4},{7,5},{8,10},{9,11},{10,... | collective-permute-start | bytes 516104 | tf_op jit(solution)/shard_map/ppermute | solution.py:54
  20.3 0.0 collective-permute-done.4.refs_7_.refs_6_
  20.3 3.6 %collective-permute-start.2 = (bf16[16,1024]{1,0:T(8,128)(2,1)S(1)}, bf16[16,1024]{1,0:T(8,128)(2,1)S(1)}, u32[]{:S(2)}, u32[]{:S(2)}) collective-permute-start(bf16[16,1024]{1,0:T(8,128)(2,1)S(1)} %get-tuple-element.42), channel_id=1, source_target_pairs={{8,40},{9,41},{10,42},{11,43},{12,44},{13,45},{14,46},{15,47},{24,... | collective-permute-start | bytes 98312 | tf_op jit(solution)/shard_map/ppermute | solution.py:54
  23.9 1.0 %collective-permute-done.2.refs_2_ = bf16[16,1024]{1,0:T(8,128)(2,1)S(1)} collective-permute-done((bf16[16,1024]{1,0:T(8,128)(2,1)S(1)}, bf16[16,1024]{1,0:T(8,128)(2,1)S(1)}, u32[]{:S(2)}, u32[]{:S(2)}) %collective-permute-start.2) | collective-permute-done | bytes 32800 | tf_op jit(solution)/shard_map/ppermute | solution.py:54
  24.9 1.1 %collective-permute-done.7.refs_11_.refs_10_ = bf16[672,128]{1,0:T(8,128)(2,1)S(1)} collective-permute-done((bf16[672,128]{1,0:T(8,128)(2,1)S(1)}, bf16[672,128]{1,0:T(8,128)(2,1)S(1)}, u32[]{:S(2)}, u32[]{:S(2)}) %collective-permute-start.7) | collective-permute-done | bytes 172064 | tf_op jit(solution)/shard_map/ppermute | solution.py:54
  26.0 0.2 pack_core.1
  26.2 2.9 %collective-permute-start.9 = (bf16[656,1024]{1,0:T(8,128)(2,1)S(1)}, bf16[656,1024]{1,0:T(8,128)(2,1)S(1)}, u32[]{:S(2)}, u32[]{:S(2)}) collective-permute-start(bf16[656,1024]{1,0:T(8,128)(2,1)S(1)} %get-tuple-element.46), channel_id=1, source_target_pairs={{0,8},{1,9},{2,10},{3,11},{4,12},{5,13},{6,14},{7,15},{8,0},{9,1},... | collective-permute-start | bytes 4030472 | tf_op jit(solution)/shard_map/ppermute | solution.py:54
  29.1 0.7 collective-permute-start.10
  29.8 2.0 %collective-permute-start.11 = (bf16[2048,128]{1,0:T(8,128)(2,1)S(1)}, bf16[2048,128]{1,0:T(8,128)(2,1)S(1)}, u32[]{:S(2)}, u32[]{:S(2)}) collective-permute-start(bf16[2048,128]{1,0:T(8,128)(2,1)S(1)} %get-tuple-element.49.refs_0_), channel_id=1, source_target_pairs={{0,2},{1,3},{2,0},{3,1},{4,6},{5,7},{6,4},{7,5},{8,10},{9,11},{10,... | collective-permute-start | bytes 1572872 | tf_op jit(solution)/shard_map/ppermute | solution.py:54
  31.9 0.8 collective-permute-start.12
  32.7 4.3 %first_scan.1 = (bf16[512,512]{1,0:T(8,128)(2,1)S(1)}, bf16[512,256]{1,0:T(8,128)(2,1)S(1)}, f32[32,128]{1,0:T(8,128)S(1)}, f32[32,128]{1,0:T(8,128)S(1)}, bf16[...) custom-call(bf16[256,1024]{1,0:T(8,128)(2,1)S(1)} %get-tuple-element, ...), custom_call_target="tpu_custom_call" | custom-call | flops 968884224 | bytes 8388608 | tf_op jit(solution)/shard_map/first_scan/pallas_call | solution.py:62
  36.9 1.7 %collective-permute-start.13 = (bf16[144,512]{1,0:T(8,128)(2,1)S(1)}, bf16[144,512]{1,0:T(8,128)(2,1)S(1)}, u32[]{:S(2)}, u32[]{:S(2)}) collective-permute-start(bf16[144,512]{1,0:T(8,128)(2,1)S(1)} %get-tuple-element.51), channel_id=1, source_target_pairs={{0,32},{1,33},{2,34},{3,35},{4,36},{5,37},{6,38},{7,39},{8,40},{9,... | collective-permute-start | bytes 442376 | tf_op jit(solution)/shard_map/ppermute | solution.py:54
  38.7 3.6 %second_scan.1 = (bf16[512,512]{1,0:T(8,128)(2,1)S(1)}, bf16[512,256]{1,0:T(8,128)(2,1)S(1)}, f32[32,128]{1,0:T(8,128)S(1)}, f32[32,128]{1,0:T(8,128)S(1)}, bf16...) custom-call(bf16[2,528,1024]{2,1,0:T(8,128)(2,1)S(1)} %get-tuple-element.48.act, ...), custom_call_target="tpu_custom_call" | custom-call | flops 15502147584 | bytes 8388608 | tf_op jit(solution)/shard_map/second_scan/pallas_call | solution.py:62
  42.3 0.0 collective-permute-done.13.mate.refs_0_
  42.3 0.1 pair_state.1.refs_10_
  42.4 1.3 %collective-permute-start.14 = (bf16[144,512]{1,0:T(8,128)(2,1)S(1)}, bf16[144,512]{1,0:T(8,128)(2,1)S(1)}, u32[]{:S(2)}, u32[]{:S(2)}) collective-permute-start(bf16[144,512]{1,0:T(8,128)(2,1)S(1)} %pair_state.1.refs_10_), channel_id=1, source_target_pairs={{32,96},{33,97},{34,98},{35,99},{36,100},{37,101},{38,102},{39,103... | collective-permute-start | bytes 442376 | tf_op jit(solution)/shard_map/ppermute | solution.py:54
  43.7 1.3 %collective-permute-start.15 = (bf16[144,512]{1,0:T(8,128)(2,1)S(1)}, bf16[144,512]{1,0:T(8,128)(2,1)S(1)}, u32[]{:S(2)}, u32[]{:S(2)}) collective-permute-start(bf16[144,512]{1,0:T(8,128)(2,1)S(1)} %pair_state.1.refs_10_), channel_id=1, source_target_pairs={{32,160},{33,161},{34,162},{35,163},{36,164},{37,165},{38,166},{39... | collective-permute-start | bytes 442376 | tf_op jit(solution)/shard_map/ppermute | solution.py:54
  45.0 1.3 %collective-permute-start.16 = (bf16[144,512]{1,0:T(8,128)(2,1)S(1)}, bf16[144,512]{1,0:T(8,128)(2,1)S(1)}, u32[]{:S(2)}, u32[]{:S(2)}) collective-permute-start(bf16[144,512]{1,0:T(8,128)(2,1)S(1)} %pair_state.1.refs_10_), channel_id=1, source_target_pairs={{32,224},{33,225},{34,226},{35,227},{36,228},{37,229},{38,230},{39... | collective-permute-start | bytes 442376 | tf_op jit(solution)/shard_map/ppermute | solution.py:54
  46.3 8.8 %collective-permute-done.11.refs_2_ = bf16[2048,128]{1,0:T(8,128)(2,1)S(1)} collective-permute-done((bf16[2048,128]{1,0:T(8,128)(2,1)S(1)}, bf16[2048,128]{1,0:T(8,128)(2,1)S(1)}, u32[]{:S(2)}, u32[]{:S(2)}) %collective-permute-start.11) | collective-permute-done | bytes 524320 | tf_op jit(solution)/shard_map/ppermute | solution.py:54
  55.1 0.3 collective-permute-done.12.refs_3_
  55.4 1.9 %gate_kernel.1 = (f32[2,512,512]{2,1,0:T(8,128)S(1)}, bf16[2,512,512]{2,1,0:T(8,128)(2,1)S(1)}) custom-call(bf16[2,528,1024]{2,1,0:T(8,128)(2,1)S(1)} %get-tuple-element.48.act, bf16[2048,128]{1,0:T(8,128)(2,1)S(1)} %get-tuple-element.49.refs_0_, bf16[2048,128]{1,0:T(8,128)(2,1)S(1)} %collective-permute-done.10.refs_1_, ...), custom_call_target="tpu_custom_call" | custom-call | flops 1073741824 | bytes 8388608 | tf_op jit(solution)/shard_map/gate_kernel/pallas_call | solution.py:62
  57.3 0.0 collective-permute-done.14.refs_0_
  57.3 3.0 %collective-permute-done.15.refs_1_ = bf16[144,512]{1,0:T(8,128)(2,1)S(1)} collective-permute-done((bf16[144,512]{1,0:T(8,128)(2,1)S(1)}, bf16[144,512]{1,0:T(8,128)(2,1)S(1)}, u32[]{:S(2)}, u32[]{:S(2)}) %collective-permute-start.15) | collective-permute-done | bytes 147488 | tf_op jit(solution)/shard_map/ppermute | solution.py:54
  60.4 4.7 %collective-permute-done.16.refs_2_ = bf16[144,512]{1,0:T(8,128)(2,1)S(1)} collective-permute-done((bf16[144,512]{1,0:T(8,128)(2,1)S(1)}, bf16[144,512]{1,0:T(8,128)(2,1)S(1)}, u32[]{:S(2)}, u32[]{:S(2)}) %collective-permute-start.16) | collective-permute-done | bytes 147488 | tf_op jit(solution)/shard_map/ppermute | solution.py:54
  65.1 0.1 earlier_pairs.1.refs_1_
  65.1 0.1 collective-permute-start.17
  65.2 5.0 %local_kernel.1 = (f32[2,512,512]{2,1,0:T(8,128)S(1)}, f32[2,512,512]{2,1,0:T(8,128)S(1)}, bf16[2,512,128]{2,1,0:T(8,128)(2,1)S(1)}) custom-call(bf16[512,512]{1,0:T(8,128)(2,1)S(1)} %get-tuple-element.54.refs_0_, bf16[512,256]{1,0:T(8,128)(2,1)S(1)} %get-tuple-element.55.refs_1_, f32[32,128]{1,0:T(8,128)S(1)} %get-tuple-element.56.refs_2_, ...), custom_call_target="tpu_custom_call" | custom-call | flops 4294967296 | bytes 16777216 | tf_op jit(solution)/shard_map/local_kernel/pallas_call | solution.py:62
  70.2 1.1 %first_half.1 = (bf16[2,128,512]{2,1,0:T(8,128)(2,1)S(1)}, bf16[272,1024]{1,0:T(8,128)(2,1)S(1)}, bf16[272,1024]{1,0:T(8,128)(2,1)S(1)}) custom-call(bf16[144,512]{1,0:T(8,128)(2,1)S(1)} %collective-permute-done.13.mate.refs_0_, bf16[128,512]{1,0:T(8,128)(2,1)S(1)} %earlier_pairs.1.refs_1_, bf16[128,512]{1,0:T(8,128)(2,1)S(1)} %collective-permute-done.17.refs_2_, ...), custom_call_target="tpu_custom_call" | custom-call | flops 536870912 | bytes 4194304 | tf_op jit(solution)/shard_map/first_half/pallas_call | solution.py:62
  71.4 1.2 %collective-permute-start.19 = (bf16[272,1024]{1,0:T(8,128)(2,1)S(1)}, bf16[272,1024]{1,0:T(8,128)(2,1)S(1)}, u32[]{:S(2)}, u32[]{:S(2)}) collective-permute-start(bf16[272,1024]{1,0:T(8,128)(2,1)S(1)} %get-tuple-element.72), channel_id=1, source_target_pairs={{0,8},{1,9},{2,10},{3,11},{4,12},{5,13},{6,14},{7,15},{8,0},{9,1},... | collective-permute-start | bytes 1671176 | tf_op jit(solution)/shard_map/ppermute | solution.py:54
  72.6 1.1 %second_half.1 = (bf16[272,1024]{1,0:T(8,128)(2,1)S(1)}, bf16[272,1024]{1,0:T(8,128)(2,1)S(1)}) custom-call(bf16[2,512,512]{2,1,0:T(8,128)(2,1)S(1)} %get-tuple-element.50.refs_3_.weight, bf16[2,128,512]{2,1,0:T(8,128)(2,1)S(1)} %get-tuple-element.68.entering, f32[8,768]{1,0:T(8,128)S(1)} %get-tuple-element.41.prm.refs_12_.refs_4_, ...), custom_call_target="tpu_custom_call" | custom-call | flops 536870912 | bytes 4194304 | tf_op jit(solution)/shard_map/second_half/pallas_call | solution.py:62
  73.6 0.1 collective-permute-start.18
  73.7 0.4 collective-permute-done.19.came
  74.2 0.1 pair_sum.1
  74.3 0.4 collective-permute-start.20
  74.7 0.9 %collective-permute-done.18.came = bf16[272,1024]{1,0:T(8,128)(2,1)S(1)} collective-permute-done((bf16[272,1024]{1,0:T(8,128)(2,1)S(1)}, bf16[272,1024]{1,0:T(8,128)(2,1)S(1)}, u32[]{:S(2)}, u32[]{:S(2)}) %collective-permute-start.18) | collective-permute-done | bytes 557088 | tf_op jit(solution)/shard_map/ppermute | solution.py:54
  75.7 12.5 %collective-permute-done.20.far = bf16[272,1024]{1,0:T(8,128)(2,1)S(1)} collective-permute-done((bf16[272,1024]{1,0:T(8,128)(2,1)S(1)}, bf16[272,1024]{1,0:T(8,128)(2,1)S(1)}, u32[]{:S(2)}, u32[]{:S(2)}) %collective-permute-start.20) | collective-permute-done | bytes 557088 | tf_op jit(solution)/shard_map/ppermute | solution.py:54
  88.2 1.3 %last_kernel.1 = bf16[128,2048]{1,0:T(8,128)(2,1)} custom-call(bf16[272,1024]{1,0:T(8,128)(2,1)S(1)} %get-tuple-element.69.second.mine, bf16[272,1024]{1,0:T(8,128)(2,1)S(1)} %collective-permute-done.18.came, bf16[272,1024]{1,0:T(8,128)(2,1)S(1)} %collective-permute-done.20.far), custom_call_target="tpu_custom_call" | custom-call | tf_op jit(solution)/shard_map/last_kernel/pallas_call | solution.py:62
  (20 shorter events, 0.1 us)
Async XLA Ops:
  0.0 10.9 %copy-start.4 = (f32[2304]{0:T(1024)S(1)}, f32[2304]{0:T(1024)}, u32[]{:S(2)}) copy-start(f32[2304]{0:T(1024)} %param.15) | copy-start | bytes 27652
  0.0 10.9 %copy-start = (f32[4,2304]{1,0:T(4,128)S(1)}, f32[4,2304]{1,0:T(4,128)}, u32[]{:S(2)}) copy-start(f32[4,2304]{1,0:T(4,128)} %cw.1) | copy-start | bytes 110596
  0.0 10.9 %copy-start.2 = (f32[32]{0:T(128)S(1)}, f32[32]{0:T(128)}, u32[]{:S(2)}) copy-start(f32[32]{0:T(128)} %param.16) | copy-start | bytes 388
  0.0 10.9 %copy-start.3 = (f32[32]{0:T(128)S(1)}, f32[32]{0:T(128)}, u32[]{:S(2)}) copy-start(f32[32]{0:T(128)} %param.17) | copy-start | bytes 388
  0.0 10.9 %copy-start.1 = (f32[2048]{0:T(1024)S(1)}, f32[2048]{0:T(1024)}, u32[]{:S(2)}) copy-start(f32[2048]{0:T(1024)} %param.18) | copy-start | bytes 24580
  2.0 15.3 %collective-permute-start = (bf16[256,1024]{1,0:T(8,128)(2,1)S(1)}, bf16[256,1024]{1,0:T(8,128)(2,1)S(1)}, u32[]{:S(2)}, u32[]{:S(2)}) collective-permute-start(bf16[256,1024]{1,0:T(8,128)(2,1)S(1)} %get-tuple-element.39.act.refs_0_), channel_id=1, source_target_pairs={{0,16},{1,17},{2,18},{3,19},{4,20},{5,21},{6,22},{7,23},{8,24},{9,... | collective-permute-start | bytes 1572872 | tf_op jit(solution)/shard_map/ppermute | solution.py:54
  4.2 11.5 %collective-permute-start.1 = (bf16[1696,128]{1,0:T(8,128)(2,1)S(1)}, bf16[1696,128]{1,0:T(8,128)(2,1)S(1)}, u32[]{:S(2)}, u32[]{:S(2)}) collective-permute-start(bf16[1696,128]{1,0:T(8,128)(2,1)S(1)} %get-tuple-element.40), channel_id=1, source_target_pairs={{0,20},{1,21},{2,22},{3,23},{4,16},{5,17},{6,18},{7,19},{8,28},{9,... | collective-permute-start | bytes 1302536 | tf_op jit(solution)/shard_map/ppermute | solution.py:54
  6.1 12.6 %collective-permute-start.3 = (bf16[672,128]{1,0:T(8,128)(2,1)S(1)}, bf16[672,128]{1,0:T(8,128)(2,1)S(1)}, u32[]{:S(2)}, u32[]{:S(2)}) collective-permute-start(bf16[672,128]{1,0:T(8,128)(2,1)S(1)} %get-tuple-element.44.refs_5_.refs_4_), channel_id=1, source_target_pairs={{0,1},{1,2},{2,3},{3,0},{4,5},{5,6},{6,7},{7,4},{8,9},{9,10},{10,1... | collective-permute-start | bytes 516104 | tf_op jit(solution)/shard_map/ppermute | solution.py:54
  7.3 13.1 %collective-permute-start.4 = (bf16[672,128]{1,0:T(8,128)(2,1)S(1)}, bf16[672,128]{1,0:T(8,128)(2,1)S(1)}, u32[]{:S(2)}, u32[]{:S(2)}) collective-permute-start(bf16[672,128]{1,0:T(8,128)(2,1)S(1)} %get-tuple-element.44.refs_5_.refs_4_), channel_id=1, source_target_pairs={{0,2},{1,3},{2,0},{3,1},{4,6},{5,7},{6,4},{7,5},{8,10},{9,11},{10,... | collective-permute-start | bytes 516104 | tf_op jit(solution)/shard_map/ppermute | solution.py:54
  9.7 14.2 %collective-permute-start.5 = (bf16[672,128]{1,0:T(8,128)(2,1)S(1)}, bf16[672,128]{1,0:T(8,128)(2,1)S(1)}, u32[]{:S(2)}, u32[]{:S(2)}) collective-permute-start(bf16[672,128]{1,0:T(8,128)(2,1)S(1)} %get-tuple-element.44.refs_5_.refs_4_), channel_id=1, source_target_pairs={{0,3},{1,0},{2,1},{3,2},{4,7},{5,4},{6,5},{7,6},{8,11},{9,8},{10,9... | collective-permute-start | bytes 516104 | tf_op jit(solution)/shard_map/ppermute | solution.py:54
  15.7 9.2 %collective-permute-start.6 = (bf16[672,128]{1,0:T(8,128)(2,1)S(1)}, bf16[672,128]{1,0:T(8,128)(2,1)S(1)}, u32[]{:S(2)}, u32[]{:S(2)}) collective-permute-start(bf16[672,128]{1,0:T(8,128)(2,1)S(1)} %split_far.1.far.refs_9_.refs_8_), channel_id=1, source_target_pairs={{0,1},{1,2},{2,3},{3,0},{4,5},{5,6},{6,7},{7,4},{8,9},{9,10},{10,1... | collective-permute-start | bytes 516104 | tf_op jit(solution)/shard_map/ppermute | solution.py:54
  17.2 7.7 %collective-permute-start.8 = (bf16[672,128]{1,0:T(8,128)(2,1)S(1)}, bf16[672,128]{1,0:T(8,128)(2,1)S(1)}, u32[]{:S(2)}, u32[]{:S(2)}) collective-permute-start(bf16[672,128]{1,0:T(8,128)(2,1)S(1)} %split_far.1.far.refs_9_.refs_8_), channel_id=1, source_target_pairs={{0,3},{1,0},{2,1},{3,2},{4,7},{5,4},{6,5},{7,6},{8,11},{9,8},{10,9... | collective-permute-start | bytes 516104 | tf_op jit(solution)/shard_map/ppermute | solution.py:54
  18.6 7.4 %collective-permute-start.7 = (bf16[672,128]{1,0:T(8,128)(2,1)S(1)}, bf16[672,128]{1,0:T(8,128)(2,1)S(1)}, u32[]{:S(2)}, u32[]{:S(2)}) collective-permute-start(bf16[672,128]{1,0:T(8,128)(2,1)S(1)} %get-tuple-element.45), channel_id=1, source_target_pairs={{0,2},{1,3},{2,0},{3,1},{4,6},{5,7},{6,4},{7,5},{8,10},{9,11},{10,... | collective-permute-start | bytes 516104 | tf_op jit(solution)/shard_map/ppermute | solution.py:54
  20.3 4.6 %collective-permute-start.2 = (bf16[16,1024]{1,0:T(8,128)(2,1)S(1)}, bf16[16,1024]{1,0:T(8,128)(2,1)S(1)}, u32[]{:S(2)}, u32[]{:S(2)}) collective-permute-start(bf16[16,1024]{1,0:T(8,128)(2,1)S(1)} %get-tuple-element.42), channel_id=1, source_target_pairs={{8,40},{9,41},{10,42},{11,43},{12,44},{13,45},{14,46},{15,47},{24,... | collective-permute-start | bytes 98312 | tf_op jit(solution)/shard_map/ppermute | solution.py:54
  26.2 6.5 %collective-permute-start.9 = (bf16[656,1024]{1,0:T(8,128)(2,1)S(1)}, bf16[656,1024]{1,0:T(8,128)(2,1)S(1)}, u32[]{:S(2)}, u32[]{:S(2)}) collective-permute-start(bf16[656,1024]{1,0:T(8,128)(2,1)S(1)} %get-tuple-element.46), channel_id=1, source_target_pairs={{0,8},{1,9},{2,10},{3,11},{4,12},{5,13},{6,14},{7,15},{8,0},{9,1},... | collective-permute-start | bytes 4030472 | tf_op jit(solution)/shard_map/ppermute | solution.py:54
  29.1 15.8 %collective-permute-start.10 = (bf16[2048,128]{1,0:T(8,128)(2,1)S(1)}, bf16[2048,128]{1,0:T(8,128)(2,1)S(1)}, u32[]{:S(2)}, u32[]{:S(2)}) collective-permute-start(bf16[2048,128]{1,0:T(8,128)(2,1)S(1)} %get-tuple-element.49.refs_0_), channel_id=1, source_target_pairs={{0,1},{1,2},{2,3},{3,0},{4,5},{5,6},{6,7},{7,4},{8,9},{9,10},{10,1... | collective-permute-start | bytes 1572872 | tf_op jit(solution)/shard_map/ppermute | solution.py:54
  29.8 25.3 %collective-permute-start.11 = (bf16[2048,128]{1,0:T(8,128)(2,1)S(1)}, bf16[2048,128]{1,0:T(8,128)(2,1)S(1)}, u32[]{:S(2)}, u32[]{:S(2)}) collective-permute-start(bf16[2048,128]{1,0:T(8,128)(2,1)S(1)} %get-tuple-element.49.refs_0_), channel_id=1, source_target_pairs={{0,2},{1,3},{2,0},{3,1},{4,6},{5,7},{6,4},{7,5},{8,10},{9,11},{10,... | collective-permute-start | bytes 1572872 | tf_op jit(solution)/shard_map/ppermute | solution.py:54
  31.9 23.5 %collective-permute-start.12 = (bf16[2048,128]{1,0:T(8,128)(2,1)S(1)}, bf16[2048,128]{1,0:T(8,128)(2,1)S(1)}, u32[]{:S(2)}, u32[]{:S(2)}) collective-permute-start(bf16[2048,128]{1,0:T(8,128)(2,1)S(1)} %get-tuple-element.49.refs_0_), channel_id=1, source_target_pairs={{0,3},{1,0},{2,1},{3,2},{4,7},{5,4},{6,5},{7,6},{8,11},{9,8},{10,9... | collective-permute-start | bytes 1572872 | tf_op jit(solution)/shard_map/ppermute | solution.py:54
  36.9 5.4 %collective-permute-start.13 = (bf16[144,512]{1,0:T(8,128)(2,1)S(1)}, bf16[144,512]{1,0:T(8,128)(2,1)S(1)}, u32[]{:S(2)}, u32[]{:S(2)}) collective-permute-start(bf16[144,512]{1,0:T(8,128)(2,1)S(1)} %get-tuple-element.51), channel_id=1, source_target_pairs={{0,32},{1,33},{2,34},{3,35},{4,36},{5,37},{6,38},{7,39},{8,40},{9,... | collective-permute-start | bytes 442376 | tf_op jit(solution)/shard_map/ppermute | solution.py:54
  42.4 15.0 %collective-permute-start.14 = (bf16[144,512]{1,0:T(8,128)(2,1)S(1)}, bf16[144,512]{1,0:T(8,128)(2,1)S(1)}, u32[]{:S(2)}, u32[]{:S(2)}) collective-permute-start(bf16[144,512]{1,0:T(8,128)(2,1)S(1)} %pair_state.1.refs_10_), channel_id=1, source_target_pairs={{32,96},{33,97},{34,98},{35,99},{36,100},{37,101},{38,102},{39,103... | collective-permute-start | bytes 442376 | tf_op jit(solution)/shard_map/ppermute | solution.py:54
  43.7 16.7 %collective-permute-start.15 = (bf16[144,512]{1,0:T(8,128)(2,1)S(1)}, bf16[144,512]{1,0:T(8,128)(2,1)S(1)}, u32[]{:S(2)}, u32[]{:S(2)}) collective-permute-start(bf16[144,512]{1,0:T(8,128)(2,1)S(1)} %pair_state.1.refs_10_), channel_id=1, source_target_pairs={{32,160},{33,161},{34,162},{35,163},{36,164},{37,165},{38,166},{39... | collective-permute-start | bytes 442376 | tf_op jit(solution)/shard_map/ppermute | solution.py:54
  45.0 20.1 %collective-permute-start.16 = (bf16[144,512]{1,0:T(8,128)(2,1)S(1)}, bf16[144,512]{1,0:T(8,128)(2,1)S(1)}, u32[]{:S(2)}, u32[]{:S(2)}) collective-permute-start(bf16[144,512]{1,0:T(8,128)(2,1)S(1)} %pair_state.1.refs_10_), channel_id=1, source_target_pairs={{32,224},{33,225},{34,226},{35,227},{36,228},{37,229},{38,230},{39... | collective-permute-start | bytes 442376 | tf_op jit(solution)/shard_map/ppermute | solution.py:54
  65.1 5.1 %collective-permute-start.17 = (bf16[128,512]{1,0:T(8,128)(2,1)S(1)}, bf16[128,512]{1,0:T(8,128)(2,1)S(1)}, u32[]{:S(2)}, u32[]{:S(2)}) collective-permute-start(bf16[128,512]{1,0:T(8,128)(2,1)S(1)} %earlier_pairs.1.refs_1_), channel_id=1, source_target_pairs={{0,32},{1,33},{2,34},{3,35},{4,36},{5,37},{6,38},{7,39},{8,40},{9,... | collective-permute-start | bytes 393224 | tf_op jit(solution)/shard_map/ppermute | solution.py:54
  71.4 2.8 %collective-permute-start.19 = (bf16[272,1024]{1,0:T(8,128)(2,1)S(1)}, bf16[272,1024]{1,0:T(8,128)(2,1)S(1)}, u32[]{:S(2)}, u32[]{:S(2)}) collective-permute-start(bf16[272,1024]{1,0:T(8,128)(2,1)S(1)} %get-tuple-element.72), channel_id=1, source_target_pairs={{0,8},{1,9},{2,10},{3,11},{4,12},{5,13},{6,14},{7,15},{8,0},{9,1},... | collective-permute-start | bytes 1671176 | tf_op jit(solution)/shard_map/ppermute | solution.py:54
  73.6 2.0 %collective-permute-start.18 = (bf16[272,1024]{1,0:T(8,128)(2,1)S(1)}, bf16[272,1024]{1,0:T(8,128)(2,1)S(1)}, u32[]{:S(2)}, u32[]{:S(2)}) collective-permute-start(bf16[272,1024]{1,0:T(8,128)(2,1)S(1)} %get-tuple-element.70), channel_id=1, source_target_pairs={{0,8},{1,9},{2,10},{3,11},{4,12},{5,13},{6,14},{7,15},{8,0},{9,1},... | collective-permute-start | bytes 1671176 | tf_op jit(solution)/shard_map/ppermute | solution.py:54
  74.3 13.9 %collective-permute-start.20 = (bf16[272,1024]{1,0:T(8,128)(2,1)S(1)}, bf16[272,1024]{1,0:T(8,128)(2,1)S(1)}, u32[]{:S(2)}, u32[]{:S(2)}) collective-permute-start(bf16[272,1024]{1,0:T(8,128)(2,1)S(1)} %pair_sum.1), channel_id=1, source_target_pairs={{0,16},{1,17},{2,18},{3,19},{4,20},{5,21},{6,22},{7,23},{8,24},{9,... | collective-permute-start | bytes 1671176 | tf_op jit(solution)/shard_map/ppermute | solution.py:54

commit v5 on v4

--- a/solution.py
+++ b/solution.py
@@ -99,7 +99,7 @@
     return ones_at(row == 256 * (col // 64) + 64 * t + lax.rem(col, 64))
 
 
-def start_kernel(hidden, tokens, base_bias, iw, ow, act, ua, ub, other, rows_in, ids_in, bias_in, iw_in, ow_in, sem):
+def start_kernel(hidden, tokens, base_bias, iw, ow, act, ua, ub, ua_other, ub_other, rows_in, ids_in, bias_in, iw_in, ow_in, sem):
     _, yl, c, _, _, t = place()
     copies = [
         pltpu.make_async_copy(tokens, ids_in, sem.at[0]),
@@ -127,20 +127,19 @@
         act[ROWS * strand : ROWS * strand + ROWS, :] = block
     for copy in copies[3:]:
         copy.wait()
-    for early, first, late, second, which in ((ua, 0, ub, 0, t), (other, 0, other, UNIT, (1 - yl) * 2 + c)):
+    for early, late, which in ((ua, ub, t), (ua_other, ub_other, (1 - yl) * 2 + c)):
         for j in range(MINE):
             row = pl.multiple_of(256 * j + 64 * which, 64)
-            early[first + 64 * j : first + 64 * j + 64, :] = iw_in[pl.ds(E + row, 64), :]
-            late[second + 64 * j : second + 64 * j + 64, :] = iw_in[pl.ds(row, 64), :]
+            early[64 * j : 64 * j + 64, :] = iw_in[pl.ds(E + row, 64), :]
+            late[64 * j : 64 * j + 64, :] = iw_in[pl.ds(row, 64), :]
             out_rows = ow_in[pl.ds(pl.multiple_of(64 * which, 64), 64), 128 * j : 128 * j + 128]
-            late[second + OWN + 64 * j : second + OWN + 64 * j + 64, :] = out_rows
-        shared = iw_in[pl.ds(pl.multiple_of(2 * E + STATE * c, STATE), STATE), :]
-        early[first + OWN : first + OWN + STATE, :] = shared
-        early[first + OWN + STATE : first + UNIT, :] = iw_in[2 * E + 2 * STATE :, :]
-
-
-def split_far(both, prm, far):
-    far[...] = both[:UNIT, :]
+            late[OWN + 64 * j : OWN + 64 * j + 64, :] = out_rows
+        early[OWN : OWN + STATE, :] = iw_in[pl.ds(pl.multiple_of(2 * E + STATE * c, STATE), STATE), :]
+        early[OWN + STATE :, :] = iw_in[2 * E + 2 * STATE :, :]
+
+
+def hold(value, far, prm, out):
+    out[...] = value[...]
 
 
 def choose_halo(act, act_y, far, halo, far_out):
@@ -172,10 +171,10 @@
 
 
 def pack_core(*refs):
-    act, act_y, halo, ub, both = refs[:5]
-    units, out, out_b = refs[5:13], refs[13], refs[14]
-    out_b[:LATE, :] = ub[...]
-    out_b[LATE:, :] = both[UNIT:, :]
+    act, act_y, halo, ub, ub_far = refs[:5]
+    units, out, late = refs[5:13], refs[13], refs[14]
+    late[:LATE, :] = ub[...]
+    late[LATE:, :] = ub_far[...]
     out[: 2 * ROWS, :] = act[...]
     out[2 * ROWS : 4 * ROWS, :] = act_y[...]
     out[4 * ROWS : 4 * ROWS + HALO, :] = halo[...]
@@ -322,6 +321,10 @@
     out[STATE:, :] = jnp.where(line == 0, hi, jnp.where(line == 1, lo, 0.0)).astype(BF16)
 
 
+def again(value, out):
+    out[...] = value[...]
+
+
 def earlier_pairs(*refs):
     *pairs, out = refs
     total = jnp.zeros((STATE, OWN), F32)
@@ -494,10 +497,10 @@
 
 
 def body(hidden, tokens, base_bias, in_weight, conv_weight, conv_bias, dt_bias, decay_rate, norm_gain, out_weight):
-    act, ua, ub, other = call(
+    act, ua, ub, ua_other, ub_other = call(
         start_kernel,
         "start_kernel",
-        [shape(2 * ROWS, D), shape(UNIT, 128), shape(LATE, 128), shape(UNIT + LATE, 128)],
+        [shape(2 * ROWS, D)] + [shape(UNIT, 128), shape(LATE, 128)] * 2,
         [ANY] * 5,
         tuple(
             pltpu.with_memory_space_constraint(value, pltpu.HBM)
@@ -514,7 +517,7 @@
         mb=16,
     )
     act_y = swap_y(act)
-    both = swap_diagonal(other)
+    far = swap_diagonal(ua_other)
     own_1, own_3, own_2 = along_x(ua, 1), along_x(ua, 3), along_x(ua, 2)
     prm, heads = call(
         pack_params,
@@ -525,8 +528,9 @@
         scratch=[pltpu.VMEM((8, E), F32)],
         mb=12,
     )
-    far = call(split_far, "split_far", shape(UNIT, 128), [VMEM] * 2, (both, prm), mb=8)
+    ub_other = call(hold, "hold", shape(LATE, 128), [VMEM] * 3, (ub_other, far, prm), mb=8)
     far_1, far_3 = along_x(far, 1), along_x(far, 3)
+    ub_far = swap_diagonal(ub_other)
     halo, far_late = call(
         choose_halo, "choose_halo", [shape(HALO, D), shape(UNIT, 128)], [VMEM] * 3, (act, act_y, far), mb=8
     )
@@ -538,7 +542,7 @@
         "pack_core",
         [shape(PAYLOAD, D), shape(2 * LATE, 128)],
         [VMEM] * 13,
-        (act, act_y, halo, ub, both, *units),
+        (act, act_y, halo, ub, ub_far, *units),
         mb=12,
     )
     swapped = swap_core(payload)
@@ -569,14 +573,17 @@
         (act, weight, prm, heads),
         scratch=[pltpu.VMEM((PAD, WA), F32)],
         mb=20,
-        flops=16 * 1056 * D * WA,
+        flops=16896 * D * WA,
         bytes_accessed=8 << 20,
     )
     mate = move(given, lambda z, yl, c, yh, x: dict(z=z ^ 1))
     pair = call(pair_state, "pair_state", shape(STATE + HALO, OWN), [VMEM] * 2, (kept, mate), mb=8)
-    earlier = [move(pair, pair_step(m)) for m in (1, 2, 3)]
-    entered = call(earlier_pairs, "earlier_pairs", shape(STATE, OWN), [VMEM] * 3, earlier, mb=8)
-    mate_entered = move(entered, lambda z, yl, c, yh, x: dict(z=z ^ 1))
+    far_first = []
+    for m in (3, 2, 1):
+        far_first.append(move(pair, pair_step(m)))
+        if m > 1:
+            pair = call(again, "again", shape(STATE + HALO, OWN), [VMEM], (pair,), mb=8)
+    earlier = far_first[::-1]
     local, carry, maps = call(
         local_kernel,
         "local_kernel",
@@ -587,6 +594,8 @@
         flops=8 * 1024 * D * OWN,
         bytes_accessed=16 << 20,
     )
+    entered = call(earlier_pairs, "earlier_pairs", shape(STATE, OWN), [VMEM] * 3, earlier, mb=8)
+    mate_entered = move(entered, lambda z, yl, c, yh, x: dict(z=z ^ 1))
     gate, weight = call(
         gate_kernel,
         "gate_kernel",

time: 89.7 us -> 88.2 us (0.983)
  waiting for transfers between devices: 37 us -> 31.2 us
  starting transfers between devices: 31 us -> 35.4 us
    ppermute x21 -> x22, waiting for transfers between devices: 37 us -> 31.2 us  [move(): return lax.ppermute(value, ('seq', 'fsdp'), pairs)]
    ppermute x21 -> x22, starting transfers between devices: 31 us -> 35.4 us  [move(): return lax.ppermute(value, ('seq', 'fsdp'), pairs)]
    pallas_call x15 -> x17, Pallas kernels: 21.2 us -> 21.2 us  [call(): pl.pallas_call(kernel, out_shape=outs, in_specs=ins, out_specs=jax.tree.m...]
  transfers between devices with their start and end apart: 21 -> 22, of which waited for: 10 -> 8; matrix products, arithmetic and copies ran while one was open for 0% -> 0% of each run, Pallas kernels for 19% -> 19%
where the time goes in v5:
time: 88.2 us; the launch traced here: 88.1 us
  starting transfers between devices  35.4 us (40%)
  waiting for transfers between devices  31.2 us (35%)
  Pallas kernels  21.2 us (24%)
    ppermute x22, starting transfers between devices, move(): return lax.ppermute(value, ('seq', 'fsdp'), pairs)  35.4 us
    ppermute x22, waiting for transfers between devices, move(): return lax.ppermute(value, ('seq', 'fsdp'), pairs)  31.2 us
    pallas_call x17, Pallas kernels, call(): pl.pallas_call(kernel, out_shape=outs, in_specs=ins, out_specs=jax.tree.m...  21.2 us
  transfers between devices with their start and end apart: 22, of which 8 were waited for; matrix products, arithmetic and copies ran while one was open for 0% of the time, Pallas kernels for 19%

profile of v5, /device:TPU:1, one launch (start us, length us, event | category | flops | bytes accessed | tf_op | source)
XLA Modules:
  0.0 88.1 jit_solution(14690049811076071914)
XLA Ops:
  0.0 1.9 %start_kernel.1 = (bf16[256,1024]{1,0:T(8,128)(2,1)S(1)}, bf16[672,128]{1,0:T(8,128)(2,1)S(1)}, bf16[1024,128]{1,0:T(8,128)(2,1)S(1)}, bf16[672,128]{1,0:T(8,128)(2,1)S(1)}, bf16[1024,128]{1,0:T(8,128)(2,1)S(1)}) custom-call(bf16[128,2048]{1,0:T(8,128)(2,1)} %bitcast.10, s32[1,128]{1,0:T(1,128)} %tokens.1, bf16[5,2048]{1,0:T(8,128)(2,1)} %base_bias.1, ...), custom_call_target="tpu_custom_call" | custom-call | tf_op jit(solution)/shard_map/start_kernel/pallas_call | solution.py:62
  2.0 2.2 %collective-permute-start = (bf16[256,1024]{1,0:T(8,128)(2,1)S(1)}, bf16[256,1024]{1,0:T(8,128)(2,1)S(1)}, u32[]{:S(2)}, u32[]{:S(2)}) collective-permute-start(bf16[256,1024]{1,0:T(8,128)(2,1)S(1)} %get-tuple-element.40.act.refs_0_), channel_id=1, source_target_pairs={{0,16},{1,17},{2,18},{3,19},{4,20},{5,21},{6,22},{7,23},{8,24},{9,... | collective-permute-start | bytes 1572872 | tf_op jit(solution)/shard_map/ppermute | solution.py:54
  4.2 1.9 %collective-permute-start.1 = (bf16[672,128]{1,0:T(8,128)(2,1)S(1)}, bf16[672,128]{1,0:T(8,128)(2,1)S(1)}, u32[]{:S(2)}, u32[]{:S(2)}) collective-permute-start(bf16[672,128]{1,0:T(8,128)(2,1)S(1)} %get-tuple-element.41), channel_id=1, source_target_pairs={{0,20},{1,21},{2,22},{3,23},{4,16},{5,17},{6,18},{7,19},{8,28},{9,... | collective-permute-start | bytes 516104 | tf_op jit(solution)/shard_map/ppermute | solution.py:54
  6.1 1.2 %collective-permute-start.4 = (bf16[672,128]{1,0:T(8,128)(2,1)S(1)}, bf16[672,128]{1,0:T(8,128)(2,1)S(1)}, u32[]{:S(2)}, u32[]{:S(2)}) collective-permute-start(bf16[672,128]{1,0:T(8,128)(2,1)S(1)} %get-tuple-element.46.refs_5_.refs_4_), channel_id=1, source_target_pairs={{0,1},{1,2},{2,3},{3,0},{4,5},{5,6},{6,7},{7,4},{8,9},{9,10},{10,1... | collective-permute-start | bytes 516104 | tf_op jit(solution)/shard_map/ppermute | solution.py:54
  7.3 2.5 %collective-permute-start.5 = (bf16[672,128]{1,0:T(8,128)(2,1)S(1)}, bf16[672,128]{1,0:T(8,128)(2,1)S(1)}, u32[]{:S(2)}, u32[]{:S(2)}) collective-permute-start(bf16[672,128]{1,0:T(8,128)(2,1)S(1)} %get-tuple-element.46.refs_5_.refs_4_), channel_id=1, source_target_pairs={{0,2},{1,3},{2,0},{3,1},{4,6},{5,7},{6,4},{7,5},{8,10},{9,11},{10,... | collective-permute-start | bytes 516104 | tf_op jit(solution)/shard_map/ppermute | solution.py:54
  9.8 0.6 pack_params.1
  10.3 0.0 collective-permute-done.1.far.refs_9_.refs_8_
  10.4 1.9 %collective-permute-start.3 = (bf16[1024,128]{1,0:T(8,128)(2,1)S(1)}, bf16[1024,128]{1,0:T(8,128)(2,1)S(1)}, u32[]{:S(2)}, u32[]{:S(2)}) collective-permute-start(bf16[1024,128]{1,0:T(8,128)(2,1)S(1)} %hold.1), channel_id=1, source_target_pairs={{0,20},{1,21},{2,22},{3,23},{4,16},{5,17},{6,18},{7,19},{8,28},{9,... | collective-permute-start | bytes 786440 | tf_op jit(solution)/shard_map/ppermute | solution.py:54
  12.3 2.5 %collective-permute-start.6 = (bf16[672,128]{1,0:T(8,128)(2,1)S(1)}, bf16[672,128]{1,0:T(8,128)(2,1)S(1)}, u32[]{:S(2)}, u32[]{:S(2)}) collective-permute-start(bf16[672,128]{1,0:T(8,128)(2,1)S(1)} %get-tuple-element.46.refs_5_.refs_4_), channel_id=1, source_target_pairs={{0,3},{1,0},{2,1},{3,2},{4,7},{5,4},{6,5},{7,6},{8,11},{9,8},{10,9... | collective-permute-start | bytes 516104 | tf_op jit(solution)/shard_map/ppermute | solution.py:54
  14.8 2.1 %collective-permute-start.7 = (bf16[672,128]{1,0:T(8,128)(2,1)S(1)}, bf16[672,128]{1,0:T(8,128)(2,1)S(1)}, u32[]{:S(2)}, u32[]{:S(2)}) collective-permute-start(bf16[672,128]{1,0:T(8,128)(2,1)S(1)} %collective-permute-done.1.far.refs_9_.refs_8_), channel_id=1, source_target_pairs={{0,1},{1,2},{2,3},{3,0},{4,5},{5,6},{6,7},{7,4},{8,9},{9,10},{10,1... | collective-permute-start | bytes 516104 | tf_op jit(solution)/shard_map/ppermute | solution.py:54
  16.9 0.0 collective-permute-done.4.refs_6_.refs_5_
  16.9 1.4 %collective-permute-start.9 = (bf16[672,128]{1,0:T(8,128)(2,1)S(1)}, bf16[672,128]{1,0:T(8,128)(2,1)S(1)}, u32[]{:S(2)}, u32[]{:S(2)}) collective-permute-start(bf16[672,128]{1,0:T(8,128)(2,1)S(1)} %collective-permute-done.1.far.refs_9_.refs_8_), channel_id=1, source_target_pairs={{0,3},{1,0},{2,1},{3,2},{4,7},{5,4},{6,5},{7,6},{8,11},{9,8},{10,9... | collective-permute-start | bytes 516104 | tf_op jit(solution)/shard_map/ppermute | solution.py:54
  18.3 1.7 %collective-permute-start.8 = (bf16[672,128]{1,0:T(8,128)(2,1)S(1)}, bf16[672,128]{1,0:T(8,128)(2,1)S(1)}, u32[]{:S(2)}, u32[]{:S(2)}) collective-permute-start(bf16[672,128]{1,0:T(8,128)(2,1)S(1)} %get-tuple-element.47), channel_id=1, source_target_pairs={{0,2},{1,3},{2,0},{3,1},{4,6},{5,7},{6,4},{7,5},{8,10},{9,11},{10,... | collective-permute-start | bytes 516104 | tf_op jit(solution)/shard_map/ppermute | solution.py:54
  20.0 0.0 collective-permute-done.6.refs_8_.refs_7_
  20.0 3.5 %collective-permute-start.2 = (bf16[16,1024]{1,0:T(8,128)(2,1)S(1)}, bf16[16,1024]{1,0:T(8,128)(2,1)S(1)}, u32[]{:S(2)}, u32[]{:S(2)}) collective-permute-start(bf16[16,1024]{1,0:T(8,128)(2,1)S(1)} %get-tuple-element.42), channel_id=1, source_target_pairs={{8,40},{9,41},{10,42},{11,43},{12,44},{13,45},{14,46},{15,47},{24,... | collective-permute-start | bytes 98312 | tf_op jit(solution)/shard_map/ppermute | solution.py:54
  23.5 0.0 collective-permute-done.7.refs_10_.refs_9_
  23.6 0.6 collective-permute-done.9.refs_12_.refs_11_
  24.1 0.4 collective-permute-done.2.refs_2_
  24.5 1.2 %collective-permute-done.8.refs_11_.refs_10_ = bf16[672,128]{1,0:T(8,128)(2,1)S(1)} collective-permute-done((bf16[672,128]{1,0:T(8,128)(2,1)S(1)}, bf16[672,128]{1,0:T(8,128)(2,1)S(1)}, u32[]{:S(2)}, u32[]{:S(2)}) %collective-permute-start.8) | collective-permute-done | bytes 172064 | tf_op jit(solution)/shard_map/ppermute | solution.py:54
  25.8 0.2 pack_core.1
  25.9 2.7 %collective-permute-start.10 = (bf16[656,1024]{1,0:T(8,128)(2,1)S(1)}, bf16[656,1024]{1,0:T(8,128)(2,1)S(1)}, u32[]{:S(2)}, u32[]{:S(2)}) collective-permute-start(bf16[656,1024]{1,0:T(8,128)(2,1)S(1)} %get-tuple-element.48), channel_id=1, source_target_pairs={{0,8},{1,9},{2,10},{3,11},{4,12},{5,13},{6,14},{7,15},{8,0},{9,1},... | collective-permute-start | bytes 4030472 | tf_op jit(solution)/shard_map/ppermute | solution.py:54
  28.7 1.0 %collective-permute-start.11 = (bf16[2048,128]{1,0:T(8,128)(2,1)S(1)}, bf16[2048,128]{1,0:T(8,128)(2,1)S(1)}, u32[]{:S(2)}, u32[]{:S(2)}) collective-permute-start(bf16[2048,128]{1,0:T(8,128)(2,1)S(1)} %get-tuple-element.51.refs_0_), channel_id=1, source_target_pairs={{0,1},{1,2},{2,3},{3,0},{4,5},{5,6},{6,7},{7,4},{8,9},{9,10},{10,1... | collective-permute-start | bytes 1572872 | tf_op jit(solution)/shard_map/ppermute | solution.py:54
  29.6 2.8 %collective-permute-start.12 = (bf16[2048,128]{1,0:T(8,128)(2,1)S(1)}, bf16[2048,128]{1,0:T(8,128)(2,1)S(1)}, u32[]{:S(2)}, u32[]{:S(2)}) collective-permute-start(bf16[2048,128]{1,0:T(8,128)(2,1)S(1)} %get-tuple-element.51.refs_0_), channel_id=1, source_target_pairs={{0,2},{1,3},{2,0},{3,1},{4,6},{5,7},{6,4},{7,5},{8,10},{9,11},{10,... | collective-permute-start | bytes 1572872 | tf_op jit(solution)/shard_map/ppermute | solution.py:54
  32.4 0.0 collective-permute-start.13
  32.4 0.0 collective-permute-done.10.refs_3_
  32.4 4.3 %first_scan.1 = (bf16[512,512]{1,0:T(8,128)(2,1)S(1)}, bf16[512,256]{1,0:T(8,128)(2,1)S(1)}, f32[32,128]{1,0:T(8,128)S(1)}, f32[32,128]{1,0:T(8,128)S(1)}, bf16[...) custom-call(bf16[256,1024]{1,0:T(8,128)(2,1)S(1)} %get-tuple-element, ...), custom_call_target="tpu_custom_call" | custom-call | flops 968884224 | bytes 8388608 | tf_op jit(solution)/shard_map/first_scan/pallas_call | solution.py:62
  36.7 1.7 %collective-permute-start.14 = (bf16[144,512]{1,0:T(8,128)(2,1)S(1)}, bf16[144,512]{1,0:T(8,128)(2,1)S(1)}, u32[]{:S(2)}, u32[]{:S(2)}) collective-permute-start(bf16[144,512]{1,0:T(8,128)(2,1)S(1)} %get-tuple-element.53), channel_id=1, source_target_pairs={{0,32},{1,33},{2,34},{3,35},{4,36},{5,37},{6,38},{7,39},{8,40},{9,... | collective-permute-start | bytes 442376 | tf_op jit(solution)/shard_map/ppermute | solution.py:54
  38.4 3.6 %second_scan.1 = (bf16[512,512]{1,0:T(8,128)(2,1)S(1)}, bf16[512,256]{1,0:T(8,128)(2,1)S(1)}, f32[32,128]{1,0:T(8,128)S(1)}, f32[32,128]{1,0:T(8,128)S(1)}, bf16...) custom-call(bf16[2,528,1024]{2,1,0:T(8,128)(2,1)S(1)} %get-tuple-element.50.act, ...), custom_call_target="tpu_custom_call" | custom-call | flops 15502147584 | bytes 8388608 | tf_op jit(solution)/shard_map/second_scan/pallas_call | solution.py:62
  42.0 0.1 pair_state.1.value
  42.1 1.3 %collective-permute-start.16 = (bf16[144,512]{1,0:T(8,128)(2,1)S(1)}, bf16[144,512]{1,0:T(8,128)(2,1)S(1)}, u32[]{:S(2)}, u32[]{:S(2)}) collective-permute-start(bf16[144,512]{1,0:T(8,128)(2,1)S(1)} %again.2.value), channel_id=1, source_target_pairs={{32,160},{33,161},{34,162},{35,163},{36,164},{37,165},{38,166},{39... | collective-permute-start | bytes 442376 | tf_op jit(solution)/shard_map/ppermute | solution.py:54
  43.4 1.3 %collective-permute-start.15 = (bf16[144,512]{1,0:T(8,128)(2,1)S(1)}, bf16[144,512]{1,0:T(8,128)(2,1)S(1)}, u32[]{:S(2)}, u32[]{:S(2)}) collective-permute-start(bf16[144,512]{1,0:T(8,128)(2,1)S(1)} %again.3.refs_10_), channel_id=1, source_target_pairs={{32,96},{33,97},{34,98},{35,99},{36,100},{37,101},{38,102},{39,103... | collective-permute-start | bytes 442376 | tf_op jit(solution)/shard_map/ppermute | solution.py:54
  44.8 1.3 %collective-permute-start.17 = (bf16[144,512]{1,0:T(8,128)(2,1)S(1)}, bf16[144,512]{1,0:T(8,128)(2,1)S(1)}, u32[]{:S(2)}, u32[]{:S(2)}) collective-permute-start(bf16[144,512]{1,0:T(8,128)(2,1)S(1)} %pair_state.1.value), channel_id=1, source_target_pairs={{32,224},{33,225},{34,226},{35,227},{36,228},{37,229},{38,230},{39... | collective-permute-start | bytes 442376 | tf_op jit(solution)/shard_map/ppermute | solution.py:54
  46.1 9.6 %collective-permute-done.12.refs_2_ = bf16[2048,128]{1,0:T(8,128)(2,1)S(1)} collective-permute-done((bf16[2048,128]{1,0:T(8,128)(2,1)S(1)}, bf16[2048,128]{1,0:T(8,128)(2,1)S(1)}, u32[]{:S(2)}, u32[]{:S(2)}) %collective-permute-start.12) | collective-permute-done | bytes 524320 | tf_op jit(solution)/shard_map/ppermute | solution.py:54
  55.7 1.9 %gate_kernel.1 = (f32[2,512,512]{2,1,0:T(8,128)S(1)}, bf16[2,512,512]{2,1,0:T(8,128)(2,1)S(1)}) custom-call(bf16[2,528,1024]{2,1,0:T(8,128)(2,1)S(1)} %get-tuple-element.50.act, bf16[2048,128]{1,0:T(8,128)(2,1)S(1)} %get-tuple-element.51.refs_0_, bf16[2048,128]{1,0:T(8,128)(2,1)S(1)} %collective-permute-done.11.refs_1_, ...), custom_call_target="tpu_custom_call" | custom-call | flops 1073741824 | bytes 8388608 | tf_op jit(solution)/shard_map/gate_kernel/pallas_call | solution.py:62
  57.6 6.0 %collective-permute-done.17.refs_2_ = bf16[144,512]{1,0:T(8,128)(2,1)S(1)} collective-permute-done((bf16[144,512]{1,0:T(8,128)(2,1)S(1)}, bf16[144,512]{1,0:T(8,128)(2,1)S(1)}, u32[]{:S(2)}, u32[]{:S(2)}) %collective-permute-start.17) | collective-permute-done | bytes 147488 | tf_op jit(solution)/shard_map/ppermute | solution.py:54
  63.6 0.1 earlier_pairs.1.refs_1_
  63.7 0.1 collective-permute-start.18
  63.8 5.0 %local_kernel.1 = (f32[2,512,512]{2,1,0:T(8,128)S(1)}, f32[2,512,512]{2,1,0:T(8,128)S(1)}, bf16[2,512,128]{2,1,0:T(8,128)(2,1)S(1)}) custom-call(bf16[512,512]{1,0:T(8,128)(2,1)S(1)} %get-tuple-element.56.refs_0_, bf16[512,256]{1,0:T(8,128)(2,1)S(1)} %get-tuple-element.57.refs_1_, f32[32,128]{1,0:T(8,128)S(1)} %get-tuple-element.58.refs_2_, ...), custom_call_target="tpu_custom_call" | custom-call | flops 4294967296 | bytes 16777216 | tf_op jit(solution)/shard_map/local_kernel/pallas_call | solution.py:62
  68.8 1.1 %first_half.1 = (bf16[2,128,512]{2,1,0:T(8,128)(2,1)S(1)}, bf16[272,1024]{1,0:T(8,128)(2,1)S(1)}, bf16[272,1024]{1,0:T(8,128)(2,1)S(1)}) custom-call(bf16[144,512]{1,0:T(8,128)(2,1)S(1)} %collective-permute-done.14.mate.refs_0_, bf16[128,512]{1,0:T(8,128)(2,1)S(1)} %earlier_pairs.1.refs_1_, bf16[128,512]{1,0:T(8,128)(2,1)S(1)} %collective-permute-done.18.refs_2_, ...), custom_call_target="tpu_custom_call" | custom-call | flops 536870912 | bytes 4194304 | tf_op jit(solution)/shard_map/first_half/pallas_call | solution.py:62
  69.9 1.2 %collective-permute-start.20 = (bf16[272,1024]{1,0:T(8,128)(2,1)S(1)}, bf16[272,1024]{1,0:T(8,128)(2,1)S(1)}, u32[]{:S(2)}, u32[]{:S(2)}) collective-permute-start(bf16[272,1024]{1,0:T(8,128)(2,1)S(1)} %get-tuple-element.74), channel_id=1, source_target_pairs={{0,8},{1,9},{2,10},{3,11},{4,12},{5,13},{6,14},{7,15},{8,0},{9,1},... | collective-permute-start | bytes 1671176 | tf_op jit(solution)/shard_map/ppermute | solution.py:54
  71.1 1.0 %second_half.1 = (bf16[272,1024]{1,0:T(8,128)(2,1)S(1)}, bf16[272,1024]{1,0:T(8,128)(2,1)S(1)}) custom-call(bf16[2,512,512]{2,1,0:T(8,128)(2,1)S(1)} %get-tuple-element.52.refs_3_.weight, bf16[2,128,512]{2,1,0:T(8,128)(2,1)S(1)} %get-tuple-element.70.entering, f32[8,768]{1,0:T(8,128)S(1)} %get-tuple-element.45.prm.refs_12_.refs_4_, ...), custom_call_target="tpu_custom_call" | custom-call | flops 536870912 | bytes 4194304 | tf_op jit(solution)/shard_map/second_half/pallas_call | solution.py:62
  72.2 0.1 collective-permute-start.19
  72.3 0.4 collective-permute-done.20.came
  72.7 0.1 pair_sum.1
  72.9 1.0 %collective-permute-start.21 = (bf16[272,1024]{1,0:T(8,128)(2,1)S(1)}, bf16[272,1024]{1,0:T(8,128)(2,1)S(1)}, u32[]{:S(2)}, u32[]{:S(2)}) collective-permute-start(bf16[272,1024]{1,0:T(8,128)(2,1)S(1)} %pair_sum.1), channel_id=1, source_target_pairs={{0,16},{1,17},{2,18},{3,19},{4,20},{5,21},{6,22},{7,23},{8,24},{9,... | collective-permute-start | bytes 1671176 | tf_op jit(solution)/shard_map/ppermute | solution.py:54
  73.9 0.3 collective-permute-done.19.came
  74.2 12.6 %collective-permute-done.21.far = bf16[272,1024]{1,0:T(8,128)(2,1)S(1)} collective-permute-done((bf16[272,1024]{1,0:T(8,128)(2,1)S(1)}, bf16[272,1024]{1,0:T(8,128)(2,1)S(1)}, u32[]{:S(2)}, u32[]{:S(2)}) %collective-permute-start.21) | collective-permute-done | bytes 557088 | tf_op jit(solution)/shard_map/ppermute | solution.py:54
  86.8 1.3 %last_kernel.1 = bf16[128,2048]{1,0:T(8,128)(2,1)} custom-call(bf16[272,1024]{1,0:T(8,128)(2,1)S(1)} %get-tuple-element.71.second.mine, bf16[272,1024]{1,0:T(8,128)(2,1)S(1)} %collective-permute-done.19.came, bf16[272,1024]{1,0:T(8,128)(2,1)S(1)} %collective-permute-done.21.far), custom_call_target="tpu_custom_call" | custom-call | tf_op jit(solution)/shard_map/last_kernel/pallas_call | solution.py:62
  (24 shorter events, 0.1 us)
Async XLA Ops:
  0.0 9.7 %copy-start.4 = (f32[2304]{0:T(1024)S(1)}, f32[2304]{0:T(1024)}, u32[]{:S(2)}) copy-start(f32[2304]{0:T(1024)} %param.15) | copy-start | bytes 27652
  0.0 9.8 %copy-start = (f32[4,2304]{1,0:T(4,128)S(1)}, f32[4,2304]{1,0:T(4,128)}, u32[]{:S(2)}) copy-start(f32[4,2304]{1,0:T(4,128)} %cw.1) | copy-start | bytes 110596
  0.0 9.8 %copy-start.2 = (f32[32]{0:T(128)S(1)}, f32[32]{0:T(128)}, u32[]{:S(2)}) copy-start(f32[32]{0:T(128)} %param.16) | copy-start | bytes 388
  0.0 9.8 %copy-start.3 = (f32[32]{0:T(128)S(1)}, f32[32]{0:T(128)}, u32[]{:S(2)}) copy-start(f32[32]{0:T(128)} %param.17) | copy-start | bytes 388
  0.0 9.8 %copy-start.1 = (f32[2048]{0:T(1024)S(1)}, f32[2048]{0:T(1024)}, u32[]{:S(2)}) copy-start(f32[2048]{0:T(1024)} %param.18) | copy-start | bytes 24580
  2.0 12.8 %collective-permute-start = (bf16[256,1024]{1,0:T(8,128)(2,1)S(1)}, bf16[256,1024]{1,0:T(8,128)(2,1)S(1)}, u32[]{:S(2)}, u32[]{:S(2)}) collective-permute-start(bf16[256,1024]{1,0:T(8,128)(2,1)S(1)} %get-tuple-element.40.act.refs_0_), channel_id=1, source_target_pairs={{0,16},{1,17},{2,18},{3,19},{4,20},{5,21},{6,22},{7,23},{8,24},{9,... | collective-permute-start | bytes 1572872 | tf_op jit(solution)/shard_map/ppermute | solution.py:54
  4.2 6.2 %collective-permute-start.1 = (bf16[672,128]{1,0:T(8,128)(2,1)S(1)}, bf16[672,128]{1,0:T(8,128)(2,1)S(1)}, u32[]{:S(2)}, u32[]{:S(2)}) collective-permute-start(bf16[672,128]{1,0:T(8,128)(2,1)S(1)} %get-tuple-element.41), channel_id=1, source_target_pairs={{0,20},{1,21},{2,22},{3,23},{4,16},{5,17},{6,18},{7,19},{8,28},{9,... | collective-permute-start | bytes 516104 | tf_op jit(solution)/shard_map/ppermute | solution.py:54
  6.1 10.8 %collective-permute-start.4 = (bf16[672,128]{1,0:T(8,128)(2,1)S(1)}, bf16[672,128]{1,0:T(8,128)(2,1)S(1)}, u32[]{:S(2)}, u32[]{:S(2)}) collective-permute-start(bf16[672,128]{1,0:T(8,128)(2,1)S(1)} %get-tuple-element.46.refs_5_.refs_4_), channel_id=1, source_target_pairs={{0,1},{1,2},{2,3},{3,0},{4,5},{5,6},{6,7},{7,4},{8,9},{9,10},{10,1... | collective-permute-start | bytes 516104 | tf_op jit(solution)/shard_map/ppermute | solution.py:54
  7.3 11.0 %collective-permute-start.5 = (bf16[672,128]{1,0:T(8,128)(2,1)S(1)}, bf16[672,128]{1,0:T(8,128)(2,1)S(1)}, u32[]{:S(2)}, u32[]{:S(2)}) collective-permute-start(bf16[672,128]{1,0:T(8,128)(2,1)S(1)} %get-tuple-element.46.refs_5_.refs_4_), channel_id=1, source_target_pairs={{0,2},{1,3},{2,0},{3,1},{4,6},{5,7},{6,4},{7,5},{8,10},{9,11},{10,... | collective-permute-start | bytes 516104 | tf_op jit(solution)/shard_map/ppermute | solution.py:54
  10.4 13.8 %collective-permute-start.3 = (bf16[1024,128]{1,0:T(8,128)(2,1)S(1)}, bf16[1024,128]{1,0:T(8,128)(2,1)S(1)}, u32[]{:S(2)}, u32[]{:S(2)}) collective-permute-start(bf16[1024,128]{1,0:T(8,128)(2,1)S(1)} %hold.1), channel_id=1, source_target_pairs={{0,20},{1,21},{2,22},{3,23},{4,16},{5,17},{6,18},{7,19},{8,28},{9,... | collective-permute-start | bytes 786440 | tf_op jit(solution)/shard_map/ppermute | solution.py:54
  12.3 7.7 %collective-permute-start.6 = (bf16[672,128]{1,0:T(8,128)(2,1)S(1)}, bf16[672,128]{1,0:T(8,128)(2,1)S(1)}, u32[]{:S(2)}, u32[]{:S(2)}) collective-permute-start(bf16[672,128]{1,0:T(8,128)(2,1)S(1)} %get-tuple-element.46.refs_5_.refs_4_), channel_id=1, source_target_pairs={{0,3},{1,0},{2,1},{3,2},{4,7},{5,4},{6,5},{7,6},{8,11},{9,8},{10,9... | collective-permute-start | bytes 516104 | tf_op jit(solution)/shard_map/ppermute | solution.py:54
  14.8 8.7 %collective-permute-start.7 = (bf16[672,128]{1,0:T(8,128)(2,1)S(1)}, bf16[672,128]{1,0:T(8,128)(2,1)S(1)}, u32[]{:S(2)}, u32[]{:S(2)}) collective-permute-start(bf16[672,128]{1,0:T(8,128)(2,1)S(1)} %collective-permute-done.1.far.refs_9_.refs_8_), channel_id=1, source_target_pairs={{0,1},{1,2},{2,3},{3,0},{4,5},{5,6},{6,7},{7,4},{8,9},{9,10},{10,1... | collective-permute-start | bytes 516104 | tf_op jit(solution)/shard_map/ppermute | solution.py:54
  16.9 7.2 %collective-permute-start.9 = (bf16[672,128]{1,0:T(8,128)(2,1)S(1)}, bf16[672,128]{1,0:T(8,128)(2,1)S(1)}, u32[]{:S(2)}, u32[]{:S(2)}) collective-permute-start(bf16[672,128]{1,0:T(8,128)(2,1)S(1)} %collective-permute-done.1.far.refs_9_.refs_8_), channel_id=1, source_target_pairs={{0,3},{1,0},{2,1},{3,2},{4,7},{5,4},{6,5},{7,6},{8,11},{9,8},{10,9... | collective-permute-start | bytes 516104 | tf_op jit(solution)/shard_map/ppermute | solution.py:54
  18.3 7.5 %collective-permute-start.8 = (bf16[672,128]{1,0:T(8,128)(2,1)S(1)}, bf16[672,128]{1,0:T(8,128)(2,1)S(1)}, u32[]{:S(2)}, u32[]{:S(2)}) collective-permute-start(bf16[672,128]{1,0:T(8,128)(2,1)S(1)} %get-tuple-element.47), channel_id=1, source_target_pairs={{0,2},{1,3},{2,0},{3,1},{4,6},{5,7},{6,4},{7,5},{8,10},{9,11},{10,... | collective-permute-start | bytes 516104 | tf_op jit(solution)/shard_map/ppermute | solution.py:54
  20.0 4.5 %collective-permute-start.2 = (bf16[16,1024]{1,0:T(8,128)(2,1)S(1)}, bf16[16,1024]{1,0:T(8,128)(2,1)S(1)}, u32[]{:S(2)}, u32[]{:S(2)}) collective-permute-start(bf16[16,1024]{1,0:T(8,128)(2,1)S(1)} %get-tuple-element.42), channel_id=1, source_target_pairs={{8,40},{9,41},{10,42},{11,43},{12,44},{13,45},{14,46},{15,47},{24,... | collective-permute-start | bytes 98312 | tf_op jit(solution)/shard_map/ppermute | solution.py:54
  25.9 6.5 %collective-permute-start.10 = (bf16[656,1024]{1,0:T(8,128)(2,1)S(1)}, bf16[656,1024]{1,0:T(8,128)(2,1)S(1)}, u32[]{:S(2)}, u32[]{:S(2)}) collective-permute-start(bf16[656,1024]{1,0:T(8,128)(2,1)S(1)} %get-tuple-element.48), channel_id=1, source_target_pairs={{0,8},{1,9},{2,10},{3,11},{4,12},{5,13},{6,14},{7,15},{8,0},{9,1},... | collective-permute-start | bytes 4030472 | tf_op jit(solution)/shard_map/ppermute | solution.py:54
  28.7 16.1 %collective-permute-start.11 = (bf16[2048,128]{1,0:T(8,128)(2,1)S(1)}, bf16[2048,128]{1,0:T(8,128)(2,1)S(1)}, u32[]{:S(2)}, u32[]{:S(2)}) collective-permute-start(bf16[2048,128]{1,0:T(8,128)(2,1)S(1)} %get-tuple-element.51.refs_0_), channel_id=1, source_target_pairs={{0,1},{1,2},{2,3},{3,0},{4,5},{5,6},{6,7},{7,4},{8,9},{9,10},{10,1... | collective-permute-start | bytes 1572872 | tf_op jit(solution)/shard_map/ppermute | solution.py:54
  29.6 26.0 %collective-permute-start.12 = (bf16[2048,128]{1,0:T(8,128)(2,1)S(1)}, bf16[2048,128]{1,0:T(8,128)(2,1)S(1)}, u32[]{:S(2)}, u32[]{:S(2)}) collective-permute-start(bf16[2048,128]{1,0:T(8,128)(2,1)S(1)} %get-tuple-element.51.refs_0_), channel_id=1, source_target_pairs={{0,2},{1,3},{2,0},{3,1},{4,6},{5,7},{6,4},{7,5},{8,10},{9,11},{10,... | collective-permute-start | bytes 1572872 | tf_op jit(solution)/shard_map/ppermute | solution.py:54
  32.4 23.2 %collective-permute-start.13 = (bf16[2048,128]{1,0:T(8,128)(2,1)S(1)}, bf16[2048,128]{1,0:T(8,128)(2,1)S(1)}, u32[]{:S(2)}, u32[]{:S(2)}) collective-permute-start(bf16[2048,128]{1,0:T(8,128)(2,1)S(1)} %get-tuple-element.51.refs_0_), channel_id=1, source_target_pairs={{0,3},{1,0},{2,1},{3,2},{4,7},{5,4},{6,5},{7,6},{8,11},{9,8},{10,9... | collective-permute-start | bytes 1572872 | tf_op jit(solution)/shard_map/ppermute | solution.py:54
  36.7 5.4 %collective-permute-start.14 = (bf16[144,512]{1,0:T(8,128)(2,1)S(1)}, bf16[144,512]{1,0:T(8,128)(2,1)S(1)}, u32[]{:S(2)}, u32[]{:S(2)}) collective-permute-start(bf16[144,512]{1,0:T(8,128)(2,1)S(1)} %get-tuple-element.53), channel_id=1, source_target_pairs={{0,32},{1,33},{2,34},{3,35},{4,36},{5,37},{6,38},{7,39},{8,40},{9,... | collective-permute-start | bytes 442376 | tf_op jit(solution)/shard_map/ppermute | solution.py:54
  42.1 15.5 %collective-permute-start.16 = (bf16[144,512]{1,0:T(8,128)(2,1)S(1)}, bf16[144,512]{1,0:T(8,128)(2,1)S(1)}, u32[]{:S(2)}, u32[]{:S(2)}) collective-permute-start(bf16[144,512]{1,0:T(8,128)(2,1)S(1)} %again.2.value), channel_id=1, source_target_pairs={{32,160},{33,161},{34,162},{35,163},{36,164},{37,165},{38,166},{39... | collective-permute-start | bytes 442376 | tf_op jit(solution)/shard_map/ppermute | solution.py:54
  43.4 14.2 %collective-permute-start.15 = (bf16[144,512]{1,0:T(8,128)(2,1)S(1)}, bf16[144,512]{1,0:T(8,128)(2,1)S(1)}, u32[]{:S(2)}, u32[]{:S(2)}) collective-permute-start(bf16[144,512]{1,0:T(8,128)(2,1)S(1)} %again.3.refs_10_), channel_id=1, source_target_pairs={{32,96},{33,97},{34,98},{35,99},{36,100},{37,101},{38,102},{39,103... | collective-permute-start | bytes 442376 | tf_op jit(solution)/shard_map/ppermute | solution.py:54
  44.8 18.9 %collective-permute-start.17 = (bf16[144,512]{1,0:T(8,128)(2,1)S(1)}, bf16[144,512]{1,0:T(8,128)(2,1)S(1)}, u32[]{:S(2)}, u32[]{:S(2)}) collective-permute-start(bf16[144,512]{1,0:T(8,128)(2,1)S(1)} %pair_state.1.value), channel_id=1, source_target_pairs={{32,224},{33,225},{34,226},{35,227},{36,228},{37,229},{38,230},{39... | collective-permute-start | bytes 442376 | tf_op jit(solution)/shard_map/ppermute | solution.py:54
  63.7 5.1 %collective-permute-start.18 = (bf16[128,512]{1,0:T(8,128)(2,1)S(1)}, bf16[128,512]{1,0:T(8,128)(2,1)S(1)}, u32[]{:S(2)}, u32[]{:S(2)}) collective-permute-start(bf16[128,512]{1,0:T(8,128)(2,1)S(1)} %earlier_pairs.1.refs_1_), channel_id=1, source_target_pairs={{0,32},{1,33},{2,34},{3,35},{4,36},{5,37},{6,38},{7,39},{8,40},{9,... | collective-permute-start | bytes 393224 | tf_op jit(solution)/shard_map/ppermute | solution.py:54
  69.9 2.8 %collective-permute-start.20 = (bf16[272,1024]{1,0:T(8,128)(2,1)S(1)}, bf16[272,1024]{1,0:T(8,128)(2,1)S(1)}, u32[]{:S(2)}, u32[]{:S(2)}) collective-permute-start(bf16[272,1024]{1,0:T(8,128)(2,1)S(1)} %get-tuple-element.74), channel_id=1, source_target_pairs={{0,8},{1,9},{2,10},{3,11},{4,12},{5,13},{6,14},{7,15},{8,0},{9,1},... | collective-permute-start | bytes 1671176 | tf_op jit(solution)/shard_map/ppermute | solution.py:54
  72.2 2.0 %collective-permute-start.19 = (bf16[272,1024]{1,0:T(8,128)(2,1)S(1)}, bf16[272,1024]{1,0:T(8,128)(2,1)S(1)}, u32[]{:S(2)}, u32[]{:S(2)}) collective-permute-start(bf16[272,1024]{1,0:T(8,128)(2,1)S(1)} %get-tuple-element.72), channel_id=1, source_target_pairs={{0,8},{1,9},{2,10},{3,11},{4,12},{5,13},{6,14},{7,15},{8,0},{9,1},... | collective-permute-start | bytes 1671176 | tf_op jit(solution)/shard_map/ppermute | solution.py:54
  72.9 13.9 %collective-permute-start.21 = (bf16[272,1024]{1,0:T(8,128)(2,1)S(1)}, bf16[272,1024]{1,0:T(8,128)(2,1)S(1)}, u32[]{:S(2)}, u32[]{:S(2)}) collective-permute-start(bf16[272,1024]{1,0:T(8,128)(2,1)S(1)} %pair_sum.1), channel_id=1, source_target_pairs={{0,16},{1,17},{2,18},{3,19},{4,20},{5,21},{6,22},{7,23},{8,24},{9,... | collective-permute-start | bytes 1671176 | tf_op jit(solution)/shard_map/ppermute | solution.py:54

commit v6 on v5

--- a/solution.py
+++ b/solution.py
@@ -321,15 +321,11 @@
     out[STATE:, :] = jnp.where(line == 0, hi, jnp.where(line == 1, lo, 0.0)).astype(BF16)
 
 
-def again(value, out):
-    out[...] = value[...]
-
-
 def earlier_pairs(*refs):
-    *pairs, out = refs
+    second, first, third, out = refs
     total = jnp.zeros((STATE, OWN), F32)
     gone = jnp.zeros((1, OWN), F32)
-    for pair in pairs:
+    for pair in (first, second, third):
         total = total + jnp.exp(gone) * pair[:STATE, :].astype(F32)
         gone = gone + decay_of(pair)
     out[...] = total.astype(BF16)
@@ -450,13 +446,14 @@
     out[2 * ROWS :, :] = jnp.where(line == 0, hi, jnp.where(line == 1, lo, 0.0)).astype(BF16)
 
 
-def last_kernel(mine, came, far, out):
+def last_kernel(mine, came, far, out, held, sem):
     def tail(ref):
         rows = ref[2 * ROWS :, :].astype(F32)
         return rows[0:1] + rows[1:2]
 
     squares = tail(mine) + tail(came) + tail(far)
     diagonal = iota2((ROWS, ROWS), 0) == iota2((ROWS, ROWS), 1)
+    copies = []
     for strand in range(2):
         rows = slice(ROWS * strand, ROWS * strand + ROWS)
         mean = jnp.sum(jnp.where(diagonal, squares[:, rows], 0.0), axis=1, keepdims=True) * (1.0 / E)
@@ -464,7 +461,11 @@
         block = (main * lax.rsqrt(mean + 1e-05)).astype(BF16)
         if strand:
             block = flipped(block)
-        out[:, D * strand : D * strand + D] = block
+        held[strand] = block
+        copies.append(pltpu.make_async_copy(held.at[strand], out.at[:, pl.ds(D * strand, D)], sem.at[strand]))
+        copies[-1].start()
+    for copy in copies:
+        copy.wait()
 
 
 def swap_core(value):
@@ -578,12 +579,8 @@
     )
     mate = move(given, lambda z, yl, c, yh, x: dict(z=z ^ 1))
     pair = call(pair_state, "pair_state", shape(STATE + HALO, OWN), [VMEM] * 2, (kept, mate), mb=8)
-    far_first = []
-    for m in (3, 2, 1):
-        far_first.append(move(pair, pair_step(m)))
-        if m > 1:
-            pair = call(again, "again", shape(STATE + HALO, OWN), [VMEM], (pair,), mb=8)
-    earlier = far_first[::-1]
+    one, two, three = [move(pair, pair_step(m)) for m in (1, 2, 3)]
+    earlier = (two, one, three)
     local, carry, maps = call(
         local_kernel,
         "local_kernel",
@@ -635,7 +632,16 @@
         pair_sum, "pair_sum", shape(2 * ROWS + HALO, D), [VMEM] * 3, (keep, swap_core(give), keep_2), mb=8
     )
     far_part = swap_y(part)
-    out = call(last_kernel, "last_kernel", shape(ROWS, 2 * D), [VMEM] * 3, (keep_2, swap_core(give_2), far_part), mb=8)
+    out = call(
+        last_kernel,
+        "last_kernel",
+        shape(ROWS, 2 * D),
+        [VMEM] * 3,
+        (keep_2, swap_core(give_2), far_part),
+        scratch=[pltpu.VMEM((2, ROWS, D), BF16), pltpu.SemaphoreType.DMA((2,))],
+        mb=8,
+        out_specs=ANY,
+    )
     return out[None]
 
 

time: 88.2 us -> 88.3 us (level)
    pallas_call x17 -> x15, Pallas kernels: 21.2 us -> 21.2 us  [call(): pl.pallas_call(kernel, out_shape=outs, in_specs=ins, out_specs=jax.tree.m...]
where the time goes in v6:
time: 88.3 us; the launch traced here: 88.1 us
  starting transfers between devices  35.4 us (40%)
  waiting for transfers between devices  31.1 us (35%)
  Pallas kernels  21.2 us (24%)
    ppermute x22, starting transfers between devices, move(): return lax.ppermute(value, ('seq', 'fsdp'), pairs)  35.4 us
    ppermute x22, waiting for transfers between devices, move(): return lax.ppermute(value, ('seq', 'fsdp'), pairs)  31.1 us
    pallas_call x15, Pallas kernels, call(): pl.pallas_call(kernel, out_shape=outs, in_specs=ins, out_specs=jax.tree.m...  21.2 us
  transfers between devices with their start and end apart: 22, of which 8 were waited for; matrix products, arithmetic and copies ran while one was open for 0% of the time, Pallas kernels for 19%

profile of v6, /device:TPU:1, one launch (start us, length us, event | category | flops | bytes accessed | tf_op | source)
XLA Modules:
  0.0 88.1 jit_solution(15205023188076844062)
XLA Ops:
  0.0 1.9 %start_kernel.1 = (bf16[256,1024]{1,0:T(8,128)(2,1)S(1)}, bf16[672,128]{1,0:T(8,128)(2,1)S(1)}, bf16[1024,128]{1,0:T(8,128)(2,1)S(1)}, bf16[672,128]{1,0:T(8,128)(2,1)S(1)}, bf16[1024,128]{1,0:T(8,128)(2,1)S(1)}) custom-call(bf16[128,2048]{1,0:T(8,128)(2,1)} %bitcast.10, s32[1,128]{1,0:T(1,128)} %tokens.1, bf16[5,2048]{1,0:T(8,128)(2,1)} %base_bias.1, ...), custom_call_target="tpu_custom_call" | custom-call | tf_op jit(solution)/shard_map/start_kernel/pallas_call | solution.py:62
  2.0 2.2 %collective-permute-start = (bf16[256,1024]{1,0:T(8,128)(2,1)S(1)}, bf16[256,1024]{1,0:T(8,128)(2,1)S(1)}, u32[]{:S(2)}, u32[]{:S(2)}) collective-permute-start(bf16[256,1024]{1,0:T(8,128)(2,1)S(1)} %get-tuple-element.40.act.refs_0_), channel_id=1, source_target_pairs={{0,16},{1,17},{2,18},{3,19},{4,20},{5,21},{6,22},{7,23},{8,24},{9,... | collective-permute-start | bytes 1572872 | tf_op jit(solution)/shard_map/ppermute | solution.py:54
  4.2 1.9 %collective-permute-start.1 = (bf16[672,128]{1,0:T(8,128)(2,1)S(1)}, bf16[672,128]{1,0:T(8,128)(2,1)S(1)}, u32[]{:S(2)}, u32[]{:S(2)}) collective-permute-start(bf16[672,128]{1,0:T(8,128)(2,1)S(1)} %get-tuple-element.41), channel_id=1, source_target_pairs={{0,20},{1,21},{2,22},{3,23},{4,16},{5,17},{6,18},{7,19},{8,28},{9,... | collective-permute-start | bytes 516104 | tf_op jit(solution)/shard_map/ppermute | solution.py:54
  6.1 1.2 %collective-permute-start.4 = (bf16[672,128]{1,0:T(8,128)(2,1)S(1)}, bf16[672,128]{1,0:T(8,128)(2,1)S(1)}, u32[]{:S(2)}, u32[]{:S(2)}) collective-permute-start(bf16[672,128]{1,0:T(8,128)(2,1)S(1)} %get-tuple-element.46.refs_5_.refs_4_), channel_id=1, source_target_pairs={{0,1},{1,2},{2,3},{3,0},{4,5},{5,6},{6,7},{7,4},{8,9},{9,10},{10,1... | collective-permute-start | bytes 516104 | tf_op jit(solution)/shard_map/ppermute | solution.py:54
  7.3 2.5 %collective-permute-start.5 = (bf16[672,128]{1,0:T(8,128)(2,1)S(1)}, bf16[672,128]{1,0:T(8,128)(2,1)S(1)}, u32[]{:S(2)}, u32[]{:S(2)}) collective-permute-start(bf16[672,128]{1,0:T(8,128)(2,1)S(1)} %get-tuple-element.46.refs_5_.refs_4_), channel_id=1, source_target_pairs={{0,2},{1,3},{2,0},{3,1},{4,6},{5,7},{6,4},{7,5},{8,10},{9,11},{10,... | collective-permute-start | bytes 516104 | tf_op jit(solution)/shard_map/ppermute | solution.py:54
  9.8 0.6 pack_params.1
  10.4 1.9 %collective-permute-start.3 = (bf16[1024,128]{1,0:T(8,128)(2,1)S(1)}, bf16[1024,128]{1,0:T(8,128)(2,1)S(1)}, u32[]{:S(2)}, u32[]{:S(2)}) collective-permute-start(bf16[1024,128]{1,0:T(8,128)(2,1)S(1)} %hold.1), channel_id=1, source_target_pairs={{0,20},{1,21},{2,22},{3,23},{4,16},{5,17},{6,18},{7,19},{8,28},{9,... | collective-permute-start | bytes 786440 | tf_op jit(solution)/shard_map/ppermute | solution.py:54
  12.3 2.5 %collective-permute-start.6 = (bf16[672,128]{1,0:T(8,128)(2,1)S(1)}, bf16[672,128]{1,0:T(8,128)(2,1)S(1)}, u32[]{:S(2)}, u32[]{:S(2)}) collective-permute-start(bf16[672,128]{1,0:T(8,128)(2,1)S(1)} %get-tuple-element.46.refs_5_.refs_4_), channel_id=1, source_target_pairs={{0,3},{1,0},{2,1},{3,2},{4,7},{5,4},{6,5},{7,6},{8,11},{9,8},{10,9... | collective-permute-start | bytes 516104 | tf_op jit(solution)/shard_map/ppermute | solution.py:54
  14.8 0.0 collective-permute-done.act_y.refs_1_
  14.8 2.1 %collective-permute-start.7 = (bf16[672,128]{1,0:T(8,128)(2,1)S(1)}, bf16[672,128]{1,0:T(8,128)(2,1)S(1)}, u32[]{:S(2)}, u32[]{:S(2)}) collective-permute-start(bf16[672,128]{1,0:T(8,128)(2,1)S(1)} %collective-permute-done.1.far.refs_9_.refs_8_), channel_id=1, source_target_pairs={{0,1},{1,2},{2,3},{3,0},{4,5},{5,6},{6,7},{7,4},{8,9},{9,10},{10,1... | collective-permute-start | bytes 516104 | tf_op jit(solution)/shard_map/ppermute | solution.py:54
  16.9 0.0 collective-permute-done.4.refs_6_.refs_5_
  16.9 1.4 %collective-permute-start.9 = (bf16[672,128]{1,0:T(8,128)(2,1)S(1)}, bf16[672,128]{1,0:T(8,128)(2,1)S(1)}, u32[]{:S(2)}, u32[]{:S(2)}) collective-permute-start(bf16[672,128]{1,0:T(8,128)(2,1)S(1)} %collective-permute-done.1.far.refs_9_.refs_8_), channel_id=1, source_target_pairs={{0,3},{1,0},{2,1},{3,2},{4,7},{5,4},{6,5},{7,6},{8,11},{9,8},{10,9... | collective-permute-start | bytes 516104 | tf_op jit(solution)/shard_map/ppermute | solution.py:54
  18.3 0.0 collective-permute-done.5.refs_7_.refs_6_
  18.3 1.7 %collective-permute-start.8 = (bf16[672,128]{1,0:T(8,128)(2,1)S(1)}, bf16[672,128]{1,0:T(8,128)(2,1)S(1)}, u32[]{:S(2)}, u32[]{:S(2)}) collective-permute-start(bf16[672,128]{1,0:T(8,128)(2,1)S(1)} %get-tuple-element.47), channel_id=1, source_target_pairs={{0,2},{1,3},{2,0},{3,1},{4,6},{5,7},{6,4},{7,5},{8,10},{9,11},{10,... | collective-permute-start | bytes 516104 | tf_op jit(solution)/shard_map/ppermute | solution.py:54
  20.0 3.5 %collective-permute-start.2 = (bf16[16,1024]{1,0:T(8,128)(2,1)S(1)}, bf16[16,1024]{1,0:T(8,128)(2,1)S(1)}, u32[]{:S(2)}, u32[]{:S(2)}) collective-permute-start(bf16[16,1024]{1,0:T(8,128)(2,1)S(1)} %get-tuple-element.42), channel_id=1, source_target_pairs={{8,40},{9,41},{10,42},{11,43},{12,44},{13,45},{14,46},{15,47},{24,... | collective-permute-start | bytes 98312 | tf_op jit(solution)/shard_map/ppermute | solution.py:54
  23.6 0.6 collective-permute-done.9.refs_12_.refs_11_
  24.1 0.0 collective-permute-done.3.refs_4_
  24.1 0.4 collective-permute-done.2.refs_2_
  24.5 1.2 %collective-permute-done.8.refs_11_.refs_10_ = bf16[672,128]{1,0:T(8,128)(2,1)S(1)} collective-permute-done((bf16[672,128]{1,0:T(8,128)(2,1)S(1)}, bf16[672,128]{1,0:T(8,128)(2,1)S(1)}, u32[]{:S(2)}, u32[]{:S(2)}) %collective-permute-start.8) | collective-permute-done | bytes 172064 | tf_op jit(solution)/shard_map/ppermute | solution.py:54
  25.8 0.2 pack_core.1
  25.9 2.7 %collective-permute-start.10 = (bf16[656,1024]{1,0:T(8,128)(2,1)S(1)}, bf16[656,1024]{1,0:T(8,128)(2,1)S(1)}, u32[]{:S(2)}, u32[]{:S(2)}) collective-permute-start(bf16[656,1024]{1,0:T(8,128)(2,1)S(1)} %get-tuple-element.48), channel_id=1, source_target_pairs={{0,8},{1,9},{2,10},{3,11},{4,12},{5,13},{6,14},{7,15},{8,0},{9,1},... | collective-permute-start | bytes 4030472 | tf_op jit(solution)/shard_map/ppermute | solution.py:54
  28.7 1.0 %collective-permute-start.11 = (bf16[2048,128]{1,0:T(8,128)(2,1)S(1)}, bf16[2048,128]{1,0:T(8,128)(2,1)S(1)}, u32[]{:S(2)}, u32[]{:S(2)}) collective-permute-start(bf16[2048,128]{1,0:T(8,128)(2,1)S(1)} %get-tuple-element.51.refs_0_), channel_id=1, source_target_pairs={{0,1},{1,2},{2,3},{3,0},{4,5},{5,6},{6,7},{7,4},{8,9},{9,10},{10,1... | collective-permute-start | bytes 1572872 | tf_op jit(solution)/shard_map/ppermute | solution.py:54
  29.6 2.8 %collective-permute-start.12 = (bf16[2048,128]{1,0:T(8,128)(2,1)S(1)}, bf16[2048,128]{1,0:T(8,128)(2,1)S(1)}, u32[]{:S(2)}, u32[]{:S(2)}) collective-permute-start(bf16[2048,128]{1,0:T(8,128)(2,1)S(1)} %get-tuple-element.51.refs_0_), channel_id=1, source_target_pairs={{0,2},{1,3},{2,0},{3,1},{4,6},{5,7},{6,4},{7,5},{8,10},{9,11},{10,... | collective-permute-start | bytes 1572872 | tf_op jit(solution)/shard_map/ppermute | solution.py:54
  32.4 0.0 collective-permute-start.13
  32.4 0.0 collective-permute-done.10.refs_3_
  32.4 4.3 %first_scan.1 = (bf16[512,512]{1,0:T(8,128)(2,1)S(1)}, bf16[512,256]{1,0:T(8,128)(2,1)S(1)}, f32[32,128]{1,0:T(8,128)S(1)}, f32[32,128]{1,0:T(8,128)S(1)}, bf16[...) custom-call(bf16[256,1024]{1,0:T(8,128)(2,1)S(1)} %get-tuple-element, ...), custom_call_target="tpu_custom_call" | custom-call | flops 968884224 | bytes 8388608 | tf_op jit(solution)/shard_map/first_scan/pallas_call | solution.py:62
  36.7 1.7 %collective-permute-start.14 = (bf16[144,512]{1,0:T(8,128)(2,1)S(1)}, bf16[144,512]{1,0:T(8,128)(2,1)S(1)}, u32[]{:S(2)}, u32[]{:S(2)}) collective-permute-start(bf16[144,512]{1,0:T(8,128)(2,1)S(1)} %get-tuple-element.53), channel_id=1, source_target_pairs={{0,32},{1,33},{2,34},{3,35},{4,36},{5,37},{6,38},{7,39},{8,40},{9,... | collective-permute-start | bytes 442376 | tf_op jit(solution)/shard_map/ppermute | solution.py:54
  38.4 3.6 %second_scan.1 = (bf16[512,512]{1,0:T(8,128)(2,1)S(1)}, bf16[512,256]{1,0:T(8,128)(2,1)S(1)}, f32[32,128]{1,0:T(8,128)S(1)}, f32[32,128]{1,0:T(8,128)S(1)}, bf16...) custom-call(bf16[2,528,1024]{2,1,0:T(8,128)(2,1)S(1)} %get-tuple-element.50.act, ...), custom_call_target="tpu_custom_call" | custom-call | flops 15502147584 | bytes 8388608 | tf_op jit(solution)/shard_map/second_scan/pallas_call | solution.py:62
  42.0 0.1 pair_state.1.refs_10_
  42.1 1.3 %collective-permute-start.15 = (bf16[144,512]{1,0:T(8,128)(2,1)S(1)}, bf16[144,512]{1,0:T(8,128)(2,1)S(1)}, u32[]{:S(2)}, u32[]{:S(2)}) collective-permute-start(bf16[144,512]{1,0:T(8,128)(2,1)S(1)} %pair_state.1.refs_10_), channel_id=1, source_target_pairs={{32,160},{33,161},{34,162},{35,163},{36,164},{37,165},{38,166},{39... | collective-permute-start | bytes 442376 | tf_op jit(solution)/shard_map/ppermute | solution.py:54
  43.4 1.3 %collective-permute-start.16 = (bf16[144,512]{1,0:T(8,128)(2,1)S(1)}, bf16[144,512]{1,0:T(8,128)(2,1)S(1)}, u32[]{:S(2)}, u32[]{:S(2)}) collective-permute-start(bf16[144,512]{1,0:T(8,128)(2,1)S(1)} %pair_state.1.refs_10_), channel_id=1, source_target_pairs={{32,96},{33,97},{34,98},{35,99},{36,100},{37,101},{38,102},{39,103... | collective-permute-start | bytes 442376 | tf_op jit(solution)/shard_map/ppermute | solution.py:54
  44.7 1.3 %collective-permute-start.17 = (bf16[144,512]{1,0:T(8,128)(2,1)S(1)}, bf16[144,512]{1,0:T(8,128)(2,1)S(1)}, u32[]{:S(2)}, u32[]{:S(2)}) collective-permute-start(bf16[144,512]{1,0:T(8,128)(2,1)S(1)} %pair_state.1.refs_10_), channel_id=1, source_target_pairs={{32,224},{33,225},{34,226},{35,227},{36,228},{37,229},{38,230},{39... | collective-permute-start | bytes 442376 | tf_op jit(solution)/shard_map/ppermute | solution.py:54
  46.0 9.6 %collective-permute-done.12.refs_2_ = bf16[2048,128]{1,0:T(8,128)(2,1)S(1)} collective-permute-done((bf16[2048,128]{1,0:T(8,128)(2,1)S(1)}, bf16[2048,128]{1,0:T(8,128)(2,1)S(1)}, u32[]{:S(2)}, u32[]{:S(2)}) %collective-permute-start.12) | collective-permute-done | bytes 524320 | tf_op jit(solution)/shard_map/ppermute | solution.py:54
  55.7 1.9 %gate_kernel.1 = (f32[2,512,512]{2,1,0:T(8,128)S(1)}, bf16[2,512,512]{2,1,0:T(8,128)(2,1)S(1)}) custom-call(bf16[2,528,1024]{2,1,0:T(8,128)(2,1)S(1)} %get-tuple-element.50.act, bf16[2048,128]{1,0:T(8,128)(2,1)S(1)} %get-tuple-element.51.refs_0_, bf16[2048,128]{1,0:T(8,128)(2,1)S(1)} %collective-permute-done.11.refs_1_, ...), custom_call_target="tpu_custom_call" | custom-call | flops 1073741824 | bytes 8388608 | tf_op jit(solution)/shard_map/gate_kernel/pallas_call | solution.py:62
  57.6 6.0 %collective-permute-done.17.refs_2_ = bf16[144,512]{1,0:T(8,128)(2,1)S(1)} collective-permute-done((bf16[144,512]{1,0:T(8,128)(2,1)S(1)}, bf16[144,512]{1,0:T(8,128)(2,1)S(1)}, u32[]{:S(2)}, u32[]{:S(2)}) %collective-permute-start.17) | collective-permute-done | bytes 147488 | tf_op jit(solution)/shard_map/ppermute | solution.py:54
  63.6 0.1 earlier_pairs.1.refs_1_
  63.7 0.1 collective-permute-start.18
  63.8 5.0 %local_kernel.1 = (f32[2,512,512]{2,1,0:T(8,128)S(1)}, f32[2,512,512]{2,1,0:T(8,128)S(1)}, bf16[2,512,128]{2,1,0:T(8,128)(2,1)S(1)}) custom-call(bf16[512,512]{1,0:T(8,128)(2,1)S(1)} %get-tuple-element.56.refs_0_, bf16[512,256]{1,0:T(8,128)(2,1)S(1)} %get-tuple-element.57.refs_1_, f32[32,128]{1,0:T(8,128)S(1)} %get-tuple-element.58.refs_2_, ...), custom_call_target="tpu_custom_call" | custom-call | flops 4294967296 | bytes 16777216 | tf_op jit(solution)/shard_map/local_kernel/pallas_call | solution.py:62
  68.7 1.1 %first_half.1 = (bf16[2,128,512]{2,1,0:T(8,128)(2,1)S(1)}, bf16[272,1024]{1,0:T(8,128)(2,1)S(1)}, bf16[272,1024]{1,0:T(8,128)(2,1)S(1)}) custom-call(bf16[144,512]{1,0:T(8,128)(2,1)S(1)} %collective-permute-done.14.mate.refs_0_, bf16[128,512]{1,0:T(8,128)(2,1)S(1)} %earlier_pairs.1.refs_1_, bf16[128,512]{1,0:T(8,128)(2,1)S(1)} %collective-permute-done.18.refs_2_, ...), custom_call_target="tpu_custom_call" | custom-call | flops 536870912 | bytes 4194304 | tf_op jit(solution)/shard_map/first_half/pallas_call | solution.py:62
  69.9 1.2 %collective-permute-start.20 = (bf16[272,1024]{1,0:T(8,128)(2,1)S(1)}, bf16[272,1024]{1,0:T(8,128)(2,1)S(1)}, u32[]{:S(2)}, u32[]{:S(2)}) collective-permute-start(bf16[272,1024]{1,0:T(8,128)(2,1)S(1)} %get-tuple-element.74), channel_id=1, source_target_pairs={{0,8},{1,9},{2,10},{3,11},{4,12},{5,13},{6,14},{7,15},{8,0},{9,1},... | collective-permute-start | bytes 1671176 | tf_op jit(solution)/shard_map/ppermute | solution.py:54
  71.1 1.0 %second_half.1 = (bf16[272,1024]{1,0:T(8,128)(2,1)S(1)}, bf16[272,1024]{1,0:T(8,128)(2,1)S(1)}) custom-call(bf16[2,512,512]{2,1,0:T(8,128)(2,1)S(1)} %get-tuple-element.52.refs_3_.weight, bf16[2,128,512]{2,1,0:T(8,128)(2,1)S(1)} %get-tuple-element.70.entering, f32[8,768]{1,0:T(8,128)S(1)} %get-tuple-element.45.prm.refs_12_.refs_4_, ...), custom_call_target="tpu_custom_call" | custom-call | flops 536870912 | bytes 4194304 | tf_op jit(solution)/shard_map/second_half/pallas_call | solution.py:62
  72.1 0.1 collective-permute-start.19
  72.2 0.4 collective-permute-done.20.came
  72.7 0.1 pair_sum.1
  72.8 1.0 %collective-permute-start.21 = (bf16[272,1024]{1,0:T(8,128)(2,1)S(1)}, bf16[272,1024]{1,0:T(8,128)(2,1)S(1)}, u32[]{:S(2)}, u32[]{:S(2)}) collective-permute-start(bf16[272,1024]{1,0:T(8,128)(2,1)S(1)} %pair_sum.1), channel_id=1, source_target_pairs={{0,16},{1,17},{2,18},{3,19},{4,20},{5,21},{6,22},{7,23},{8,24},{9,... | collective-permute-start | bytes 1671176 | tf_op jit(solution)/shard_map/ppermute | solution.py:54
  73.9 0.3 collective-permute-done.19.came
  74.2 12.6 %collective-permute-done.21.far = bf16[272,1024]{1,0:T(8,128)(2,1)S(1)} collective-permute-done((bf16[272,1024]{1,0:T(8,128)(2,1)S(1)}, bf16[272,1024]{1,0:T(8,128)(2,1)S(1)}, u32[]{:S(2)}, u32[]{:S(2)}) %collective-permute-start.21) | collective-permute-done | bytes 557088 | tf_op jit(solution)/shard_map/ppermute | solution.py:54
  86.7 1.2 %last_kernel.1 = bf16[128,2048]{1,0:T(8,128)(2,1)} custom-call(bf16[272,1024]{1,0:T(8,128)(2,1)S(1)} %get-tuple-element.71.second.mine, bf16[272,1024]{1,0:T(8,128)(2,1)S(1)} %collective-permute-done.19.came, bf16[272,1024]{1,0:T(8,128)(2,1)S(1)} %collective-permute-done.21.far), custom_call_target="tpu_custom_call" | custom-call | tf_op jit(solution)/shard_map/last_kernel/pallas_call | solution.py:62
  (22 shorter events, 0.1 us)
Async XLA Ops:
  0.0 9.7 %copy-start.4 = (f32[2304]{0:T(1024)S(1)}, f32[2304]{0:T(1024)}, u32[]{:S(2)}) copy-start(f32[2304]{0:T(1024)} %param.15) | copy-start | bytes 27652
  0.0 9.8 %copy-start = (f32[4,2304]{1,0:T(4,128)S(1)}, f32[4,2304]{1,0:T(4,128)}, u32[]{:S(2)}) copy-start(f32[4,2304]{1,0:T(4,128)} %cw.1) | copy-start | bytes 110596
  0.0 9.8 %copy-start.2 = (f32[32]{0:T(128)S(1)}, f32[32]{0:T(128)}, u32[]{:S(2)}) copy-start(f32[32]{0:T(128)} %param.16) | copy-start | bytes 388
  0.0 9.8 %copy-start.3 = (f32[32]{0:T(128)S(1)}, f32[32]{0:T(128)}, u32[]{:S(2)}) copy-start(f32[32]{0:T(128)} %param.17) | copy-start | bytes 388
  0.0 9.8 %copy-start.1 = (f32[2048]{0:T(1024)S(1)}, f32[2048]{0:T(1024)}, u32[]{:S(2)}) copy-start(f32[2048]{0:T(1024)} %param.18) | copy-start | bytes 24580
  2.0 12.8 %collective-permute-start = (bf16[256,1024]{1,0:T(8,128)(2,1)S(1)}, bf16[256,1024]{1,0:T(8,128)(2,1)S(1)}, u32[]{:S(2)}, u32[]{:S(2)}) collective-permute-start(bf16[256,1024]{1,0:T(8,128)(2,1)S(1)} %get-tuple-element.40.act.refs_0_), channel_id=1, source_target_pairs={{0,16},{1,17},{2,18},{3,19},{4,20},{5,21},{6,22},{7,23},{8,24},{9,... | collective-permute-start | bytes 1572872 | tf_op jit(solution)/shard_map/ppermute | solution.py:54
  4.2 6.2 %collective-permute-start.1 = (bf16[672,128]{1,0:T(8,128)(2,1)S(1)}, bf16[672,128]{1,0:T(8,128)(2,1)S(1)}, u32[]{:S(2)}, u32[]{:S(2)}) collective-permute-start(bf16[672,128]{1,0:T(8,128)(2,1)S(1)} %get-tuple-element.41), channel_id=1, source_target_pairs={{0,20},{1,21},{2,22},{3,23},{4,16},{5,17},{6,18},{7,19},{8,28},{9,... | collective-permute-start | bytes 516104 | tf_op jit(solution)/shard_map/ppermute | solution.py:54
  6.1 10.8 %collective-permute-start.4 = (bf16[672,128]{1,0:T(8,128)(2,1)S(1)}, bf16[672,128]{1,0:T(8,128)(2,1)S(1)}, u32[]{:S(2)}, u32[]{:S(2)}) collective-permute-start(bf16[672,128]{1,0:T(8,128)(2,1)S(1)} %get-tuple-element.46.refs_5_.refs_4_), channel_id=1, source_target_pairs={{0,1},{1,2},{2,3},{3,0},{4,5},{5,6},{6,7},{7,4},{8,9},{9,10},{10,1... | collective-permute-start | bytes 516104 | tf_op jit(solution)/shard_map/ppermute | solution.py:54
  7.3 11.0 %collective-permute-start.5 = (bf16[672,128]{1,0:T(8,128)(2,1)S(1)}, bf16[672,128]{1,0:T(8,128)(2,1)S(1)}, u32[]{:S(2)}, u32[]{:S(2)}) collective-permute-start(bf16[672,128]{1,0:T(8,128)(2,1)S(1)} %get-tuple-element.46.refs_5_.refs_4_), channel_id=1, source_target_pairs={{0,2},{1,3},{2,0},{3,1},{4,6},{5,7},{6,4},{7,5},{8,10},{9,11},{10,... | collective-permute-start | bytes 516104 | tf_op jit(solution)/shard_map/ppermute | solution.py:54
  10.4 13.8 %collective-permute-start.3 = (bf16[1024,128]{1,0:T(8,128)(2,1)S(1)}, bf16[1024,128]{1,0:T(8,128)(2,1)S(1)}, u32[]{:S(2)}, u32[]{:S(2)}) collective-permute-start(bf16[1024,128]{1,0:T(8,128)(2,1)S(1)} %hold.1), channel_id=1, source_target_pairs={{0,20},{1,21},{2,22},{3,23},{4,16},{5,17},{6,18},{7,19},{8,28},{9,... | collective-permute-start | bytes 786440 | tf_op jit(solution)/shard_map/ppermute | solution.py:54
  12.3 7.7 %collective-permute-start.6 = (bf16[672,128]{1,0:T(8,128)(2,1)S(1)}, bf16[672,128]{1,0:T(8,128)(2,1)S(1)}, u32[]{:S(2)}, u32[]{:S(2)}) collective-permute-start(bf16[672,128]{1,0:T(8,128)(2,1)S(1)} %get-tuple-element.46.refs_5_.refs_4_), channel_id=1, source_target_pairs={{0,3},{1,0},{2,1},{3,2},{4,7},{5,4},{6,5},{7,6},{8,11},{9,8},{10,9... | collective-permute-start | bytes 516104 | tf_op jit(solution)/shard_map/ppermute | solution.py:54
  14.8 8.7 %collective-permute-start.7 = (bf16[672,128]{1,0:T(8,128)(2,1)S(1)}, bf16[672,128]{1,0:T(8,128)(2,1)S(1)}, u32[]{:S(2)}, u32[]{:S(2)}) collective-permute-start(bf16[672,128]{1,0:T(8,128)(2,1)S(1)} %collective-permute-done.1.far.refs_9_.refs_8_), channel_id=1, source_target_pairs={{0,1},{1,2},{2,3},{3,0},{4,5},{5,6},{6,7},{7,4},{8,9},{9,10},{10,1... | collective-permute-start | bytes 516104 | tf_op jit(solution)/shard_map/ppermute | solution.py:54
  16.9 7.2 %collective-permute-start.9 = (bf16[672,128]{1,0:T(8,128)(2,1)S(1)}, bf16[672,128]{1,0:T(8,128)(2,1)S(1)}, u32[]{:S(2)}, u32[]{:S(2)}) collective-permute-start(bf16[672,128]{1,0:T(8,128)(2,1)S(1)} %collective-permute-done.1.far.refs_9_.refs_8_), channel_id=1, source_target_pairs={{0,3},{1,0},{2,1},{3,2},{4,7},{5,4},{6,5},{7,6},{8,11},{9,8},{10,9... | collective-permute-start | bytes 516104 | tf_op jit(solution)/shard_map/ppermute | solution.py:54
  18.3 7.5 %collective-permute-start.8 = (bf16[672,128]{1,0:T(8,128)(2,1)S(1)}, bf16[672,128]{1,0:T(8,128)(2,1)S(1)}, u32[]{:S(2)}, u32[]{:S(2)}) collective-permute-start(bf16[672,128]{1,0:T(8,128)(2,1)S(1)} %get-tuple-element.47), channel_id=1, source_target_pairs={{0,2},{1,3},{2,0},{3,1},{4,6},{5,7},{6,4},{7,5},{8,10},{9,11},{10,... | collective-permute-start | bytes 516104 | tf_op jit(solution)/shard_map/ppermute | solution.py:54
  20.0 4.5 %collective-permute-start.2 = (bf16[16,1024]{1,0:T(8,128)(2,1)S(1)}, bf16[16,1024]{1,0:T(8,128)(2,1)S(1)}, u32[]{:S(2)}, u32[]{:S(2)}) collective-permute-start(bf16[16,1024]{1,0:T(8,128)(2,1)S(1)} %get-tuple-element.42), channel_id=1, source_target_pairs={{8,40},{9,41},{10,42},{11,43},{12,44},{13,45},{14,46},{15,47},{24,... | collective-permute-start | bytes 98312 | tf_op jit(solution)/shard_map/ppermute | solution.py:54
  25.9 6.5 %collective-permute-start.10 = (bf16[656,1024]{1,0:T(8,128)(2,1)S(1)}, bf16[656,1024]{1,0:T(8,128)(2,1)S(1)}, u32[]{:S(2)}, u32[]{:S(2)}) collective-permute-start(bf16[656,1024]{1,0:T(8,128)(2,1)S(1)} %get-tuple-element.48), channel_id=1, source_target_pairs={{0,8},{1,9},{2,10},{3,11},{4,12},{5,13},{6,14},{7,15},{8,0},{9,1},... | collective-permute-start | bytes 4030472 | tf_op jit(solution)/shard_map/ppermute | solution.py:54
  28.7 16.0 %collective-permute-start.11 = (bf16[2048,128]{1,0:T(8,128)(2,1)S(1)}, bf16[2048,128]{1,0:T(8,128)(2,1)S(1)}, u32[]{:S(2)}, u32[]{:S(2)}) collective-permute-start(bf16[2048,128]{1,0:T(8,128)(2,1)S(1)} %get-tuple-element.51.refs_0_), channel_id=1, source_target_pairs={{0,1},{1,2},{2,3},{3,0},{4,5},{5,6},{6,7},{7,4},{8,9},{9,10},{10,1... | collective-permute-start | bytes 1572872 | tf_op jit(solution)/shard_map/ppermute | solution.py:54
  29.6 26.0 %collective-permute-start.12 = (bf16[2048,128]{1,0:T(8,128)(2,1)S(1)}, bf16[2048,128]{1,0:T(8,128)(2,1)S(1)}, u32[]{:S(2)}, u32[]{:S(2)}) collective-permute-start(bf16[2048,128]{1,0:T(8,128)(2,1)S(1)} %get-tuple-element.51.refs_0_), channel_id=1, source_target_pairs={{0,2},{1,3},{2,0},{3,1},{4,6},{5,7},{6,4},{7,5},{8,10},{9,11},{10,... | collective-permute-start | bytes 1572872 | tf_op jit(solution)/shard_map/ppermute | solution.py:54
  32.4 23.2 %collective-permute-start.13 = (bf16[2048,128]{1,0:T(8,128)(2,1)S(1)}, bf16[2048,128]{1,0:T(8,128)(2,1)S(1)}, u32[]{:S(2)}, u32[]{:S(2)}) collective-permute-start(bf16[2048,128]{1,0:T(8,128)(2,1)S(1)} %get-tuple-element.51.refs_0_), channel_id=1, source_target_pairs={{0,3},{1,0},{2,1},{3,2},{4,7},{5,4},{6,5},{7,6},{8,11},{9,8},{10,9... | collective-permute-start | bytes 1572872 | tf_op jit(solution)/shard_map/ppermute | solution.py:54
  36.7 5.4 %collective-permute-start.14 = (bf16[144,512]{1,0:T(8,128)(2,1)S(1)}, bf16[144,512]{1,0:T(8,128)(2,1)S(1)}, u32[]{:S(2)}, u32[]{:S(2)}) collective-permute-start(bf16[144,512]{1,0:T(8,128)(2,1)S(1)} %get-tuple-element.53), channel_id=1, source_target_pairs={{0,32},{1,33},{2,34},{3,35},{4,36},{5,37},{6,38},{7,39},{8,40},{9,... | collective-permute-start | bytes 442376 | tf_op jit(solution)/shard_map/ppermute | solution.py:54
  42.1 15.5 %collective-permute-start.15 = (bf16[144,512]{1,0:T(8,128)(2,1)S(1)}, bf16[144,512]{1,0:T(8,128)(2,1)S(1)}, u32[]{:S(2)}, u32[]{:S(2)}) collective-permute-start(bf16[144,512]{1,0:T(8,128)(2,1)S(1)} %pair_state.1.refs_10_), channel_id=1, source_target_pairs={{32,160},{33,161},{34,162},{35,163},{36,164},{37,165},{38,166},{39... | collective-permute-start | bytes 442376 | tf_op jit(solution)/shard_map/ppermute | solution.py:54
  43.4 14.2 %collective-permute-start.16 = (bf16[144,512]{1,0:T(8,128)(2,1)S(1)}, bf16[144,512]{1,0:T(8,128)(2,1)S(1)}, u32[]{:S(2)}, u32[]{:S(2)}) collective-permute-start(bf16[144,512]{1,0:T(8,128)(2,1)S(1)} %pair_state.1.refs_10_), channel_id=1, source_target_pairs={{32,96},{33,97},{34,98},{35,99},{36,100},{37,101},{38,102},{39,103... | collective-permute-start | bytes 442376 | tf_op jit(solution)/shard_map/ppermute | solution.py:54
  44.7 18.9 %collective-permute-start.17 = (bf16[144,512]{1,0:T(8,128)(2,1)S(1)}, bf16[144,512]{1,0:T(8,128)(2,1)S(1)}, u32[]{:S(2)}, u32[]{:S(2)}) collective-permute-start(bf16[144,512]{1,0:T(8,128)(2,1)S(1)} %pair_state.1.refs_10_), channel_id=1, source_target_pairs={{32,224},{33,225},{34,226},{35,227},{36,228},{37,229},{38,230},{39... | collective-permute-start | bytes 442376 | tf_op jit(solution)/shard_map/ppermute | solution.py:54
  63.7 5.1 %collective-permute-start.18 = (bf16[128,512]{1,0:T(8,128)(2,1)S(1)}, bf16[128,512]{1,0:T(8,128)(2,1)S(1)}, u32[]{:S(2)}, u32[]{:S(2)}) collective-permute-start(bf16[128,512]{1,0:T(8,128)(2,1)S(1)} %earlier_pairs.1.refs_1_), channel_id=1, source_target_pairs={{0,32},{1,33},{2,34},{3,35},{4,36},{5,37},{6,38},{7,39},{8,40},{9,... | collective-permute-start | bytes 393224 | tf_op jit(solution)/shard_map/ppermute | solution.py:54
  69.9 2.8 %collective-permute-start.20 = (bf16[272,1024]{1,0:T(8,128)(2,1)S(1)}, bf16[272,1024]{1,0:T(8,128)(2,1)S(1)}, u32[]{:S(2)}, u32[]{:S(2)}) collective-permute-start(bf16[272,1024]{1,0:T(8,128)(2,1)S(1)} %get-tuple-element.74), channel_id=1, source_target_pairs={{0,8},{1,9},{2,10},{3,11},{4,12},{5,13},{6,14},{7,15},{8,0},{9,1},... | collective-permute-start | bytes 1671176 | tf_op jit(solution)/shard_map/ppermute | solution.py:54
  72.1 2.0 %collective-permute-start.19 = (bf16[272,1024]{1,0:T(8,128)(2,1)S(1)}, bf16[272,1024]{1,0:T(8,128)(2,1)S(1)}, u32[]{:S(2)}, u32[]{:S(2)}) collective-permute-start(bf16[272,1024]{1,0:T(8,128)(2,1)S(1)} %get-tuple-element.72), channel_id=1, source_target_pairs={{0,8},{1,9},{2,10},{3,11},{4,12},{5,13},{6,14},{7,15},{8,0},{9,1},... | collective-permute-start | bytes 1671176 | tf_op jit(solution)/shard_map/ppermute | solution.py:54
  72.8 13.9 %collective-permute-start.21 = (bf16[272,1024]{1,0:T(8,128)(2,1)S(1)}, bf16[272,1024]{1,0:T(8,128)(2,1)S(1)}, u32[]{:S(2)}, u32[]{:S(2)}) collective-permute-start(bf16[272,1024]{1,0:T(8,128)(2,1)S(1)} %pair_sum.1), channel_id=1, source_target_pairs={{0,16},{1,17},{2,18},{3,19},{4,20},{5,21},{6,22},{7,23},{8,24},{9,... | collective-permute-start | bytes 1671176 | tf_op jit(solution)/shard_map/ppermute | solution.py:54
